TPU v7x, 32 devices: a whole 2x2x4 slice. The times are simulated.
32 devices in a mesh: dp: 8 (over z, core), ns: 4 (over y, x).
Axes of the slice: x: 2, y: 2, z: 4, core: 2. Of those that a mesh axis runs over, the one named last changes fastest.
Arguments:
- frames: bfloat16 [2, 128, 121, 2048], P(None, ('dp', 'ns')), may hold values from -9 to 9
- game_ids: int32 [2, 128, 1], P(None, ('dp', 'ns')), may hold values from 0 to 7; in each aligned block of 16 rows (0 to 15, 16 to 31, ..., all dimensions but the last counted through in order) at most 4 rows name the same one
- actions: int32 [2, 128], P(None, ('dp', 'ns')), may hold values from 0 to 17
- groups: int32 [2, 128], P(None, ('dp', 'ns')), may hold values from 0 to 1
- targets: bfloat16 [2, 128], P(None, ('dp', 'ns')), may hold values from -1.796875 to 1.796875
- w_pair: float32 [2, 2, 2048, 512], P(None, None, 'ns'), may hold values from -0.125 to 0.125
- w_spatial: float32 [2, 4608, 512], P(None, 'ns'), may hold values from -0.09375 to 0.09375
- mom_pair: float32 [2, 2, 2048, 512], P(None, None, 'ns'), may hold values from -1.8384316e-05 to 1.8384316e-05
- mom_spatial: float32 [2, 4608, 512], P(None, 'ns'), may hold values from -1.8384316e-05 to 1.8384316e-05
- head_table: float32 [8, 2048, 918], P('dp', 'ns'), may hold values from -0.375 to 0.375
- head_first: float32 [8, 2048, 918], P('dp', 'ns'), may hold values from -1.1444092e-05 to 1.1444092e-05
- head_second: float32 [8, 2048, 918], P('dp', 'ns'), may hold values from 2.2114943e-13 to 8.7625247e-13
- norm_params: float32 [2, 2, 3072], replicated, may hold values from -1.5 to 2.5
- norm_first: float32 [2, 2, 3072], replicated, may hold values from -4.5776367e-05 to 4.5776367e-05
- norm_second: float32 [2, 2, 3072], replicated, may hold values from 3.5050099e-12 to 1.4186944e-11
Outputs:
- w_pair_new: float32 [2, 2, 2048, 512], P(None, None, 'ns')
- w_spatial_new: float32 [2, 4608, 512], P(None, 'ns')
- mom_pair_new: float32 [2, 2, 2048, 512], P(None, None, 'ns')
- mom_spatial_new: float32 [2, 4608, 512], P(None, 'ns')
- head_table_new: float32 [8, 2048, 918], P('dp', 'ns')
- head_first_new: float32 [8, 2048, 918], P('dp', 'ns')
- head_second_new: float32 [8, 2048, 918], P('dp', 'ns')
- norm_params_new: float32 [2, 2, 3072], replicated
- norm_first_new: float32 [2, 2, 3072], replicated
- norm_second_new: float32 [2, 2, 3072], replicated
- grad_norm: float32 [], replicated
- loss_sum: float32 [], replicated
- weight_total: float32 [], replicated
Inputs may be any that keep to these rules, and one draw needn't show every extreme that they name: `game_ids`: in each aligned block of 16 samples of a micro-batch (the samples of one index of dp) no game is named by more than 4 samples; in some block one game is named by exactly 4.
All inputs are finite; a program needn't handle non-finite values.
Results may differ from a plain program's by a relative error of at most 0.015.
Values may be sent and summed in bfloat16 or wider, within the bound.
No kernel may reach another device: no remote copies, remote signals or barrier semaphores. Data moves between devices by JAX's collectives and lax.ppermute only.
A program may use at most 384 MiB of HBM per device.

v0:
```python
import math

import jax
import jax.numpy as jnp
from jax import lax
from jax.sharding import PartitionSpec as P

C = 2048
MID = 512
ACTIONS = 18
ATOMS = 51
GROUPS = 32
SIDE = 11
BLOCKS = 2
MB = 2
NS_ITERS = 2
STEP = 10


highest = lax.Precision.HIGHEST
eps_norm = 1e-05
decay_moment = 0.5
beta_second = 0.95
adam_eps = 1e-08
rate_muon = 0.2
decay_muon = 0.01
rate_head = 0.02
decay_head = 0.01
rate_gain = 0.05
clip_limit = 0.01
cql_alpha = 0.05
value_max = 3.0
coef_a = 3.4445
coef_b = -4.775
coef_c = 2.0315


def group_norm(stream, gain, bias):
    frame_count, pixel_count, channels = stream.shape
    grouped = stream.reshape(frame_count, pixel_count, GROUPS, channels // GROUPS)
    center = jnp.mean(grouped, axis=(1, 3), keepdims=True)
    spread = jnp.mean(jnp.square(grouped - center), axis=(1, 3), keepdims=True)
    normed = ((grouped - center) * lax.rsqrt(spread + eps_norm)).reshape(
        frame_count, pixel_count, channels
    )
    return normed * gain + bias


def norm_act(stream, gain, bias):
    return jax.nn.silu(group_norm(stream, gain, bias))


def residual_tail(stream, last_out, gain, bias):
    return jax.nn.silu(stream + group_norm(last_out, gain, bias))


def spread_taps(hidden):
    frame_count, pixel_count, channels = hidden.shape
    grid = hidden.reshape(frame_count, SIDE, SIDE, channels)
    padded = jnp.pad(grid, ((0, 0), (1, 1), (1, 1), (0, 0)))
    pieces = [
        padded[:, row_off : row_off + SIDE, col_off : col_off + SIDE, :]
        for row_off in range(3)
        for col_off in range(3)
    ]
    return jnp.concatenate(pieces, axis=3).reshape(frame_count, pixel_count, 9 * channels)


def gain_parts(gain_rows):
    return (
        gain_rows[0, :MID],
        gain_rows[1, :MID],
        gain_rows[0, MID : 2 * MID],
        gain_rows[1, MID : 2 * MID],
        gain_rows[0, 2 * MID :],
        gain_rows[1, 2 * MID :],
    )


def sample_loss(logits, sample_meta, support):
    dist = jax.nn.softmax(logits.reshape(-1, ACTIONS, ATOMS), axis=2)
    q_values = jnp.sum(dist * support, axis=2)
    action_hot = (sample_meta[:, 3:4] == jnp.arange(ACTIONS, dtype=jnp.float32)[None, :]).astype(
        jnp.float32
    )
    chosen = jnp.sum(q_values * action_hot, axis=1)
    soft_top = jax.nn.logsumexp(q_values, axis=1)
    return sample_meta[:, 1] * (
        jnp.square(chosen - sample_meta[:, 0]) + cql_alpha * (soft_top - chosen)
    )


def block_forward(stream, w_first, w_middle, w_last, gain_rows):
    g_one, b_one, g_two, b_two, g_three, b_three = gain_parts(gain_rows)
    first_out = jnp.einsum(
        "fpc,cm->fpm", stream.astype(jnp.bfloat16), w_first, preferred_element_type=jnp.float32
    )
    tap_rows = spread_taps(norm_act(first_out, g_one, b_one).astype(jnp.bfloat16))
    middle = jnp.einsum("fpk,km->fpm", tap_rows, w_middle, preferred_element_type=jnp.float32)
    second = norm_act(middle, g_two, b_two).astype(jnp.bfloat16)
    last_out = jnp.einsum("fpm,cm->fpc", second, w_last, preferred_element_type=jnp.float32)
    output = residual_tail(stream, last_out, g_three, b_three)
    return (output, (stream, first_out, tap_rows, middle, second, last_out))


def block_backward(grad_out, kept_acts, w_first, w_middle, w_last, gain_rows):
    stream, first_out, tap_rows, middle, second, last_out = kept_acts
    g_one, b_one, g_two, b_two, g_three, b_three = gain_parts(gain_rows)
    unused, pull_tail = jax.vjp(residual_tail, stream, last_out, g_three, b_three)
    grad_stream, grad_last, grad_g3, grad_b3 = pull_tail(grad_out)
    grad_last = grad_last.astype(jnp.bfloat16)
    grad_w_last = jnp.einsum("fpc,fpm->cm", grad_last, second, preferred_element_type=jnp.float32)
    grad_second = jnp.einsum("fpc,cm->fpm", grad_last, w_last, preferred_element_type=jnp.float32)
    unused, pull_two = jax.vjp(norm_act, middle, g_two, b_two)
    grad_middle, grad_g2, grad_b2 = pull_two(grad_second)
    grad_middle = grad_middle.astype(jnp.bfloat16)
    grad_w_middle = jnp.einsum(
        "fpk,fpm->km", tap_rows, grad_middle, preferred_element_type=jnp.float32
    )
    grad_taps = jnp.einsum("fpm,km->fpk", grad_middle, w_middle, preferred_element_type=jnp.float32)
    unused, pull_taps = jax.vjp(spread_taps, jnp.zeros(first_out.shape, jnp.float32))
    (grad_act,) = pull_taps(grad_taps)
    unused, pull_one = jax.vjp(norm_act, first_out, g_one, b_one)
    grad_first, grad_g1, grad_b1 = pull_one(grad_act)
    grad_first = grad_first.astype(jnp.bfloat16)
    grad_w_first = jnp.einsum(
        "fpc,fpm->cm", stream.astype(jnp.bfloat16), grad_first, preferred_element_type=jnp.float32
    )
    grad_in = grad_stream + jnp.einsum(
        "fpm,cm->fpc", grad_first, w_first, preferred_element_type=jnp.float32
    )
    gain_grad = jnp.stack(
        [jnp.concatenate([grad_g1, grad_g2, grad_g3]), jnp.concatenate([grad_b1, grad_b2, grad_b3])]
    )
    return (grad_in, grad_w_first, grad_w_middle, grad_w_last, gain_grad)


def head_pass(pooled, sample_meta, head_local, support):
    rows_dev, channels = pooled.shape
    ns_size = lax.axis_size("ns")
    owners = lax.axis_size("dp")
    col_width = channels // ns_size
    meta_copies = jnp.broadcast_to(
        sample_meta[:, None, :], (rows_dev, ns_size, sample_meta.shape[1])
    )
    col_share, meta_all = (
        lax.all_to_all(
            pooled.reshape(rows_dev, ns_size, col_width),
            "ns",
            split_axis=1,
            concat_axis=0,
            tiled=True,
        ),
        lax.all_to_all(meta_copies, "ns", split_axis=1, concat_axis=0, tiled=True),
    )
    col_share = col_share.reshape(ns_size * rows_dev, col_width)
    meta_all = meta_all.reshape(ns_size * rows_dev, sample_meta.shape[1])
    game_col = meta_all[:, 2].astype(jnp.float32).astype(jnp.int32)
    game_hot = (game_col[:, None] == jnp.arange(owners, dtype=jnp.int32)[None, :]).astype(
        jnp.float32
    )
    earlier = jnp.cumsum(game_hot, axis=0) - game_hot
    slot_idx = jnp.sum(earlier * game_hot, axis=1).astype(jnp.int32)
    capacity = 2 * ns_size * rows_dev // owners
    place_idx = game_col * capacity + slot_idx
    dispatch = (
        jnp.arange(owners * capacity, dtype=jnp.int32)[:, None] == place_idx[None, :]
    ).astype(jnp.bfloat16)
    feat_buckets = jnp.dot(dispatch, col_share, preferred_element_type=jnp.float32).astype(
        jnp.bfloat16
    )
    meta_buckets = jnp.dot(dispatch, meta_all, preferred_element_type=jnp.float32).astype(
        jnp.bfloat16
    )
    feat_rows, meta_rows = (
        lax.all_to_all(
            feat_buckets.reshape(owners, capacity, col_width),
            "dp",
            split_axis=0,
            concat_axis=0,
            tiled=True,
        ),
        lax.all_to_all(
            meta_buckets.reshape(owners, capacity, sample_meta.shape[1]),
            "dp",
            split_axis=0,
            concat_axis=0,
            tiled=True,
        ),
    )
    feat_rows = feat_rows.reshape(owners * capacity, col_width)
    meta_rows = meta_rows.reshape(owners * capacity, sample_meta.shape[1]).astype(jnp.float32)
    logit_part = jnp.dot(feat_rows, head_local, preferred_element_type=jnp.float32)
    logits = lax.psum(logit_part, "ns")
    row_loss, pullback = jax.vjp(lambda logit_in: sample_loss(logit_in, meta_rows, support), logits)
    (grad_logits,) = pullback(jnp.ones_like(row_loss))
    grad_low = grad_logits.astype(jnp.bfloat16)
    grad_head = jnp.einsum("rc,ro->co", feat_rows, grad_low, preferred_element_type=jnp.float32)
    grad_feat = jnp.einsum(
        "ro,co->rc", grad_low, head_local, preferred_element_type=jnp.float32
    ).astype(jnp.bfloat16)
    row_block = owners * capacity // ns_size
    mine = (
        jnp.arange(owners * capacity, dtype=jnp.int32) // row_block == lax.axis_index("ns")
    ).astype(jnp.float32)
    loss_part = jnp.sum(row_loss * mine)
    weight_part = jnp.sum(meta_rows[:, 1] * mine)
    returned = lax.all_to_all(
        grad_feat.reshape(owners, capacity, col_width),
        "dp",
        split_axis=0,
        concat_axis=0,
        tiled=True,
    )
    back_rows = jnp.einsum(
        "kr,kc->rc",
        dispatch,
        returned.reshape(owners * capacity, col_width),
        preferred_element_type=jnp.float32,
    ).astype(jnp.bfloat16)
    grad_pooled = lax.all_to_all(
        back_rows.reshape(ns_size, rows_dev, col_width),
        "ns",
        split_axis=0,
        concat_axis=2,
        tiled=True,
    )
    return (grad_pooled.reshape(rows_dev, channels), grad_head, loss_part, weight_part)


def newton_step(current, gram_mat):
    poly_mat = coef_b * gram_mat + coef_c * jnp.einsum(
        "...ij,...jk->...ik", gram_mat, gram_mat, precision=highest
    )
    return coef_a * current + jnp.einsum("...ri,...ij->...rj", current, poly_mat, precision=highest)


def adam_step(weight, first, second, grad_in, rate, decay):
    first_new = decay_moment * first + (1.0 - decay_moment) * grad_in
    second_new = beta_second * second + (1.0 - beta_second) * grad_in * grad_in
    normed = (
        first_new
        / (1.0 - decay_moment**STEP)
        / (jnp.sqrt(second_new / (1.0 - beta_second**STEP)) + adam_eps)
    )
    return (weight - rate * (normed + decay * weight), first_new, second_new)


def local(
    frames,
    game_ids,
    actions,
    groups,
    targets,
    w_pair,
    w_spatial,
    mom_pair,
    mom_spatial,
    head_table,
    head_first,
    head_second,
    norm_params,
    norm_first,
    norm_second,
):
    pair_full, spatial_full = (
        lax.all_gather(w_pair.astype(jnp.bfloat16), "ns", axis=2, tiled=True),
        lax.all_gather(w_spatial.astype(jnp.bfloat16), "ns", axis=1, tiled=True),
    )
    head_local = head_table[0].astype(jnp.bfloat16)
    support = value_max * (jnp.arange(ATOMS, dtype=jnp.float32) * (2.0 / (ATOMS - 1)) - 1.0)
    pair_grad = jnp.zeros(pair_full.shape, jnp.float32)
    spatial_grad = jnp.zeros(spatial_full.shape, jnp.float32)
    head_grad = jnp.zeros(head_local.shape, jnp.float32)
    gain_grad = jnp.zeros(norm_params.shape, jnp.float32)
    loss_acc = jnp.zeros((), jnp.float32)
    weight_acc = jnp.zeros((), jnp.float32)
    for micro_idx in range(MB):
        sample_meta = jnp.stack(
            [
                targets[micro_idx].astype(jnp.float32),
                0.25 + 0.75 * groups[micro_idx].astype(jnp.float32),
                game_ids[micro_idx, :, 0].astype(jnp.float32),
                actions[micro_idx].astype(jnp.float32),
            ],
            axis=1,
        ).astype(jnp.bfloat16)
        stream = frames[micro_idx].astype(jnp.float32)
        kept_all = []
        for layer_idx in range(BLOCKS):
            stream, kept_acts = block_forward(
                stream,
                pair_full[layer_idx, 0],
                spatial_full[layer_idx],
                pair_full[layer_idx, 1],
                norm_params[layer_idx],
            )
            kept_all.append(kept_acts)
        pooled = jnp.mean(stream, axis=1).astype(jnp.bfloat16)
        grad_pooled, grad_head_mb, loss_part, weight_part = head_pass(
            pooled, sample_meta, head_local, support
        )
        head_grad = head_grad + grad_head_mb
        loss_acc = loss_acc + loss_part
        weight_acc = weight_acc + weight_part
        grad_stream = jnp.broadcast_to(
            grad_pooled.astype(jnp.float32)[:, None, :] / stream.shape[1], stream.shape
        )
        first_list = [None] * BLOCKS
        middle_list = [None] * BLOCKS
        last_list = [None] * BLOCKS
        gain_list = [None] * BLOCKS
        for layer_idx in reversed(range(BLOCKS)):
            (
                grad_stream,
                first_list[layer_idx],
                middle_list[layer_idx],
                last_list[layer_idx],
                gain_list[layer_idx],
            ) = block_backward(
                grad_stream,
                kept_all[layer_idx],
                pair_full[layer_idx, 0],
                spatial_full[layer_idx],
                pair_full[layer_idx, 1],
                norm_params[layer_idx],
            )
        pair_grad = pair_grad + jnp.stack(
            [jnp.stack([first_list[idx], last_list[idx]]) for idx in range(BLOCKS)]
        )
        spatial_grad = spatial_grad + jnp.stack(middle_list)
        gain_grad = gain_grad + jnp.stack(gain_list)
    pair_share, spatial_share = (
        lax.psum_scatter(pair_grad, "ns", scatter_dimension=2, tiled=True),
        lax.psum_scatter(spatial_grad, "ns", scatter_dimension=1, tiled=True),
    )
    pair_share, spatial_share = lax.psum((pair_share, spatial_share), "dp")
    gain_sum, loss_sum, weight_total = lax.psum((gain_grad, loss_acc, weight_acc), ("dp", "ns"))
    lead = (lax.axis_index("dp") == 0).astype(jnp.float32)
    head_sq = jnp.sum(jnp.square(head_grad))
    gain_sq = jnp.sum(jnp.square(gain_sum))
    joint_sums = lax.psum(
        (
            lead * jnp.sum(jnp.square(mom_pair), axis=(2, 3)),
            lead * jnp.sum(mom_pair * pair_share, axis=(2, 3)),
            lead * jnp.sum(jnp.square(pair_share), axis=(2, 3)),
            lead * jnp.sum(jnp.square(mom_spatial), axis=(1, 2)),
            lead * jnp.sum(mom_spatial * spatial_share, axis=(1, 2)),
            lead * jnp.sum(jnp.square(spatial_share), axis=(1, 2)),
            head_sq,
        ),
        ("dp", "ns"),
    )
    pair_mm, pair_mg, pair_gg, spatial_mm, spatial_mg, spatial_gg, head_total = joint_sums
    grad_norm = (
        jnp.sqrt(jnp.sum(pair_gg) + jnp.sum(spatial_gg) + head_total + gain_sq) / weight_total
    )
    factor = jnp.minimum(1.0, clip_limit / grad_norm) / weight_total
    pair_moment = decay_moment * mom_pair + factor * pair_share
    spatial_moment = decay_moment * mom_spatial + factor * spatial_share
    pair_frob = (
        decay_moment * decay_moment * pair_mm
        + 2.0 * decay_moment * factor * pair_mg
        + factor * factor * pair_gg
    )
    spatial_frob = (
        decay_moment * decay_moment * spatial_mm
        + 2.0 * decay_moment * factor * spatial_mg
        + factor * factor * spatial_gg
    )
    pair_cur = pair_moment / (jnp.sqrt(pair_frob)[:, :, None, None] + 1e-07)
    spatial_cur = spatial_moment / (jnp.sqrt(spatial_frob)[:, None, None] + 1e-07)
    for sweep_idx in range(NS_ITERS):
        pair_gram, spatial_gram = lax.psum(
            (
                jnp.einsum("...ri,...rj->...ij", pair_cur, pair_cur, precision=highest),
                jnp.einsum("...ri,...rj->...ij", spatial_cur, spatial_cur, precision=highest),
            ),
            "ns",
        )
        pair_cur = newton_step(pair_cur, pair_gram)
        spatial_cur = newton_step(spatial_cur, spatial_gram)
    pair_new = w_pair - rate_muon * (decay_muon * w_pair + 0.2 * math.sqrt(C) * pair_cur)
    spatial_new = w_spatial - rate_muon * (
        decay_muon * w_spatial + 0.2 * math.sqrt(9 * MID) * spatial_cur
    )
    head_new, head_first_new, head_second_new = adam_step(
        head_table, head_first, head_second, factor * head_grad[None], rate_head, decay_head
    )
    norm_new, norm_first_new, norm_second_new = adam_step(
        norm_params, norm_first, norm_second, factor * gain_sum, rate_gain, 0.0
    )
    return (
        pair_new,
        spatial_new,
        pair_moment,
        spatial_moment,
        head_new,
        head_first_new,
        head_second_new,
        norm_new,
        norm_first_new,
        norm_second_new,
        grad_norm,
        loss_sum,
        weight_total,
    )


def solution(mesh):
    in_specs = (
        P(None, ("dp", "ns"), None, None),
        P(None, ("dp", "ns"), None),
        P(None, ("dp", "ns")),
        P(None, ("dp", "ns")),
        P(None, ("dp", "ns")),
        P(None, None, "ns", None),
        P(None, "ns", None),
        P(None, None, "ns", None),
        P(None, "ns", None),
        P("dp", "ns", None),
        P("dp", "ns", None),
        P("dp", "ns", None),
        P(),
        P(),
        P(),
    )
    out_specs = (
        P(None, None, "ns", None),
        P(None, "ns", None),
        P(None, None, "ns", None),
        P(None, "ns", None),
        P("dp", "ns", None),
        P("dp", "ns", None),
        P("dp", "ns", None),
        P(),
        P(),
        P(),
        P(),
        P(),
        P(),
    )
    return jax.shard_map(local, mesh=mesh, in_specs=in_specs, out_specs=out_specs, check_vma=False)
```

profile of v0, /device:TPU:0, one launch (start us, length us, event | category | flops | bytes accessed | tf_op | source)
XLA Modules:
  0.0 1985.2 jit_solution(2024406521593554916)
XLA Ops:
  77.0 24.5 %all-gather.3.cloned.1.call-done = bf16[2,2,2048,512]{3,2,1,0:T(8,128)(2,1)} async-done(((bf16[2,2,512,512]{3,2,1,0:T(8,128)(2,1)}), bf16[2,2,2048,512]{3,2,1,0:T(8,128)(2,1)}) %all-gather.3.cloned.1.call-update) | async-done | bytes 8388624 | tf_op jit(solution)/shard_map/all_gather | solution.py:267
  123.3 8.4 copy.1091
  134.6 7.8 copy.1102
  143.9 7.6 reshape.1347
  151.5 8.3 reshape.1351
  218.7 8.1 slice_bitcast_fusion
  240.2 8.3 fusion.222
  274.5 7.4 multiply_convert_fusion
  284.7 7.4 copy.1094
  298.8 7.4 copy.1105
  314.7 8.3 reshape.1352
  373.3 8.3 fusion.229
  426.2 11.4 multiply_reduce_fusion.13
  508.9 14.2 all-reduce.56.cloned.1.call-done
  590.1 17.1 multiply_reduce_fusion.27
  635.8 8.0 reshape.1349
  643.9 10.8 fusion.15
  654.6 10.1 fusion.216
  690.9 9.0 fusion.13
  700.0 10.0 fusion.217
  729.2 7.5 copy.887
  741.4 7.5 copy.976
  760.8 9.4 multiply_reduce_fusion.8
  812.5 8.9 fusion.11
  821.4 10.1 fusion.214
  836.8 10.1 multiply_reduce_fusion.6
  889.0 9.1 fusion.9
  898.1 10.1 fusion.215
  927.4 7.5 copy.903
  983.3 7.8 maximum_bitcast_fusion.1
  991.1 12.4 maximum_add_fusion.1
  1018.1 7.9 convolution_bitcast_fusion.1
  1026.0 12.4 maximum_add_fusion
  1050.9 103.0 %reduce-scatter.3.cloned.1.call-done = f32[2,2,512,512]{2,3,1,0:T(8,128)} async-done(((f32[2,2,2048,512]{2,3,1,0:T(8,128)}), f32[2,2,512,512]{2,3,1,0:T(8,128)}) %reduce-scatter.3.cloned.1.call-update) | async-done | bytes 4194320 | tf_op jit(solution)/shard_map/reduce_scatter | solution.py:334
  1153.9 174.2 %reduce-scatter.5.cloned.1.call-done = f32[2,1152,512]{2,1,0:T(8,128)} async-done(((f32[2,4608,512]{2,1,0:T(8,128)}), f32[2,1152,512]{2,1,0:T(8,128)}) %reduce-scatter.5.cloned.1.call-update) | async-done | bytes 4718608 | tf_op jit(solution)/shard_map/reduce_scatter | solution.py:335
  1338.5 177.7 %all-reduce.50.cloned.1.call-done = (f32[2,2,512,512]{2,3,1,0:T(8,128)}, f32[2,1152,512]{2,1,0:T(8,128)}) async-done(((f32[2,2,512,512]{2,3,1,0:T(8,128)}, f32[2,1152,512]{2,1,0:T(8,128)}), (f32[2,2,512,512]{2,3,1,0:T(8,128)}, f32[2,1152,512]{2,1,0:T(8,128)})) %all-reduce.50.cloned.1.call-update) | async-done | bytes 8912912 | tf_op jit(solution)/shard_map/psum | solution.py:337
  1525.1 41.3 %all-reduce.40 = (f32[]{:T(128)}, f32[2,2]{1,0:T(2,128)S(1)}, f32[2]{0:T(128)S(1)}, f32[]{:T(128)}, f32[2,2,3072]{2,1,0:T(2,128)S(1)}, /*index=5*/f32[2,2]{1,0:T...) all-reduce(f32[]{:T(128)S(6)} %add.871, ...), channel_id=1, replica_groups=mesh['dp'=8,'ns'=4] {'dp','ns'}, use_global_device_ids=true, to_apply=%region_6.7 | all-reduce | flops 12309 | bytes 98472 | tf_op jit(solution)/shard_map/psum | solution.py:338
  1580.8 10.5 fusion.148
  1591.3 8.9 fusion.95
  1600.3 138.6 %all-reduce.54.cloned.1.call-done = (f32[2,2,512,512]{3,2,1,0:T(8,128)}, f32[2,512,512]{2,1,0:T(8,128)}) async-done(((f32[2,2,512,512]{3,2,1,0:T(8,128)}, f32[2,512,512]{2,1,0:T(8,128)}), (f32[2,2,512,512]{3,2,1,0:T(8,128)}, f32[2,512,512]{2,1,0:T(8,128)})) %all-reduce.54.cloned.1.call-update) | async-done | bytes 6291472 | tf_op jit(solution)/shard_map/psum | solution.py:374
  1744.8 12.4 convolution_add_fusion.1
  1757.2 10.0 fusion.237
  1767.2 7.9 fusion.233
  1775.1 9.4 multiply_add_fusion.1
  1786.5 8.4 fusion.234
  1820.6 113.3 %all-reduce.52.cloned.1.call-done = (f32[2,2,512,512]{3,2,1,0:T(8,128)}, f32[2,512,512]{2,1,0:T(8,128)}) async-done(((f32[2,2,512,512]{3,2,1,0:T(8,128)}, f32[2,512,512]{2,1,0:T(8,128)}), (f32[2,2,512,512]{3,2,1,0:T(8,128)}, f32[2,512,512]{2,1,0:T(8,128)})) %all-reduce.52.cloned.1.call-update) | async-done | bytes 6291472 | tf_op jit(solution)/shard_map/psum | solution.py:374
  1939.8 14.9 multiply_subtract_fusion
  1961.8 9.8 multiply_subtract_fusion.1
  (1164 shorter events, 794.6 us)
Async XLA Ops:
  7.2 94.4 %all-gather.3.cloned.1.call-start = ((), (), s32[]{:S(2)}) async-start(), calls=%async_computation.14 | async-start | bytes 10485760 | tf_op jit(solution)/shard_map/all_gather | solution.py:267
  11.1 207.6 %all-gather.5.cloned.1.call-start = ((), (), s32[]{:S(2)}) async-start(), calls=%async_computation.15 | async-start | bytes 11796480 | tf_op jit(solution)/shard_map/all_gather | solution.py:268
  16.2 37.8 %all-to-all-start.2 = ((bf16[4,4,4]{2,0,1:T(4,128)(2,1)}), bf16[4,4,4]{2,0,1:T(4,128)(2,1)S(1)}, u32[]{:S(2)}, u32[]{:S(2)}) async-start(bf16[4,4,4]{2,0,1:T(4,128)(2,1)} %broadcast_in_dim.61), calls=%async_computation.2 | async-start | bytes 8192 | tf_op jit(solution)/shard_map/all_to_all | solution.py:154
  22.0 187.6 %copy-start.209 = (f32[1,512]{1,0:T(1,128)}, f32[1,512]{1,0:T(1,128)S(1)}, u32[]{:S(2)}) copy-start(f32[1,512]{1,0:T(1,128)S(1)} %get-tuple-element.376) | copy-start | bytes 6148
  22.0 187.6 %copy-start.211 = (f32[1,512]{1,0:T(1,128)}, f32[1,512]{1,0:T(1,128)S(1)}, u32[]{:S(2)}) copy-start(f32[1,512]{1,0:T(1,128)S(1)} %get-tuple-element.377) | copy-start | bytes 6148
  22.0 345.9 %copy-start.213 = (f32[1,512]{1,0:T(1,128)}, f32[1,512]{1,0:T(1,128)S(1)}, u32[]{:S(2)}) copy-start(f32[1,512]{1,0:T(1,128)S(1)} %get-tuple-element.308) | copy-start | bytes 6148
  48.3 226.2 %copy-start.176 = (f32[1,2048]{1,0:T(1,128)}, f32[1,2048]{1,0:T(1,128)S(1)}, u32[]{:S(2)}) copy-start(f32[1,2048]{1,0:T(1,128)S(1)} %get-tuple-element.384) | copy-start | bytes 24580
  48.3 226.2 %copy-start.180 = (f32[1,2048]{1,0:T(1,128)}, f32[1,2048]{1,0:T(1,128)S(1)}, u32[]{:S(2)}) copy-start(f32[1,2048]{1,0:T(1,128)S(1)} %get-tuple-element.385) | copy-start | bytes 24580
  54.6 8.9 all-to-all-start
  65.4 10.7 all-to-all-start.1
  123.3 19.0 copy-start.44
  426.2 23.3 %copy-start.293 = (s32[16]{0:T(128)S(1)}, s32[16]{0:T(128)}, u32[]{:S(2)}) copy-start(s32[16]{0:T(128)} %copy-done.292) | copy-start | bytes 196
  426.2 32.6 %copy-start.295 = (s32[16]{0:T(128)S(1)}, s32[16]{0:T(128)}, u32[]{:S(2)}) copy-start(s32[16]{0:T(128)} %copy-done.294) | copy-start | bytes 196
  426.2 53.1 %copy-start.291 = (f32[32,4]{0,1:T(4,128)S(1)}, f32[32,4]{0,1:T(4,128)}, u32[]{:S(2)}) copy-start(f32[32,4]{0,1:T(4,128)} %reshape.1304) | copy-start | bytes 1540
  437.6 50.4 %copy-start.224 = (f32[4,32]{1,0:T(4,128)S(1)}, f32[4,32]{1,0:T(4,128)}, u32[]{:S(2)}) copy-start(f32[4,32]{1,0:T(4,128)} %copy-done.223) | copy-start | bytes 1540
  438.2 7.9 all-to-all-start.8
  446.2 7.9 all-to-all-start.4
  454.1 10.4 all-to-all-start.9
  464.5 9.0 all-to-all-start.5
  467.8 23.8 %copy-start.143 = (bf16[32,512]{1,0:T(8,128)(2,1)}, bf16[32,512]{1,0:T(8,128)(2,1)S(1)}, u32[]{:S(2)}) copy-start(bf16[32,512]{1,0:T(8,128)(2,1)S(1)} %reshape.1292) | copy-start | bytes 98308
  473.5 8.8 all-to-all-start.3
  476.8 46.4 %all-reduce.56.cloned.1.call-start = ((), (), s32[]{:S(2)}) async-start(), calls=%async_computation.21 | async-start | bytes 524288 | tf_op jit(solution)/shard_map/psum | solution.py:194
  477.0 17.2 copy-start.145
  501.2 28.5 %copy-start.290 = (f32[51]{0:T(128)S(1)}, f32[51]{0:T(128)}, u32[]{:S(2)}) copy-start(f32[51]{0:T(128)} %copy-done.289) | copy-start | bytes 616
  549.7 40.2 %copy-start.151 = (f32[32,64]{1,0:T(8,128)S(1)}, f32[32,64]{1,0:T(8,128)}, u32[]{:S(2)}) copy-start(f32[32,64]{1,0:T(8,128)} %mul.1851) | copy-start | bytes 24580
  549.7 40.2 %copy-start.159 = (f32[4,32]{1,0:T(4,128)S(1)}, f32[4,32]{1,0:T(4,128)}, u32[]{:S(2)}) copy-start(f32[4,32]{1,0:T(4,128)} %copy-done.158) | copy-start | bytes 1540
  549.7 40.3 %copy-start.162 = (f32[4,32]{1,0:T(4,128)S(1)}, f32[4,32]{1,0:T(4,128)}, u32[]{:S(2)}) copy-start(f32[4,32]{1,0:T(4,128)} %copy-done.161) | copy-start | bytes 1540
  549.7 40.3 %copy-start.190 = (f32[4,32]{1,0:T(4,128)S(1)}, f32[4,32]{1,0:T(4,128)}, u32[]{:S(2)}) copy-start(f32[4,32]{1,0:T(4,128)} %copy-done.189) | copy-start | bytes 1540
  549.7 40.3 %copy-start.192 = (f32[4,32]{1,0:T(4,128)S(1)}, f32[4,32]{1,0:T(4,128)}, u32[]{:S(2)}) copy-start(f32[4,32]{1,0:T(4,128)} %copy-done.191) | copy-start | bytes 1540
  549.7 40.3 %copy-start.194 = (f32[32,64]{1,0:T(8,128)S(1)}, f32[32,64]{1,0:T(8,128)}, u32[]{:S(2)}) copy-start(f32[32,64]{1,0:T(8,128)} %add.914) | copy-start | bytes 24580
  549.7 40.3 %copy-start.195 = (f32[32,64]{1,0:T(8,128)S(1)}, f32[32,64]{1,0:T(8,128)}, u32[]{:S(2)}) copy-start(f32[32,64]{1,0:T(8,128)} %add.919) | copy-start | bytes 24580
  549.7 40.3 %copy-start.196 = (f32[32,64]{1,0:T(8,128)S(1)}, f32[32,64]{1,0:T(8,128)}, u32[]{:S(2)}) copy-start(f32[32,64]{1,0:T(8,128)} %mul.1847) | copy-start | bytes 24580
  549.8 40.3 %copy-start.201 = (f32[4,32]{1,0:T(4,128)S(1)}, f32[4,32]{1,0:T(4,128)}, u32[]{:S(2)}) copy-start(f32[4,32]{1,0:T(4,128)} %copy-done.199) | copy-start | bytes 1540
  549.8 40.3 %copy-start.205 = (f32[4,32]{1,0:T(4,128)S(1)}, f32[4,32]{1,0:T(4,128)}, u32[]{:S(2)}) copy-start(f32[4,32]{1,0:T(4,128)} %copy-done.203) | copy-start | bytes 1540
  549.8 40.3 %copy-start.246 = (f32[4,32]{1,0:T(4,128)S(1)}, f32[4,32]{1,0:T(4,128)}, u32[]{:S(2)}) copy-start(f32[4,32]{1,0:T(4,128)} %copy-done.245) | copy-start | bytes 1540
  549.8 40.3 %copy-start.248 = (f32[4,32]{1,0:T(4,128)S(1)}, f32[4,32]{1,0:T(4,128)}, u32[]{:S(2)}) copy-start(f32[4,32]{1,0:T(4,128)} %copy-done.247) | copy-start | bytes 1540
  551.2 55.9 %copy-start.136 = (bf16[32,918]{1,0:T(8,128)(2,1)}, bf16[32,918]{1,0:T(8,128)(2,1)S(1)}, u32[]{:S(2)}) copy-start(bf16[32,918]{1,0:T(8,128)(2,1)S(1)} %get-tuple-element.329) | copy-start | bytes 176260
  553.9 10.3 all-to-all-start.6
  564.3 9.0 all-to-all-start.10
  573.3 7.9 all-to-all-start.7
  581.3 7.9 all-to-all-start.11
  584.5 569.4 %reduce-scatter.3.cloned.1.call-start = ((), (), s32[]{:S(2)}) async-start(), calls=%async_computation.16 | async-start | bytes 20971520 | tf_op jit(solution)/shard_map/reduce_scatter | solution.py:334
  590.1 17.1 copy-start.254
  590.1 17.1 copy-start.5
  1003.5 324.6 %reduce-scatter.5.cloned.1.call-start = ((), (), s32[]{:S(2)}) async-start(), calls=%async_computation.17 | async-start | bytes 23592960 | tf_op jit(solution)/shard_map/reduce_scatter | solution.py:335
  1038.4 477.8 %all-reduce.50.cloned.1.call-start = ((), (), s32[]{:S(2)}) async-start(), calls=%async_computation.18 | async-start | bytes 17825792 | tf_op jit(solution)/shard_map/psum | solution.py:337
  1328.3 410.6 %all-reduce.54.cloned.1.call-start = ((), (), s32[]{:S(2)}) async-start(), calls=%async_computation.20 | async-start | bytes 12582912 | tf_op jit(solution)/shard_map/psum | solution.py:374
  1600.2 333.7 %all-reduce.52.cloned.1.call-start = ((), (), s32[]{:S(2)}) async-start(), calls=%async_computation.19 | async-start | bytes 12582912 | tf_op jit(solution)/shard_map/psum | solution.py:374
  (292 other events, 1669.5 us)
Sparse Core Ops, SparseCore 0:
  11.1 90.3 all-gather.2
  103.9 96.3 all-gather.4
  480.5 42.5 all-reduce.55
  1003.6 150.2 reduce-scatter.2
  1157.2 170.8 reduce-scatter.4
  1330.4 185.7 all-reduce.49
  1600.4 138.4 all-reduce.53
  1795.1 138.7 all-reduce.51
where the time goes:
time: 2000 us; the launch traced here: 1990 us
  waiting for transfers between devices  788 us (39%)
  local copies, waits for them, and re-layouts  527 us (26%)
  matrix products  304 us (15%)
  other arithmetic  249 us (12%)
  starting transfers between devices  47.6 us (2%)
  blocking collectives  41.3 us (2%)
  between operations  27.4 us (1%)
    psum x2, waiting for transfers between devices, local(): lax.psum((jnp.einsum('...ri,...rj->...ij', pair_cur, pair_cur, precision=...  252 us
    psum x1, waiting for transfers between devices, local(): pair_share, spatial_share = lax.psum((pair_share, spatial_share), 'dp')  178 us
    reduce_scatter x1, waiting for transfers between devices, local(): lax.psum_scatter(spatial_grad, 'ns', scatter_dimension=1, tiled=True)  174 us
    reshape x22, local copies, waits for them, and re-layouts, group_norm(): ((grouped - center) * lax.rsqrt(spread + eps_norm)).reshape(frame_count,...  112 us
    reduce_scatter x1, waiting for transfers between devices, local(): lax.psum_scatter(pair_grad, 'ns', scatter_dimension=2, tiled=True)  103 us
    unnamed x676, local copies, waits for them, and re-layouts  81.3 us
    convert_element_type x12, local copies, waits for them, and re-layouts, block_backward(): grad_middle = grad_middle.astype(jnp.bfloat16)  57.4 us
    slice x36, local copies, waits for them, and re-layouts, spread_taps(): padded[:, row_off:row_off + SIDE, col_off:col_off + SIDE, :]  52.2 us
  transfers between devices with their start and end apart: 20, of which 18 were waited for; matrix products, arithmetic and copies ran while one was open for 14% of the time, Pallas kernels for 0%

commit v1 on v0

v1 whole, which is shorter than its diff:
```python
import functools
import math

import jax
import jax.numpy as jnp
import numpy as np
from jax import lax
from jax.experimental import pallas as pl
from jax.experimental.pallas import tpu as pltpu
from jax.sharding import PartitionSpec as P

C = 2048
MID = 512
ACTIONS = 18
ATOMS = 51
GROUPS = 32
SIDE = 11
PIX = SIDE * SIDE
BLOCKS = 2
MB = 2
STEP = 10
SEG = 64
HPAD = ACTIONS * SEG
HOUT = ACTIONS * ATOMS

bf16 = jnp.bfloat16
f32 = jnp.float32

eps_norm = 1e-05
decay_moment = 0.5
beta_second = 0.95
adam_eps = 1e-08
rate_muon = 0.2
decay_muon = 0.01
rate_head = 0.02
decay_head = 0.01
rate_gain = 0.05
clip_limit = 0.01
cql_alpha = 0.05
value_max = 3.0
coef_a = 3.4445
coef_b = -4.775
coef_c = 2.0315

FROWS = 128
FPB = 2
BROWS = FPB * FROWS
TAPS = [(dr, dc) for dr in (-1, 0, 1) for dc in (-1, 0, 1)]
MIB = 1024 * 1024


def tap_masks():
    pixel = np.arange(FROWS)
    row, col = pixel // SIDE, pixel % SIDE
    masks = [
        (pixel < PIX) & (row + dr >= 0) & (row + dr < SIDE) & (col + dc >= 0) & (col + dc < SIDE)
        for dr, dc in TAPS
    ]
    return np.repeat(np.stack(masks).astype(np.float32).reshape(9 * FROWS, 1), 128, axis=1)


class Net:
    def __init__(self, dp, ns):
        self.dp, self.ns = dp, ns
        self.ns_bits = [1 << i for i in range(ns.bit_length() - 1)]
        self.dp_bits = [1 << i for i in range(dp.bit_length() - 1)]
        self.plain = not (dp == 8 and ns == 4)

    def swap(self, value, axis, bit):
        pairs = []
        for d in range(self.dp):
            for n in range(self.ns):
                partner = (d ^ bit) * self.ns + n if axis == "dp" else d * self.ns + (n ^ bit)
                pairs.append((d * self.ns + n, partner))
        return lax.ppermute(value, ("dp", "ns"), pairs)

    def add_all(self, value, axes=("dp", "ns")):
        for axis in axes:
            for bit in self.dp_bits if axis == "dp" else self.ns_bits:
                value = value + self.swap(value, axis, bit)
        return value


def pick(value, index, axis):
    return lax.dynamic_index_in_dim(value, index, axis, keepdims=False)


def bit_of(index, shift):
    return lax.rem(lax.div(index, 1 << shift), 2)


class Shards:
    def __init__(self, arrays, offsets):
        self.arrays, self.offsets = arrays, offsets


def gather_rows(net, shards):
    if net.plain:
        return [Shards((lax.all_gather(s.astype(bf16), "ns", axis=0, tiled=True),), None) for s in shards]
    core = bit_of(lax.axis_index("dp"), 0)
    parts, offsets, start = [], [], 0
    for s in shards:
        n = s.shape[0] // 4
        parts.append(pick(s.astype(bf16).reshape(2, 2, n, MID), core, 0))
        offsets.append((start, n))
        start += n
    own = jnp.concatenate(parts, axis=1) if len(parts) > 1 else parts[0]
    path_a, path_b = own[0:1], own[1:2]
    two_a = jnp.concatenate([path_a, net.swap(path_a, "ns", 1)], axis=0)
    two_b = jnp.concatenate([path_b, net.swap(path_b, "ns", 2)], axis=0)
    four_a = net.swap(two_a, "ns", 2)
    four_b = net.swap(two_b, "ns", 1)
    mine = jnp.concatenate([two_a, four_a, two_b, four_b], axis=0)
    other = net.swap(mine, "dp", 1)
    return [Shards((mine, other), off) for off in offsets]


def load_rows(shard, refs, pos_ref, buffer, sems):
    if shard.offsets is None:
        copy = pltpu.make_async_copy(refs[0], buffer, sems.at[0])
        copy.start()
        copy.wait()
        return
    start, n = shard.offsets
    here, core = pos_ref[0], pos_ref[1]
    copies = []
    for half, ref in enumerate(refs):
        for k in range(8):
            path = k // 4
            rel = k if path == 0 else (0, 2, 1, 3)[k - 4]
            place = ((here ^ rel) * 4 + (core ^ half) * 2 + path) * n
            copies.append(
                pltpu.make_async_copy(
                    ref.at[k, pl.ds(start, n)],
                    buffer.at[pl.ds(pl.multiple_of(place, 16), n)],
                    sems.at[half * 8 + k],
                )
            )
    for copy in copies:
        copy.start()
    for copy in copies:
        copy.wait()


def reduce_rows(net, grads):
    if net.plain:
        out = []
        for g in grads:
            share = lax.psum_scatter(g.astype(f32), "ns", scatter_dimension=0, tiled=True)
            out.append(lax.psum(share, "dp").astype(bf16))
        return out
    dp_idx, ns_idx = lax.axis_index("dp"), lax.axis_index("ns")
    core, z_low = bit_of(dp_idx, 0), bit_of(dp_idx, 1)
    x, y = bit_of(ns_idx, 0), bit_of(ns_idx, 1)
    sizes = [g.shape[0] // 16 for g in grads]

    def half(which):
        parts = [
            pick(g.reshape(4, 2, 2, n, MID), which, 1) for g, n in zip(grads, sizes, strict=True)
        ]
        return jnp.concatenate(parts, axis=2) if len(parts) > 1 else parts[0]

    got = net.swap(half(1 - core), "dp", 1)
    total = half(core) + got
    rows = total.shape[2]
    first = total[:, 0].reshape(2, 2, rows, MID)
    second = total[:, 1].reshape(2, 2, rows, MID)
    got_a = net.swap(pick(first, 1 - x, 1), "ns", 1)
    got_b = net.swap(pick(second, 1 - y, 0), "ns", 2)
    first = pick(first, x, 1) + got_a
    second = pick(second, y, 0) + got_b
    got_a = net.swap(pick(first, 1 - y, 0), "ns", 2)
    got_b = net.swap(pick(second, 1 - x, 0), "ns", 1)
    both = jnp.stack([pick(first, y, 0) + got_a, pick(second, x, 0) + got_b])
    kept = pick(both, z_low, 0) + net.swap(pick(both, 1 - z_low, 0), "dp", 2)
    kept = kept + net.swap(kept, "dp", 4)
    given = net.swap(kept, "dp", 2)
    low = z_low == 0
    whole = jnp.stack([jnp.where(low, kept, given), jnp.where(low, given, kept)])
    other = net.swap(whole, "dp", 1)
    lead = core == 0
    whole = jnp.stack([jnp.where(lead, whole, other), jnp.where(lead, other, whole)])
    out, start = [], 0
    for n in sizes:
        out.append(whole[:, :, start : start + n].reshape(4 * n, MID))
        start += n
    return out


GRAM_ROWS = MID + 64


def pack_grams(upper, lower):
    row = lax.broadcasted_iota(jnp.int32, (MID, MID), 0)
    col = lax.broadcasted_iota(jnp.int32, (MID, MID), 1)
    body = jnp.where(row < col, upper, lower)
    diag = jnp.sum(jnp.where(row == col, upper, 0.0), axis=-2, keepdims=True)
    tail = jnp.broadcast_to(diag, diag.shape[:-2] + (GRAM_ROWS - MID, MID))
    return jnp.concatenate([body, tail], axis=-2).astype(bf16)


def unpack_grams(packed):
    packed = packed.astype(f32)
    body, diag = packed[..., :MID, :], packed[..., MID : MID + 1, :]
    row = lax.broadcasted_iota(jnp.int32, (MID, MID), 0)
    col = lax.broadcasted_iota(jnp.int32, (MID, MID), 1)
    flip = jnp.swapaxes(body, -1, -2)
    upper = jnp.where(row < col, body, jnp.where(row == col, diag, flip))
    lower = jnp.where(row < col, flip, body)
    return upper, lower


def reduce_grams(net, packed):
    if net.plain:
        return lax.psum(packed.astype(f32), "ns").astype(bf16)
    n = packed.shape[0]
    core = bit_of(lax.axis_index("dp"), 0)
    mine = pick(packed.reshape(n, 2, 2, GRAM_ROWS // 4, MID), core, 1)
    first, second = mine[:, 0], mine[:, 1]
    first, second = first + net.swap(first, "ns", 1), second + net.swap(second, "ns", 2)
    first, second = first + net.swap(first, "ns", 2), second + net.swap(second, "ns", 1)
    mine = jnp.stack([first, second], axis=1)
    other = net.swap(mine, "dp", 1)
    lead = core == 0
    whole = jnp.stack([jnp.where(lead, mine, other), jnp.where(lead, other, mine)], axis=1)
    return whole.reshape(n, GRAM_ROWS, MID)


def sigmoid(v):
    return 0.5 * jnp.tanh(0.5 * v) + 0.5


def group_sum(t, size):
    tiles = t.shape[1] // 128
    u = jnp.concatenate([t[:, j * 128 : (j + 1) * 128] for j in range(tiles)], axis=0)
    lane = lax.broadcasted_iota(jnp.int32, u.shape, 1)
    step = 1
    while step < size:
        u = u + jnp.where(
            (lane & step) == 0, pltpu.roll(u, 128 - step, 1), pltpu.roll(u, step, 1)
        )
        step *= 2
    return jnp.concatenate([u[8 * j : 8 * j + 8] for j in range(tiles)], axis=1)


def live_rows():
    return lax.broadcasted_iota(jnp.int32, (FROWS, 128), 0) < PIX


def norm_stats(st, size):
    sums = group_sum(st[...], size) * (1.0 / (PIX * size))
    mean = sums[0:FPB]
    spread = jnp.maximum(sums[FPB : 2 * FPB] - mean * mean, 0.0)
    return mean, lax.rsqrt(spread + eps_norm)


def add_stats(st, f, lanes, v):
    st[f : f + 1, lanes] = jnp.sum(v, axis=0, keepdims=True)
    st[FPB + f : FPB + f + 1, lanes] = jnp.sum(v * v, axis=0, keepdims=True)


def units(width):
    for j in range(width // 128):
        for f in range(FPB):
            yield f, pl.ds(f * FROWS, FROWS), slice(j * 128, (j + 1) * 128)


def first_step(body):
    pl.when(pl.program_id(0) == 0)(body)


def reduce_kernel(shard, pos, x, gb, *rest):
    n = len(shard.arrays)
    refs, (h, xh, rs, buf, sems, acc, st) = rest[:n], rest[n:]

    @first_step
    def _():
        load_rows(shard, refs, pos, buf, sems)
        st[...] = jnp.zeros_like(st)

    for j in range(MID // 256):
        lanes = slice(j * 256, (j + 1) * 256)
        a = jnp.dot(x[...], buf[:, lanes], preferred_element_type=f32)
        acc[:, lanes] = a
        for f in range(FPB):
            add_stats(st, f, lanes, a[f * FROWS : (f + 1) * FROWS])
    norm_out(acc, st, gb, h, xh, rs)


def norm_out(acc, st, gb, h, xh, rs):
    mean, rstd = norm_stats(st, MID // GROUPS)
    rs[...] = jnp.zeros_like(rs)
    rs[0:FPB] = rstd
    live = live_rows()
    for f, rows, lanes in units(MID):
        v = jnp.where(live, (acc[rows, lanes] - mean[f : f + 1, lanes]) * rstd[f : f + 1, lanes], 0.0)
        xh[rows, lanes] = v.astype(bf16)
        v = v * gb[0:1, lanes] + gb[1:2, lanes]
        h[rows, lanes] = jnp.where(live, v * sigmoid(v), 0.0).astype(bf16)


def spread_taps(src, masks, taps):
    for f, rows, lanes in units(MID):
        v = src[rows, lanes].astype(f32)
        for k, (dr, dc) in enumerate(TAPS):
            shift = -(dr * SIDE + dc)
            t = v if shift == 0 else pltpu.roll(v, shift % FROWS, 0)
            t = t * masks[k * FROWS : (k + 1) * FROWS]
            taps[rows, k * MID + lanes.start : k * MID + lanes.stop] = t.astype(bf16)


def conv_kernel(shard, pos, src, masks, gb, *rest):
    n = len(shard.arrays)
    refs, (taps, u2, xh, rs, buf, sems, acc, st) = rest[:n], rest[n:]

    @first_step
    def _():
        load_rows(shard, refs, pos, buf, sems)
        st[...] = jnp.zeros_like(st)

    spread_taps(src, masks, taps)
    for j in range(MID // 256):
        lanes = slice(j * 256, (j + 1) * 256)
        a = jnp.dot(taps[...], buf[:, lanes], preferred_element_type=f32)
        acc[:, lanes] = a
        for f in range(FPB):
            add_stats(st, f, lanes, a[f * FROWS : (f + 1) * FROWS])
    norm_out(acc, st, gb, u2, xh, rs)


def expand_kernel(shard, last, pos, u2, x, gb, *rest):
    n = len(shard.arrays)
    refs, (xh, rs, out, buf, sems, acc, st) = rest[:n], rest[n:]

    @first_step
    def _():
        load_rows(shard, refs, pos, buf, sems)
        st[...] = jnp.zeros_like(st)

    for j in range(C // 256):
        lanes = slice(j * 256, (j + 1) * 256)
        a = lax.dot_general(
            u2[...], buf[lanes, :], (((1,), (1,)), ((), ())), preferred_element_type=f32
        )
        acc[:, lanes] = a
        for f in range(FPB):
            add_stats(st, f, lanes, a[f * FROWS : (f + 1) * FROWS])
    mean, rstd = norm_stats(st, C // GROUPS)
    rs[...] = jnp.zeros_like(rs)
    rs[0:FPB] = rstd
    if last:
        out[...] = jnp.zeros_like(out)
    live = live_rows()
    for f, rows, lanes in units(C):
        v = jnp.where(live, (acc[rows, lanes] - mean[f : f + 1, lanes]) * rstd[f : f + 1, lanes], 0.0)
        xh[rows, lanes] = v.astype(bf16)
        v = x[rows, lanes].astype(f32) + (v * gb[0:1, lanes] + gb[1:2, lanes])
        v = jnp.where(live, v * sigmoid(v), 0.0)
        if last:
            out[f : f + 1, lanes] = jnp.sum(v, axis=0, keepdims=True) * (1.0 / PIX)
        else:
            out[rows, lanes] = v.astype(bf16)


def back_sums(st, f, lanes, dv, xhat, gain, gacc):
    by_gain = jnp.sum(dv * xhat, axis=0, keepdims=True)
    by_bias = jnp.sum(dv, axis=0, keepdims=True)
    st[f : f + 1, lanes] = by_bias * gain
    st[FPB + f : FPB + f + 1, lanes] = by_gain * gain
    gacc[0:1, lanes] += by_gain
    gacc[1:2, lanes] += by_bias


def back_norm(st, size):
    sums = group_sum(st[...], size) * (1.0 / (PIX * size))
    return sums[0:FPB], sums[FPB : 2 * FPB]


def act_back(acc, st, xh, rs, gb, gacc, out):
    live = live_rows()
    for f, rows, lanes in units(MID):
        xhat = xh[rows, lanes].astype(f32)
        v = xhat * gb[0:1, lanes] + gb[1:2, lanes]
        s = sigmoid(v)
        dv = jnp.where(live, acc[rows, lanes] * (s + v * s * (1.0 - s)), 0.0)
        acc[rows, lanes] = dv
        back_sums(st, f, lanes, dv, xhat, gb[0:1, lanes], gacc)
    m1, m2 = back_norm(st, MID // GROUPS)
    for f, rows, lanes in units(MID):
        xhat = xh[rows, lanes].astype(f32)
        da = rs[f : f + 1, lanes] * (
            acc[rows, lanes] * gb[0:1, lanes] - m1[f : f + 1, lanes] - xhat * m2[f : f + 1, lanes]
        )
        out[rows, lanes] = jnp.where(live, da, 0.0).astype(bf16)


def tail_back_kernel(shard, last, pos, d, x, xh3, rs3, gb3, xh2, rs2, gb2, *rest):
    n = len(shard.arrays)
    refs, (r, da3, da2, gacc3, gacc2, buf, sems, acc, st, acc2, st2) = rest[:n], rest[n:]

    @first_step
    def _():
        load_rows(shard, refs, pos, buf, sems)
        st[...] = jnp.zeros_like(st)
        st2[...] = jnp.zeros_like(st2)
        gacc3[...] = jnp.zeros_like(gacc3)
        gacc2[...] = jnp.zeros_like(gacc2)

    live = live_rows()
    for f, rows, lanes in units(C):
        xhat = xh3[rows, lanes].astype(f32)
        v = x[rows, lanes].astype(f32) + (xhat * gb3[0:1, lanes] + gb3[1:2, lanes])
        s = sigmoid(v)
        grad = d[f : f + 1, lanes] if last else d[rows, lanes].astype(f32)
        dv = jnp.where(live, grad * (s + v * s * (1.0 - s)), 0.0)
        acc[rows, lanes] = dv
        r[rows, lanes] = dv.astype(bf16)
        back_sums(st, f, lanes, dv, xhat, gb3[0:1, lanes], gacc3)
    m1, m2 = back_norm(st, C // GROUPS)
    for f, rows, lanes in units(C):
        xhat = xh3[rows, lanes].astype(f32)
        da = rs3[f : f + 1, lanes] * (
            acc[rows, lanes] * gb3[0:1, lanes] - m1[f : f + 1, lanes] - xhat * m2[f : f + 1, lanes]
        )
        da3[rows, lanes] = jnp.where(live, da, 0.0).astype(bf16)
    for j in range(MID // 256):
        lanes = slice(j * 256, (j + 1) * 256)
        acc2[:, lanes] = jnp.dot(da3[...], buf[:, lanes], preferred_element_type=f32)
    act_back(acc2, st2, xh2, rs2, gb2, gacc2, da2)


def conv_back_kernel(shard, shard_one, pos, da2, masks, xh1, rs1, gb1, *rest):
    n = len(shard.arrays)
    refs, rest = rest[:n], rest[n:]
    if shard_one is not None:
        n = len(shard_one.arrays)
        refs_one, (r, da1, gacc1, d, buf, sems, taps, acc, st, buf_one, sems_one) = rest[:n], rest[n:]
    else:
        da1, gacc1, buf, sems, taps, acc, st = rest

    @first_step
    def _():
        load_rows(shard, refs, pos, buf, sems)
        if shard_one is not None:
            load_rows(shard_one, refs_one, pos, buf_one, sems_one)
        st[...] = jnp.zeros_like(st)
        gacc1[...] = jnp.zeros_like(gacc1)

    spread_taps(da2, masks, taps)
    for j in range(MID // 256):
        total = None
        for k in range(9):
            part = lax.dot_general(
                taps[:, (8 - k) * MID : (9 - k) * MID],
                buf[k * MID + j * 256 : k * MID + (j + 1) * 256, :],
                (((1,), (1,)), ((), ())),
                preferred_element_type=f32,
            )
            total = part if total is None else total + part
        acc[:, j * 256 : (j + 1) * 256] = total
    act_back(acc, st, xh1, rs1, gb1, gacc1, da1)
    if shard_one is not None:
        for j in range(C // 256):
            lanes = slice(j * 256, (j + 1) * 256)
            a = lax.dot_general(
                da1[...], buf_one[lanes, :], (((1,), (1,)), ((), ())), preferred_element_type=f32
            )
            d[:, lanes] = (r[:, lanes].astype(f32) + a).astype(bf16)


def rows_spec(width):
    return pl.BlockSpec((BROWS, width), lambda i: (i, 0))


def eight_spec(width):
    return pl.BlockSpec((8, width), lambda i: (i, 0))


def whole_spec(rows, width):
    return pl.BlockSpec((rows, width), lambda i: (0, 0))


ANY = pl.BlockSpec(memory_space=pl.ANY)
SMEM = pl.BlockSpec(memory_space=pltpu.SMEM)


def sds(rows, width, dtype):
    return jax.ShapeDtypeStruct((rows, width), dtype)


def call(kernel, name, rows, in_specs, outs, scratch, flops, bytes_accessed, limit=48):
    return pl.pallas_call(
        kernel,
        name=name,
        grid=(rows // BROWS,),
        in_specs=in_specs,
        out_specs=[spec for _, spec in outs],
        out_shape=[shape for shape, _ in outs],
        scratch_shapes=scratch,
        cost_estimate=pl.CostEstimate(
            flops=int(flops), bytes_accessed=int(bytes_accessed), transcendentals=0
        ),
        compiler_params=pltpu.CompilerParams(
            vmem_limit_bytes=limit * MIB, dimension_semantics=("arbitrary",)
        ),
    )


def sem16():
    return pltpu.SemaphoreType.DMA((16,))


def run_reduce(pos, x, shard, gb):
    rows = x.shape[0]
    eights = rows // BROWS * 8
    return call(
        functools.partial(reduce_kernel, shard),
        "reduce_norm",
        rows,
        [SMEM, rows_spec(C), whole_spec(2, MID)] + [ANY] * len(shard.arrays),
        [
            (sds(rows, MID, bf16), rows_spec(MID)),
            (sds(rows, MID, bf16), rows_spec(MID)),
            (sds(eights, MID, f32), eight_spec(MID)),
        ],
        [
            pltpu.VMEM((C, MID), bf16),
            sem16(),
            pltpu.VMEM((BROWS, MID), f32),
            pltpu.VMEM((8, MID), f32),
        ],
        2 * rows * C * MID,
        rows * (C + 2 * MID) * 2 + C * MID * 2,
    )(pos, x, gb, *shard.arrays)


def run_conv(pos, h, masks, shard, gb):
    rows = h.shape[0]
    eights = rows // BROWS * 8
    return call(
        functools.partial(conv_kernel, shard),
        "conv_norm",
        rows,
        [SMEM, rows_spec(MID), whole_spec(9 * FROWS, 128), whole_spec(2, MID)]
        + [ANY] * len(shard.arrays),
        [
            (sds(rows, 9 * MID, bf16), rows_spec(9 * MID)),
            (sds(rows, MID, bf16), rows_spec(MID)),
            (sds(rows, MID, bf16), rows_spec(MID)),
            (sds(eights, MID, f32), eight_spec(MID)),
        ],
        [
            pltpu.VMEM((9 * MID, MID), bf16),
            sem16(),
            pltpu.VMEM((BROWS, MID), f32),
            pltpu.VMEM((8, MID), f32),
        ],
        2 * rows * 9 * MID * MID,
        rows * 12 * MID * 2 + 9 * MID * MID * 2,
    )(pos, h, masks, gb, *shard.arrays)


def run_expand(pos, u2, x, shard, gb, last):
    rows = x.shape[0]
    eights = rows // BROWS * 8
    return call(
        functools.partial(expand_kernel, shard, last),
        "expand_norm",
        rows,
        [SMEM, rows_spec(MID), rows_spec(C), whole_spec(2, C)] + [ANY] * len(shard.arrays),
        [
            (sds(rows, C, bf16), rows_spec(C)),
            (sds(eights, C, f32), eight_spec(C)),
            (sds(eights, C, f32), eight_spec(C)) if last else (sds(rows, C, bf16), rows_spec(C)),
        ],
        [
            pltpu.VMEM((C, MID), bf16),
            sem16(),
            pltpu.VMEM((BROWS, C), f32),
            pltpu.VMEM((8, C), f32),
        ],
        2 * rows * C * MID,
        rows * (3 * C + MID) * 2 + C * MID * 2,
    )(pos, u2, x, gb, *shard.arrays)


def run_tail_back(pos, d, x, xh3, rs3, gb3, xh2, rs2, gb2, shard, last):
    rows = x.shape[0]
    return call(
        functools.partial(tail_back_kernel, shard, last),
        "tail_back",
        rows,
        [
            SMEM,
            eight_spec(C) if last else rows_spec(C),
            rows_spec(C),
            rows_spec(C),
            eight_spec(C),
            whole_spec(2, C),
            rows_spec(MID),
            eight_spec(MID),
            whole_spec(2, MID),
        ]
        + [ANY] * len(shard.arrays),
        [
            (sds(rows, C, bf16), rows_spec(C)),
            (sds(rows, C, bf16), rows_spec(C)),
            (sds(rows, MID, bf16), rows_spec(MID)),
            (sds(8, C, f32), whole_spec(8, C)),
            (sds(8, MID, f32), whole_spec(8, MID)),
        ],
        [
            pltpu.VMEM((C, MID), bf16),
            sem16(),
            pltpu.VMEM((BROWS, C), f32),
            pltpu.VMEM((8, C), f32),
            pltpu.VMEM((BROWS, MID), f32),
            pltpu.VMEM((8, MID), f32),
        ],
        2 * rows * C * MID,
        rows * (5 * C + 2 * MID) * 2 + C * MID * 2,
    )(pos, d, x, xh3, rs3, gb3, xh2, rs2, gb2, *shard.arrays)


def run_conv_back(pos, da2, masks, xh1, rs1, gb1, shard, shard_one, r):
    rows = da2.shape[0]
    more = shard_one is not None
    extra = shard_one.arrays if more else ()
    return call(
        functools.partial(conv_back_kernel, shard, shard_one),
        "conv_back",
        rows,
        [
            SMEM,
            rows_spec(MID),
            whole_spec(9 * FROWS, 128),
            rows_spec(MID),
            eight_spec(MID),
            whole_spec(2, MID),
        ]
        + [ANY] * (len(shard.arrays) + len(extra))
        + ([rows_spec(C)] if more else []),
        [
            (sds(rows, MID, bf16), rows_spec(MID)),
            (sds(8, MID, f32), whole_spec(8, MID)),
        ]
        + ([(sds(rows, C, bf16), rows_spec(C))] if more else []),
        [
            pltpu.VMEM((9 * MID, MID), bf16),
            sem16(),
            pltpu.VMEM((BROWS, 9 * MID), bf16),
            pltpu.VMEM((BROWS, MID), f32),
            pltpu.VMEM((8, MID), f32),
        ]
        + ([pltpu.VMEM((C, MID), bf16), sem16()] if more else []),
        2 * rows * 9 * MID * MID + (2 * rows * C * MID if more else 0),
        rows * 4 * MID * 2 + 9 * MID * MID * 2 + (rows * C * 4 if more else 0),
    )(pos, da2, masks, xh1, rs1, gb1, *shard.arrays, *extra, *([r] if more else []))


def head_in_kernel(select, feats, head, rows_out, logits):
    rows = jnp.dot(select[...], feats[...], preferred_element_type=f32).astype(bf16)
    rows_out[...] = rows
    logits[...] = jnp.dot(rows, head[...], preferred_element_type=f32)


def head_loss_kernel(logits, meta, head, select, grad_out, back, loss, probs):
    count = logits.shape[0]
    lane = lax.broadcasted_iota(jnp.int32, (count, 128), 1)
    spot = lane & (SEG - 1)
    level = value_max * (spot.astype(f32) * (2.0 / (ATOMS - 1)) - 1.0)
    values = jnp.zeros((count, 128), f32)
    columns = []
    for a in range(ACTIONS):
        chunk = slice(a // 2 * 128, a // 2 * 128 + 128)
        inside = (lane >= (a % 2) * SEG) & (lane < (a % 2) * SEG + ATOMS)
        v = logits[:, chunk]
        top = jnp.max(jnp.where(inside, v, -3.0e38), axis=1, keepdims=True)
        e = jnp.where(inside, jnp.exp(jnp.minimum(v - top, 0.0)), 0.0)
        p = e / jnp.sum(e, axis=1, keepdims=True)
        q = jnp.sum(p * level, axis=1, keepdims=True)
        columns.append(q)
        values = jnp.where(lane == a, q, values)
        if a % 2 == 0:
            probs[:, chunk] = p
        else:
            probs[:, chunk] += p
    target, weight, action = meta[:, 0:1], meta[:, 1:2], meta[:, 3:4]
    real = lane < ACTIONS
    hot = (lane.astype(f32) == action).astype(f32)
    chosen = jnp.sum(values * hot, axis=1, keepdims=True)
    top = jnp.max(jnp.where(real, values, -3.0e38), axis=1, keepdims=True)
    e = jnp.where(real, jnp.exp(jnp.minimum(values - top, 0.0)), 0.0)
    total = jnp.sum(e, axis=1, keepdims=True)
    soft_top = top + jnp.log(total)
    row_loss = weight * ((chosen - target) * (chosen - target) + cql_alpha * (soft_top - chosen))
    loss[...] = jnp.zeros(loss.shape, f32) + jnp.sum(row_loss, axis=0, keepdims=True)
    slope = weight * (2.0 * (chosen - target) * hot + cql_alpha * (e / total - hot))
    for j in range(ACTIONS // 2):
        chunk = slice(j * 128, j * 128 + 128)
        low = lane < SEG
        q = jnp.where(low, columns[2 * j], columns[2 * j + 1])
        s = jnp.where(low, slope[:, 2 * j : 2 * j + 1], slope[:, 2 * j + 1 : 2 * j + 2])
        grad_out[:, chunk] = (s * probs[:, chunk] * (level - q)).astype(bf16)
    feat = lax.dot_general(
        grad_out[...], head[...], (((1,), (1,)), ((), ())), preferred_element_type=f32
    ).astype(bf16)
    back[...] = lax.dot_general(
        select[...], feat, (((0,), (0,)), ((), ())), preferred_element_type=f32
    ).astype(bf16)


def plain_call(kernel, name, outs, scratch, limit=48):
    return pl.pallas_call(
        kernel,
        name=name,
        out_shape=outs,
        scratch_shapes=scratch,
        compiler_params=pltpu.CompilerParams(vmem_limit_bytes=limit * MIB),
    )


def adam_step(weight, first, second, grad_in, rate, decay):
    first_new = decay_moment * first + (1.0 - decay_moment) * grad_in
    second_new = beta_second * second + (1.0 - beta_second) * grad_in * grad_in
    normed = (
        first_new
        / (1.0 - decay_moment**STEP)
        / (jnp.sqrt(second_new / (1.0 - beta_second**STEP)) + adam_eps)
    )
    return (weight - rate * (normed + decay * weight), first_new, second_new)


def mat(a, b):
    return jnp.einsum(
        "bij,bjk->bik", a.astype(bf16), b.astype(bf16), preferred_element_type=f32
    )


def gram(a, b):
    return jnp.einsum("ri,rj->ij", a, b, preferred_element_type=f32)


def weight_grad(a, b):
    return jnp.einsum("ri,rj->ij", a, b, preferred_element_type=f32).astype(bf16)


def local(
    net,
    frames,
    game_ids,
    actions,
    groups,
    targets,
    w_pair,
    w_spatial,
    mom_pair,
    mom_spatial,
    head_table,
    head_first,
    head_second,
    norm_params,
    norm_first,
    norm_second,
):
    dp_idx, ns_idx = lax.axis_index("dp"), lax.axis_index("ns")
    pos = jnp.stack([ns_idx, bit_of(dp_idx, 0)]).astype(jnp.int32)
    dev_rows = frames.shape[1]
    samples = MB * dev_rows
    rows = samples * FROWS
    devices = net.dp * net.ns
    everyone = devices * samples
    slots = MB * net.dp * (2 * net.ns * dev_rows // net.dp)
    col_width = C // net.ns

    (w_one0,) = gather_rows(net, [w_pair[0, 0]])
    (w_mid0,) = gather_rows(net, [w_spatial[0]])
    w_last0, w_one1 = gather_rows(net, [w_pair[0, 1], w_pair[1, 0]])
    (w_mid1,) = gather_rows(net, [w_spatial[1]])
    (w_last1,) = gather_rows(net, [w_pair[1, 1]])
    ones, mids, lasts = [w_one0, w_one1], [w_mid0, w_mid1], [w_last0, w_last1]

    meta = jnp.stack(
        [
            targets.astype(f32),
            0.25 + 0.75 * groups.astype(f32),
            game_ids[:, :, 0].astype(f32),
            actions.astype(f32),
        ]
    ).reshape(4, samples)
    meta = jnp.concatenate([meta, jnp.zeros((12, samples), f32)], axis=0).astype(bf16)
    mine = dp_idx * net.ns + ns_idx
    spread = (
        jnp.arange(everyone, dtype=jnp.int32)[None, :]
        == (mine * samples + jnp.arange(samples, dtype=jnp.int32))[:, None]
    ).astype(bf16)
    meta = jnp.dot(meta, spread, preferred_element_type=f32).astype(bf16)
    meta = net.add_all(meta).astype(f32)
    weight_total = jnp.sum(meta[1])
    match = (meta[2].astype(jnp.int32) == dp_idx).astype(jnp.int32)
    place = jnp.cumsum(match) - 1
    select = (
        (jnp.arange(slots, dtype=jnp.int32)[:, None] == place[None, :]) & (match[None, :] == 1)
    ).astype(bf16)
    meta_slots = jnp.einsum("se,me->sm", select, meta.astype(bf16), preferred_element_type=f32)

    out_col = jnp.arange(HOUT, dtype=jnp.int32)
    widen = (
        (out_col // ATOMS * SEG + out_col % ATOMS)[:, None] == jnp.arange(HPAD, dtype=jnp.int32)
    ).astype(bf16)
    head = jnp.dot(head_table[0].astype(bf16), widen, preferred_element_type=f32).astype(bf16)

    moms = [mom_pair[0, 0], mom_pair[0, 1], mom_pair[1, 0], mom_pair[1, 1], mom_spatial[0], mom_spatial[1]]
    moms_low = [m.astype(bf16) for m in moms]
    old = jnp.stack([gram(m, m) for m in moms_low])
    old_sum = reduce_grams(net, pack_grams(old[:3], old[3:]))
    old_upper, old_lower = unpack_grams(old_sum)
    gram_mm = jnp.concatenate([old_upper, old_lower], axis=0)

    masks = jnp.asarray(tap_masks())
    stream = jnp.pad(
        frames.reshape(samples, PIX, C), ((0, 0), (0, FROWS - PIX), (0, 0))
    ).reshape(rows, C)
    gbs = [
        (p[:, :MID], p[:, MID : 2 * MID], p[:, 2 * MID :])
        for p in (norm_params[layer] for layer in range(BLOCKS))
    ]
    kept = []
    for layer in range(BLOCKS):
        gb1, gb2, gb3 = gbs[layer]
        h, xh1, rs1 = run_reduce(pos, stream, ones[layer], gb1)
        taps, u2, xh2, rs2 = run_conv(pos, h, masks, mids[layer], gb2)
        last = layer == BLOCKS - 1
        xh3, rs3, out = run_expand(pos, u2, stream, lasts[layer], gb3, last)
        kept.append((stream, xh1, rs1, taps, u2, xh2, rs2, xh3, rs3))
        stream = out
    pooled = stream.reshape(-1, 8, C)[:, :FPB].reshape(samples, C).astype(bf16)

    sent = jnp.swapaxes(pooled.reshape(samples, net.ns, col_width), 0, 1)
    sent = jnp.broadcast_to(sent[None], (net.dp, net.ns, samples, col_width))
    feats = lax.all_to_all(
        sent.reshape(devices, samples, col_width), ("dp", "ns"), 0, 0, tiled=True
    ).reshape(everyone, col_width)
    feat_rows, logits = plain_call(
        head_in_kernel,
        "head_in",
        [sds(slots, col_width, bf16), sds(slots, HPAD, f32)],
        [],
    )(select, feats, head)
    logits = net.add_all(logits, ("ns",))
    grad_low, back, loss = plain_call(
        head_loss_kernel,
        "head_loss",
        [sds(slots, HPAD, bf16), sds(everyone, col_width, bf16), sds(8, 128, f32)],
        [pltpu.VMEM((slots, HPAD), f32)],
    )(logits, meta_slots, head, select)
    returned = lax.all_to_all(
        back.reshape(devices, samples, col_width), ("dp", "ns"), 0, 0, tiled=True
    ).reshape(net.dp, net.ns, samples, col_width)
    grad_pooled = jnp.sum(returned.astype(f32), axis=0)
    grad_pooled = jnp.swapaxes(grad_pooled, 0, 1).reshape(samples // FPB, FPB, C) * (1.0 / PIX)
    grad_stream = jnp.pad(grad_pooled, ((0, 0), (0, 8 - FPB), (0, 0))).reshape(-1, C)

    grad_low = lax.dot_general(
        grad_low, widen, (((1,), (1,)), ((), ())), preferred_element_type=f32
    ).astype(bf16)
    head_grad = gram(feat_rows, grad_low)
    head_sq = jnp.sum(jnp.square(head_grad))
    loss_part = jnp.where(ns_idx == 0, loss[0, 0], 0.0)

    gain_rows = [None] * BLOCKS
    grads = [None] * BLOCKS
    for layer in reversed(range(BLOCKS)):
        x, xh1, rs1, taps, u2, xh2, rs2, xh3, rs3 = kept[layer]
        gb1, gb2, gb3 = gbs[layer]
        r, da3, da2, gacc3, gacc2 = run_tail_back(
            pos, grad_stream, x, xh3, rs3, gb3, xh2, rs2, gb2, lasts[layer], layer == BLOCKS - 1
        )
        grad_last = weight_grad(da3, u2)
        grad_mid = weight_grad(taps, da2)
        got = run_conv_back(
            pos, da2, masks, xh1, rs1, gb1, mids[layer], ones[layer] if layer > 0 else None, r
        )
        da1, gacc1 = got[:2]
        grad_one = weight_grad(x, da1)
        if layer > 0:
            grad_stream = got[2]
        grads[layer] = (grad_one, grad_last, grad_mid)
        gain_rows[layer] = jnp.concatenate([gacc1[:2], gacc2[:2], gacc3[:2]], axis=1)

    shares = [None] * 6
    shares[2], shares[3], shares[5] = reduce_rows(net, list(grads[1]))
    shares[1], shares[4] = reduce_rows(net, [grads[0][1], grads[0][2]])
    (shares[0],) = reduce_rows(net, [grads[0][0]])

    def cross_grams(ids):
        packs = []
        for i in ids:
            s = gram(moms_low[i], shares[i])
            packs.append(pack_grams(s + s.T, gram(shares[i], shares[i])))
        return unpack_grams(reduce_grams(net, jnp.stack(packs)))

    mg_b, gg_b = cross_grams([2, 3, 5])
    mg_m, gg_m = cross_grams([1, 4])
    mg_a, gg_a = cross_grams([0])
    gram_mg = jnp.stack([mg_a[0], mg_m[0], mg_b[0], mg_b[1], mg_m[1], mg_b[2]])
    gram_gg = jnp.stack([gg_a[0], gg_m[0], gg_b[0], gg_b[1], gg_m[1], gg_b[2]])

    small = jnp.stack(gain_rows).reshape(-1, 1024)
    tail = jnp.zeros((16 - small.shape[0], 1024), f32)
    lane = jnp.arange(1024, dtype=jnp.int32)[None, :]
    tail = tail + jnp.where(lane == 0, loss_part, 0.0) + jnp.where(lane == 1, head_sq, 0.0)
    small = net.add_all(jnp.concatenate([small, tail], axis=0))
    gain_sum = small[:12].reshape(BLOCKS, 2, 2 * MID + C)
    loss_sum, head_total = small[12, 0], small[12, 1]

    eye = jnp.eye(MID, dtype=f32)
    diag_gg = jnp.sum(gram_gg * eye)
    grad_norm = jnp.sqrt(diag_gg + head_total + jnp.sum(jnp.square(gain_sum))) / weight_total
    factor = jnp.minimum(1.0, clip_limit / grad_norm) / weight_total

    gram_all = (
        decay_moment * decay_moment * gram_mm
        + (decay_moment * factor) * gram_mg
        + (factor * factor) * gram_gg
    )
    frob = jnp.sqrt(jnp.maximum(jnp.sum(gram_all * eye, axis=(1, 2)), 0.0))
    scale = 1.0 / (frob + 1e-07)
    g0 = gram_all * (scale * scale)[:, None, None]
    e1 = coef_b * g0 + coef_c * mat(g0, g0)
    k = coef_a * g0 + mat(g0, e1)
    g1 = coef_a * k + mat(k, e1)
    e2 = coef_b * g1 + coef_c * mat(g1, g1)
    poly = coef_a * (e1 + e2) + mat(e1, e2)

    news, moments = [], []
    weights = [w_pair[0, 0], w_pair[0, 1], w_pair[1, 0], w_pair[1, 1], w_spatial[0], w_spatial[1]]
    for i in range(6):
        moment = decay_moment * moms[i] + factor * shares[i].astype(f32)
        current = moment * scale[i]
        ortho = (coef_a * coef_a) * current + jnp.dot(
            current.astype(bf16), poly[i].astype(bf16), preferred_element_type=f32
        )
        gain = 0.2 * math.sqrt(C if i < 4 else 9 * MID)
        news.append(weights[i] - rate_muon * (decay_muon * weights[i] + gain * ortho))
        moments.append(moment)

    head_new, head_first_new, head_second_new = adam_step(
        head_table, head_first, head_second, factor * head_grad[None], rate_head, decay_head
    )
    norm_new, norm_first_new, norm_second_new = adam_step(
        norm_params, norm_first, norm_second, factor * gain_sum, rate_gain, 0.0
    )

    def pair(v):
        return jnp.stack([jnp.stack(v[0:2]), jnp.stack(v[2:4])])

    return (
        pair(news),
        jnp.stack(news[4:]),
        pair(moments),
        jnp.stack(moments[4:]),
        head_new,
        head_first_new,
        head_second_new,
        norm_new,
        norm_first_new,
        norm_second_new,
        grad_norm,
        loss_sum,
        weight_total,
    )


def solution(mesh):
    net = Net(mesh.shape["dp"], mesh.shape["ns"])
    samples = P(None, ("dp", "ns"))
    heads = P("dp", "ns", None)
    pairs, spatial = P(None, None, "ns", None), P(None, "ns", None)
    in_specs = (
        P(None, ("dp", "ns"), None, None),
        P(None, ("dp", "ns"), None),
        samples,
        samples,
        samples,
        pairs,
        spatial,
        pairs,
        spatial,
        heads,
        heads,
        heads,
        P(),
        P(),
        P(),
    )
    out_specs = (pairs, spatial, pairs, spatial, heads, heads, heads) + (P(),) * 6
    return jax.shard_map(
        functools.partial(local, net),
        mesh=mesh,
        in_specs=in_specs,
        out_specs=out_specs,
        check_vma=False,
    )
```

time: 2000 us -> 893 us (0.45)
  waiting for transfers between devices: 788 us -> 215 us
  local copies, waits for them, and re-layouts: 527 us -> 155 us
  matrix products: 304 us -> 133 us
  Pallas kernels: 0 us -> 142 us
  other arithmetic: 249 us -> 137 us
  starting transfers between devices: 47.6 us -> 90.6 us
  blocking collectives: 41.3 us -> 0 us
    psum x4 -> x0, waiting for transfers between devices: 444 us -> none  [the longest x2 252 us: local(): lax.psum((jnp.einsum('...ri,...rj->...ij', pair_cur, pair_cur, precision=...]
    reduce_scatter x2 -> x0, waiting for transfers between devices: 277 us -> none  [the longest x1 174 us: local(): lax.psum_scatter(spatial_grad, 'ns', scatter_dimension=1, tiled=True)]
    ppermute x0 -> x84, waiting for transfers between devices: none -> 207 us  [swap(): return lax.ppermute(value, ('dp', 'ns'), pairs)]
    dot_general x58 -> x39, matrix products: 304 us -> 133 us  [the longest x19 42.9 us: gram(): return jnp.einsum('ri,rj->ij', a, b, preferred_element_type=f32)]
    reshape x50 -> x2, local copies, waits for them, and re-layouts: 171 us -> 2.32 us  [the longest x1 1.47 us: local(): small = jnp.stack(gain_rows).reshape(-1, 1024)]
    pallas_call x0 -> x12, Pallas kernels: none -> 142 us  [the longest x2 38.7 us: run_tail_back(): call(functools.partial(tail_back_kernel, shard, last), 'tail_back', rows,...]
    reduce_sum x60 -> x12, other arithmetic: 106 us -> 24.6 us  [the longest x1 8.6 us: local(): frob = jnp.sqrt(jnp.maximum(jnp.sum(gram_all * eye, axis=(1, 2)), 0.0))]
    ppermute x0 -> x84, starting transfers between devices: none -> 81.2 us  [swap(): return lax.ppermute(value, ('dp', 'ns'), pairs)]
  transfers between devices with their start and end apart: 20 -> 86, of which waited for: 18 -> 37; matrix products, arithmetic and copies ran while one was open for 14% -> 28% of each run, Pallas kernels for 0% -> 16%
where the time goes in v1:
time: 893 us; the launch traced here: 882 us
  waiting for transfers between devices  215 us (24%)
  local copies, waits for them, and re-layouts  155 us (17%)
  Pallas kernels  142 us (16%)
  other arithmetic  137 us (15%)
  matrix products  133 us (15%)
  starting transfers between devices  90.6 us (10%)
  between operations  9.72 us (1%)
    ppermute x84, waiting for transfers between devices, swap(): return lax.ppermute(value, ('dp', 'ns'), pairs)  207 us
    ppermute x84, starting transfers between devices, swap(): return lax.ppermute(value, ('dp', 'ns'), pairs)  81.2 us
    unnamed x391, local copies, waits for them, and re-layouts  80.3 us
    dot_general x19, matrix products, gram(): return jnp.einsum('ri,rj->ij', a, b, preferred_element_type=f32)  42.9 us
    pallas_call x2, Pallas kernels, run_tail_back(): call(functools.partial(tail_back_kernel, shard, last), 'tail_back', rows,...  38.7 us
    dot_general x5, matrix products, mat(): jnp.einsum('bij,bjk->bik', a.astype(bf16), b.astype(bf16), preferred_elem...  38 us
    pallas_call x2, Pallas kernels, run_conv_back(): call(functools.partial(conv_back_kernel, shard, shard_one), 'conv_back',...  30.1 us
    pallas_call x2, Pallas kernels, run_expand(): call(functools.partial(expand_kernel, shard, last), 'expand_norm', rows,...  29 us
  transfers between devices with their start and end apart: 86, of which 37 were waited for; matrix products, arithmetic and copies ran while one was open for 28% of the time, Pallas kernels for 16%

profile of v1, /device:TPU:0, one launch (start us, length us, event | category | flops | bytes accessed | tf_op | source)
XLA Modules:
  0.0 881.7 jit_solution(14460924356880226284)
XLA Ops:
  6.9 3.7 fusion.222
  43.4 4.2 copy.160
  47.6 5.0 pad.10
  68.8 13.4 %collective-permute-done.11 = bf16[2,288,512]{2,1,0:T(8,128)(2,1)S(1)} collective-permute-done((bf16[2,288,512]{2,1,0:T(8,128)(2,1)S(1)}, bf16[2,288,512]{2,1,0:T(8,128)(2,1)S(1)}, u32[]{:S(2)}, u32[]{:S(2)}) %collective-permute-start.11) | collective-permute-done | bytes 589856 | tf_op jit(solution)/shard_map/ppermute | solution.py:75
  87.1 6.3 collective-permute-done.16
  95.1 17.2 %collective-permute-done.12 = bf16[1,288,512]{2,1,0:T(8,128)(2,1)S(1)} collective-permute-done((bf16[1,288,512]{2,1,0:T(8,128)(2,1)S(1)}, bf16[1,288,512]{2,1,0:T(8,128)(2,1)S(1)}, u32[]{:S(2)}, u32[]{:S(2)}) %collective-permute-start.12) | collective-permute-done | bytes 294944 | tf_op jit(solution)/shard_map/ppermute | solution.py:75
  121.6 6.4 collective-permute-done.13
  135.1 12.5 %collective-permute-done.23 = bf16[2,288,512]{2,1,0:T(8,128)(2,1)S(1)} collective-permute-done((bf16[2,288,512]{2,1,0:T(8,128)(2,1)S(1)}, bf16[2,288,512]{2,1,0:T(8,128)(2,1)S(1)}, u32[]{:S(2)}, u32[]{:S(2)}) %collective-permute-start.23) | collective-permute-done | bytes 589856 | tf_op jit(solution)/shard_map/ppermute | solution.py:75
  157.7 4.7 collective-permute-done.27
  166.6 4.7 collective-permute-done.28
  174.6 8.1 reduce_norm.2
  184.3 12.0 %conv_norm.2 = (bf16[1024,4608]{1,0:T(8,128)(2,1)}, bf16[1024,512]{1,0:T(8,128)(2,1)S(1)}, bf16[1024,512]{1,0:T(8,128)(2,1)S(1)}, f32[32,512]{1,0:T(8,128)S(1)}) custom-call(s32[2]{0:T(128)S(1)} %pad_add_fusion.pos, bf16[1024,512]{1,0:T(8,128)(2,1)S(1)} %get-tuple-element.52.src, f32[1152,128]{1,0:T(8,128)S(1)} %copy-done.37, ...), custom_call_target="tpu_custom_call" | custom-call | flops 4831838208 | bytes 17301504 | tf_op jit(solution)/shard_map/conv_norm/pallas_call | solution.py:540
  197.3 15.2 %expand_norm.2 = (bf16[1024,2048]{1,0:T(8,128)(2,1)}, f32[32,2048]{1,0:T(8,128)S(1)}, bf16[1024,2048]{1,0:T(8,128)(2,1)}) custom-call(s32[2]{0:T(128)S(1)} %pad_add_fusion.pos, bf16[1024,512]{1,0:T(8,128)(2,1)S(1)} %get-tuple-element.53.u2, bf16[1024,2048]{1,0:T(8,128)(2,1)} %bitcast.709, f32[2,2048]{1,0:T(2,128)S(1)} %slice.426.gb.gb3, ...), custom_call_target="tpu_custom_call" | custom-call | flops 2147483648 | bytes 15728640 | tf_op jit(solution)/shard_map/expand_norm/pallas_call | solution.py:566
  212.6 9.2 %reduce_norm.3 = (bf16[1024,512]{1,0:T(8,128)(2,1)S(1)}, bf16[1024,512]{1,0:T(8,128)(2,1)S(1)}, f32[32,512]{1,0:T(8,128)S(1)}) custom-call(s32[2]{0:T(128)S(1)} %pad_add_fusion.pos, bf16[1024,2048]{1,0:T(8,128)(2,1)} %get-tuple-element.54.x, f32[2,512]{1,0:T(2,128)S(1)} %get-tuple-element.258.gb.gb1, ...), custom_call_target="tpu_custom_call" | custom-call | flops 2147483648 | bytes 8388608 | tf_op jit(solution)/shard_map/reduce_norm/pallas_call | solution.py:516
  223.4 12.0 %conv_norm.3 = (bf16[1024,4608]{1,0:T(8,128)(2,1)}, bf16[1024,512]{1,0:T(8,128)(2,1)S(1)}, bf16[1024,512]{1,0:T(8,128)(2,1)S(1)}, f32[32,512]{1,0:T(8,128)S(1)}) custom-call(s32[2]{0:T(128)S(1)} %pad_add_fusion.pos, bf16[1024,512]{1,0:T(8,128)(2,1)S(1)} %get-tuple-element.55.src, f32[1152,128]{1,0:T(8,128)S(1)} %copy-done.37, ...), custom_call_target="tpu_custom_call" | custom-call | flops 4831838208 | bytes 17301504 | tf_op jit(solution)/shard_map/conv_norm/pallas_call | solution.py:540
  235.5 13.8 %expand_norm.3 = (bf16[1024,2048]{1,0:T(8,128)(2,1)}, f32[32,2048]{1,0:T(8,128)S(1)}, f32[32,2048]{1,0:T(8,128)S(1)}) custom-call(s32[2]{0:T(128)S(1)} %pad_add_fusion.pos, bf16[1024,512]{1,0:T(8,128)(2,1)S(1)} %get-tuple-element.56.u2, bf16[1024,2048]{1,0:T(8,128)(2,1)} %get-tuple-element.54.x, f32[2,2048]{1,0:T(2,128)S(1)} %slice.431.gb.gb3, ...), custom_call_target="tpu_custom_call" | custom-call | flops 2147483648 | bytes 15728640 | tf_op jit(solution)/shard_map/expand_norm/pallas_call | solution.py:566
  250.8 4.1 all-to-all-start
  260.5 5.5 all-to-all-done
  270.6 7.4 collective-permute-done.30
  283.6 3.9 collective-permute-done.31
  290.4 5.4 all-to-all-start.1
  299.7 4.4 multiply_reduce_fusion.2
  312.1 18.3 %tail_back.2 = (bf16[1024,2048]{1,0:T(8,128)(2,1)}, bf16[1024,2048]{1,0:T(8,128)(2,1)}, bf16[1024,512]{1,0:T(8,128)(2,1)S(1)}, f32[8,2048]{1,0:T(8,128)S(1)}, f32[8,512]{1,0:T(8,128)S(1)}) custom-call(s32[2]{0:T(128)S(1)} %copy-done.28, f32[32,2048]{1,0:T(8,128)S(1)} %pad_bitcast_fusion.d, bf16[1024,2048]{1,0:T(8,128)(2,1)} %get-tuple-element.54.x, ...), custom_call_target="tpu_custom_call" | custom-call | flops 2147483648 | bytes 25165824 | tf_op jit(solution)/shard_map/tail_back/pallas_call | solution.py:589
  330.4 9.1 %convolution_convert_fusion = bf16[4608,512]{1,0:T(8,128)(2,1)S(1)} fusion(bf16[1024,4608]{1,0:T(8,128)(2,1)} %get-tuple-element.81, bf16[1024,512]{1,0:T(8,128)(2,1)S(1)} %get-tuple-element.64.da2), kind=kOutput, calls=%fused_computation | convolution fusion | flops 4834197504 | bytes 15204352 | tf_op jit(solution)/shard_map/ri,rj->ij/dot_general | solution.py:745
  346.9 18.6 %conv_back.2 = (bf16[1024,512]{1,0:T(8,128)(2,1)S(1)}, f32[8,512]{1,0:T(8,128)S(1)}, bf16[1024,2048]{1,0:T(8,128)(2,1)}) custom-call(s32[2]{0:T(128)S(1)} %copy-done.28, bf16[1024,512]{1,0:T(8,128)(2,1)S(1)} %get-tuple-element.64.da2, f32[1152,128]{1,0:T(8,128)S(1)} %copy-done.38, bf16[1024,512]{1,0:T(8,128)(2,1)S(1)} %copy-done.32, ...), custom_call_target="tpu_custom_call" | custom-call | flops 6979321856 | bytes 17301504 | tf_op jit(solution)/shard_map/conv_back/pallas_call | solution.py:629
  371.5 20.5 %tail_back.3 = (bf16[1024,2048]{1,0:T(8,128)(2,1)}, bf16[1024,2048]{1,0:T(8,128)(2,1)}, bf16[1024,512]{1,0:T(8,128)(2,1)S(1)}, f32[8,2048]{1,0:T(8,128)S(1)}, f32[8,512]{1,0:T(8,128)S(1)}) custom-call(s32[2]{0:T(128)S(1)} %copy-done.28, bf16[1024,2048]{1,0:T(8,128)(2,1)} %get-tuple-element.68.d, bf16[1024,2048]{1,0:T(8,128)(2,1)} %bitcast.710, ...), custom_call_target="tpu_custom_call" | custom-call | flops 2147483648 | bytes 25165824 | tf_op jit(solution)/shard_map/tail_back/pallas_call | solution.py:589
  392.0 11.5 %conv_back.3 = (bf16[1024,512]{1,0:T(8,128)(2,1)S(1)}, f32[8,512]{1,0:T(8,128)S(1)}) custom-call(s32[2]{0:T(128)S(1)} %copy-done.28, bf16[1024,512]{1,0:T(8,128)(2,1)S(1)} %get-tuple-element.73.da2, f32[1152,128]{1,0:T(8,128)S(1)} %copy-done.38, bf16[1024,512]{1,0:T(8,128)(2,1)S(1)} %copy-done.42, f32[32,512]{1,0:T(8,128)S(1)} %copy-done.44, ...), custom_call_target="tpu_custom_call" | custom-call | flops 4831838208 | bytes 8912896 | tf_op jit(solution)/shard_map/conv_back/pallas_call | solution.py:629
  406.6 9.0 %convolution_convert_fusion.1 = bf16[4608,512]{1,0:T(8,128)(2,1)S(1)} fusion(bf16[1024,4608]{1,0:T(8,128)(2,1)} %get-tuple-element.78, bf16[1024,512]{1,0:T(8,128)(2,1)S(1)} %get-tuple-element.73.da2), kind=kOutput, calls=%fused_computation.1 | convolution fusion | flops 4834197504 | bytes 15204352 | tf_op jit(solution)/shard_map/ri,rj->ij/dot_general | solution.py:745
  425.9 7.2 collective-permute-done.33
  489.8 17.4 %collective-permute-done.47 = bf16[2,416,512]{2,1,0:T(8,128)(2,1)S(1)} collective-permute-done((bf16[2,416,512]{2,1,0:T(8,128)(2,1)S(1)}, bf16[2,416,512]{2,1,0:T(8,128)(2,1)S(1)}, u32[]{:S(2)}, u32[]{:S(2)}) %collective-permute-start.47) | collective-permute-done | bytes 852000 | tf_op jit(solution)/shard_map/ppermute | solution.py:75
  515.0 5.9 collective-permute-done.48
  526.8 4.5 collective-permute-done.51
  532.3 18.4 %collective-permute-done.44 = bf16[1,144,512]{2,1,0:T(8,128)(2,1)S(1)} collective-permute-done((bf16[1,144,512]{2,1,0:T(8,128)(2,1)S(1)}, bf16[1,144,512]{2,1,0:T(8,128)(2,1)S(1)}, u32[]{:S(2)}, u32[]{:S(2)}) %collective-permute-start.44) | collective-permute-done | bytes 147488 | tf_op jit(solution)/shard_map/ppermute | solution.py:75
  552.4 17.0 %collective-permute-done.52 = bf16[416,512]{1,0:T(8,128)(2,1)S(1)} collective-permute-done((bf16[416,512]{1,0:T(8,128)(2,1)S(1)}, bf16[416,512]{1,0:T(8,128)(2,1)S(1)}, u32[]{:S(2)}, u32[]{:S(2)}) %collective-permute-start.52) | collective-permute-done | bytes 426016 | tf_op jit(solution)/shard_map/ppermute | solution.py:75
  571.8 9.5 %collective-permute-done.53 = bf16[416,512]{1,0:T(8,128)(2,1)S(1)} collective-permute-done((bf16[416,512]{1,0:T(8,128)(2,1)S(1)}, bf16[416,512]{1,0:T(8,128)(2,1)S(1)}, u32[]{:S(2)}, u32[]{:S(2)}) %collective-permute-start.53) | collective-permute-done | bytes 426016 | tf_op jit(solution)/shard_map/ppermute | solution.py:75
  612.7 3.9 fusion.135
  623.2 4.3 collective-permute-done.66
  629.9 13.0 %collective-permute-done.67 = bf16[544,512]{1,0:T(8,128)(2,1)S(1)} collective-permute-done((bf16[544,512]{1,0:T(8,128)(2,1)S(1)}, bf16[544,512]{1,0:T(8,128)(2,1)S(1)}, u32[]{:S(2)}, u32[]{:S(2)}) %collective-permute-start.67) | collective-permute-done | bytes 557088 | tf_op jit(solution)/shard_map/ppermute | solution.py:75
  701.4 6.8 collective-permute-done.69
  737.1 10.5 %fusion.15 = (f32[3,512,512]{2,1,0:T(8,128)}, f32[3,512,512]{2,1,0:T(8,128)}, f32[3,512,512]{2,1,0:T(8,128)}, f32[3,512,512]{2,1,0:T(8,128)}) fusion(f32[3,512,512]{1,2,0:T(8,128)} %copy.228, f32[3,512]{1,0:T(4,128)S(1)} %bitcast.796, pred[512,512]{1,0:T(8,128)(4,1)} %copy-done.105, pred[512,512]{1,0:T(8,128)(4,1)} %copy-done.103, ...), kind=kLoop, calls=%fused_computation.41 | loop fusion | flops 4718592 | bytes 25702400 | tf_op jit(solution)/shard_map/jit(_where)/select_n | solution.py:208
  754.2 5.1 multiply_reduce_fusion.1
  778.7 8.6 multiply_reduce_fusion
  795.0 4.4 fusion.22
  799.4 17.3 %multiply_add_fusion = f32[6,512,512]{2,1,0:T(8,128)} fusion(f32[6,512,512]{2,1,0:T(8,128)} %fusion.22, f32[6,512,512]{2,1,0:T(8,128)} %copy-done.46), kind=kOutput, calls=%fused_computation.6 | convolution fusion | flops 1623195648 | bytes 18874368 | tf_op jit(solution)/shard_map/bij,bjk->bik/dot_general | solution.py:735
  816.7 12.0 %add_convert_fusion = bf16[6,512,512]{2,1,0:T(8,128)(2,1)} fusion(f32[6,512,512]{2,1,0:T(8,128)} %copy-done.45, f32[6,512,512]{2,1,0:T(8,128)} %multiply_add_fusion), kind=kOutput, calls=%fused_computation.5 | convolution fusion | flops 1620049920 | bytes 15728640 | tf_op jit(solution)/shard_map/bij,bjk->bik/dot_general | solution.py:735
  829.3 4.4 multiply_add_fusion.6
  840.2 5.1 fusion.12
  856.4 4.2 fusion.42
  (828 shorter events, 426.8 us)
Async XLA Ops:
  4.0 49.2 %collective-permute-start.5 = (bf16[1,128,512]{2,1,0:T(8,128)(2,1)}, bf16[1,128,512]{2,1,0:T(8,128)(2,1)}, u32[]{:S(2)}, u32[]{:S(2)}) collective-permute-start(bf16[1,128,512]{2,1,0:T(8,128)(2,1)} %get-tuple-element.172), channel_id=1, source_target_pairs={{0,1},{1,0},{2,3},{3,2},{4,5},{5,4},{6,7},{7,6},{8,9},{9,8},{10,11... | collective-permute-start | bytes 393224 | tf_op jit(solution)/shard_map/ppermute | solution.py:75
  11.5 47.8 %collective-permute-start.10 = (bf16[1,288,512]{2,1,0:T(8,128)(2,1)}, bf16[1,288,512]{2,1,0:T(8,128)(2,1)}, u32[]{:S(2)}, u32[]{:S(2)}) collective-permute-start(bf16[1,288,512]{2,1,0:T(8,128)(2,1)} %get-tuple-element.168), channel_id=1, source_target_pairs={{0,1},{1,0},{2,3},{3,2},{4,5},{5,4},{6,7},{7,6},{8,9},{9,8},{10,11... | collective-permute-start | bytes 884744 | tf_op jit(solution)/shard_map/ppermute | solution.py:75
  13.0 49.0 %collective-permute-start.15 = (bf16[1,256,512]{2,1,0:T(8,128)(2,1)}, bf16[1,256,512]{2,1,0:T(8,128)(2,1)}, u32[]{:S(2)}, u32[]{:S(2)}) collective-permute-start(bf16[1,256,512]{2,1,0:T(8,128)(2,1)} %get-tuple-element.164), channel_id=1, source_target_pairs={{0,1},{1,0},{2,3},{3,2},{4,5},{5,4},{6,7},{7,6},{8,9},{9,8},{10,11... | collective-permute-start | bytes 786440 | tf_op jit(solution)/shard_map/ppermute | solution.py:75
  15.6 17.4 %collective-permute-start = (bf16[16,256]{1,0:T(8,128)(2,1)S(1)}, bf16[16,256]{1,0:T(8,128)(2,1)S(1)}, u32[]{:S(2)}, u32[]{:S(2)}) collective-permute-start(bf16[16,256]{1,0:T(8,128)(2,1)S(1)} %convolution_convert_fusion.6), channel_id=1, source_target_pairs={{0,4},{1,5},{2,6},{3,7},{4,0},{5,1},{6,2},{7,3},{8,12},{9,13},{10,... | collective-permute-start | bytes 24584 | tf_op jit(solution)/shard_map/ppermute | solution.py:75
  16.4 39.9 %collective-permute-start.25 = (bf16[1,128,512]{2,1,0:T(8,128)(2,1)}, bf16[1,128,512]{2,1,0:T(8,128)(2,1)S(1)}, u32[]{:S(2)}, u32[]{:S(2)}) collective-permute-start(bf16[1,128,512]{2,1,0:T(8,128)(2,1)} %get-tuple-element.152), channel_id=1, source_target_pairs={{0,1},{1,0},{2,3},{3,2},{4,5},{5,4},{6,7},{7,6},{8,9},{9,8},{10,11... | collective-permute-start | bytes 393224 | tf_op jit(solution)/shard_map/ppermute | solution.py:75
  54.1 32.2 %collective-permute-start.6 = (bf16[2,128,512]{2,1,0:T(8,128)(2,1)S(1)}, bf16[2,128,512]{2,1,0:T(8,128)(2,1)S(1)}, u32[]{:S(2)}, u32[]{:S(2)}) collective-permute-start(bf16[2,128,512]{2,1,0:T(8,128)(2,1)S(1)} %pad_maximum_fusion.34), channel_id=1, source_target_pairs={{0,2},{1,3},{2,0},{3,1},{4,6},{5,7},{6,4},{7,5},{8,10},{9,11},{10,... | collective-permute-start | bytes 786440 | tf_op jit(solution)/shard_map/ppermute | solution.py:75
  57.2 97.0 %collective-permute-start.26 = (bf16[2,128,512]{2,1,0:T(8,128)(2,1)S(1)}, bf16[2,128,512]{2,1,0:T(8,128)(2,1)S(1)}, u32[]{:S(2)}, u32[]{:S(2)}) collective-permute-start(bf16[2,128,512]{2,1,0:T(8,128)(2,1)S(1)} %pad_maximum_fusion.36), channel_id=1, source_target_pairs={{0,2},{1,3},{2,0},{3,1},{4,6},{5,7},{6,4},{7,5},{8,10},{9,11},{10,... | collective-permute-start | bytes 786440 | tf_op jit(solution)/shard_map/ppermute | solution.py:75
  60.4 21.8 %collective-permute-start.11 = (bf16[2,288,512]{2,1,0:T(8,128)(2,1)S(1)}, bf16[2,288,512]{2,1,0:T(8,128)(2,1)S(1)}, u32[]{:S(2)}, u32[]{:S(2)}) collective-permute-start(bf16[2,288,512]{2,1,0:T(8,128)(2,1)S(1)} %pad_maximum_fusion.14), channel_id=1, source_target_pairs={{0,2},{1,3},{2,0},{3,1},{4,6},{5,7},{6,4},{7,5},{8,10},{9,11},{10,... | collective-permute-start | bytes 1769480 | tf_op jit(solution)/shard_map/ppermute | solution.py:75
  63.1 30.3 %collective-permute-start.16 = (bf16[2,256,512]{2,1,0:T(8,128)(2,1)S(1)}, bf16[2,256,512]{2,1,0:T(8,128)(2,1)S(1)}, u32[]{:S(2)}, u32[]{:S(2)}) collective-permute-start(bf16[2,256,512]{2,1,0:T(8,128)(2,1)S(1)} %pad_maximum_fusion.29), channel_id=1, source_target_pairs={{0,2},{1,3},{2,0},{3,1},{4,6},{5,7},{6,4},{7,5},{8,10},{9,11},{10,... | collective-permute-start | bytes 1572872 | tf_op jit(solution)/shard_map/ppermute | solution.py:75
  64.7 52.5 %collective-permute-start.21 = (bf16[2,288,512]{2,1,0:T(8,128)(2,1)S(1)}, bf16[2,288,512]{2,1,0:T(8,128)(2,1)S(1)}, u32[]{:S(2)}, u32[]{:S(2)}) collective-permute-start(bf16[2,288,512]{2,1,0:T(8,128)(2,1)S(1)} %pad_maximum_fusion.16), channel_id=1, source_target_pairs={{0,2},{1,3},{2,0},{3,1},{4,6},{5,7},{6,4},{7,5},{8,10},{9,11},{10,... | collective-permute-start | bytes 1769480 | tf_op jit(solution)/shard_map/ppermute | solution.py:75
  84.8 27.6 %collective-permute-start.12 = (bf16[1,288,512]{2,1,0:T(8,128)(2,1)S(1)}, bf16[1,288,512]{2,1,0:T(8,128)(2,1)S(1)}, u32[]{:S(2)}, u32[]{:S(2)}) collective-permute-start(bf16[1,288,512]{2,1,0:T(8,128)(2,1)S(1)} %get-tuple-element.166), channel_id=1, source_target_pairs={{0,2},{1,3},{2,0},{3,1},{4,6},{5,7},{6,4},{7,5},{8,10},{9,11},{10,... | collective-permute-start | bytes 884744 | tf_op jit(solution)/shard_map/ppermute | solution.py:75
  93.5 26.7 %collective-permute-start.17 = (bf16[1,256,512]{2,1,0:T(8,128)(2,1)S(1)}, bf16[1,256,512]{2,1,0:T(8,128)(2,1)S(1)}, u32[]{:S(2)}, u32[]{:S(2)}) collective-permute-start(bf16[1,256,512]{2,1,0:T(8,128)(2,1)S(1)} %get-tuple-element.162), channel_id=1, source_target_pairs={{0,2},{1,3},{2,0},{3,1},{4,6},{5,7},{6,4},{7,5},{8,10},{9,11},{10,... | collective-permute-start | bytes 786440 | tf_op jit(solution)/shard_map/ppermute | solution.py:75
  112.4 15.6 %collective-permute-start.13 = (bf16[2,288,512]{2,1,0:T(8,128)(2,1)S(1)}, bf16[2,288,512]{2,1,0:T(8,128)(2,1)S(1)}, u32[]{:S(2)}, u32[]{:S(2)}) collective-permute-start(bf16[2,288,512]{2,1,0:T(8,128)(2,1)S(1)} %pad_maximum_fusion.15), channel_id=1, source_target_pairs={{0,1},{1,0},{2,3},{3,2},{4,5},{5,4},{6,7},{7,6},{8,9},{9,8},{10,11... | collective-permute-start | bytes 1769480 | tf_op jit(solution)/shard_map/ppermute | solution.py:75
  115.6 15.4 %collective-permute-start.7 = (bf16[1,128,512]{2,1,0:T(8,128)(2,1)S(1)}, bf16[1,128,512]{2,1,0:T(8,128)(2,1)S(1)}, u32[]{:S(2)}, u32[]{:S(2)}) collective-permute-start(bf16[1,128,512]{2,1,0:T(8,128)(2,1)S(1)} %get-tuple-element.170), channel_id=1, source_target_pairs={{0,2},{1,3},{2,0},{3,1},{4,6},{5,7},{6,4},{7,5},{8,10},{9,11},{10,... | collective-permute-start | bytes 393224 | tf_op jit(solution)/shard_map/ppermute | solution.py:75
  120.2 14.7 %collective-permute-start.18 = (bf16[2,256,512]{2,1,0:T(8,128)(2,1)S(1)}, bf16[2,256,512]{2,1,0:T(8,128)(2,1)S(1)}, u32[]{:S(2)}, u32[]{:S(2)}) collective-permute-start(bf16[2,256,512]{2,1,0:T(8,128)(2,1)S(1)} %pad_maximum_fusion.30), channel_id=1, source_target_pairs={{0,1},{1,0},{2,3},{3,2},{4,5},{5,4},{6,7},{7,6},{8,9},{9,8},{10,11... | collective-permute-start | bytes 1572872 | tf_op jit(solution)/shard_map/ppermute | solution.py:75
  128.9 55.4 %collective-permute-start.14 = (bf16[8,288,512]{2,1,0:T(8,128)(2,1)}, bf16[8,288,512]{2,1,0:T(8,128)(2,1)}, u32[]{:S(2)}, u32[]{:S(2)}) collective-permute-start(bf16[8,288,512]{2,1,0:T(8,128)(2,1)} %constant_dynamic-update-slice_fusion.6.rest_0_), channel_id=1, source_target_pairs={{0,4},{1,5},{2,6},{3,7},{4,0},{5,1},{6,2},{7,3},{8,12},{9,13},{10,... | collective-permute-start | bytes 7077896 | tf_op jit(solution)/shard_map/ppermute | solution.py:75
  129.0 18.6 %collective-permute-start.23 = (bf16[2,288,512]{2,1,0:T(8,128)(2,1)S(1)}, bf16[2,288,512]{2,1,0:T(8,128)(2,1)S(1)}, u32[]{:S(2)}, u32[]{:S(2)}) collective-permute-start(bf16[2,288,512]{2,1,0:T(8,128)(2,1)S(1)} %pad_maximum_fusion.17), channel_id=1, source_target_pairs={{0,1},{1,0},{2,3},{3,2},{4,5},{5,4},{6,7},{7,6},{8,9},{9,8},{10,11... | collective-permute-start | bytes 1769480 | tf_op jit(solution)/shard_map/ppermute | solution.py:75
  131.1 20.8 %collective-permute-start.8 = (bf16[2,128,512]{2,1,0:T(8,128)(2,1)S(1)}, bf16[2,128,512]{2,1,0:T(8,128)(2,1)S(1)}, u32[]{:S(2)}, u32[]{:S(2)}) collective-permute-start(bf16[2,128,512]{2,1,0:T(8,128)(2,1)S(1)} %pad_maximum_fusion.35), channel_id=1, source_target_pairs={{0,1},{1,0},{2,3},{3,2},{4,5},{5,4},{6,7},{7,6},{8,9},{9,8},{10,11... | collective-permute-start | bytes 786440 | tf_op jit(solution)/shard_map/ppermute | solution.py:75
  135.0 62.3 %collective-permute-start.19 = (bf16[8,256,512]{2,1,0:T(8,128)(2,1)S(1)}, bf16[8,256,512]{2,1,0:T(8,128)(2,1)}, u32[]{:S(2)}, u32[]{:S(2)}) collective-permute-start(bf16[8,256,512]{2,1,0:T(8,128)(2,1)S(1)} %constant_dynamic-update-slice_fusion.12.rest_0_.rest_2_), channel_id=1, source_target_pairs={{0,4},{1,5},{2,6},{3,7},{4,0},{5,1},{6,2},{7,3},{8,12},{9,13},{10,... | collective-permute-start | bytes 6291464 | tf_op jit(solution)/shard_map/ppermute | solution.py:75
  148.5 74.9 %collective-permute-start.24 = (bf16[8,288,512]{2,1,0:T(8,128)(2,1)}, bf16[8,288,512]{2,1,0:T(8,128)(2,1)}, u32[]{:S(2)}, u32[]{:S(2)}) collective-permute-start(bf16[8,288,512]{2,1,0:T(8,128)(2,1)} %constant_dynamic-update-slice_fusion.18.rest_0_), channel_id=1, source_target_pairs={{0,4},{1,5},{2,6},{3,7},{4,0},{5,1},{6,2},{7,3},{8,12},{9,13},{10,... | collective-permute-start | bytes 7077896 | tf_op jit(solution)/shard_map/ppermute | solution.py:75
  154.1 20.2 %collective-permute-start.9 = (bf16[8,128,512]{2,1,0:T(8,128)(2,1)}, bf16[8,128,512]{2,1,0:T(8,128)(2,1)}, u32[]{:S(2)}, u32[]{:S(2)}) collective-permute-start(bf16[8,128,512]{2,1,0:T(8,128)(2,1)} %constant_dynamic-update-slice_fusion.rest_0_), channel_id=1, source_target_pairs={{0,4},{1,5},{2,6},{3,7},{4,0},{5,1},{6,2},{7,3},{8,12},{9,13},{10,... | collective-permute-start | bytes 3145736 | tf_op jit(solution)/shard_map/ppermute | solution.py:75
  171.3 84.4 %collective-permute-start.79 = (bf16[3,144,512]{2,1,0:T(8,128)(2,1)}, bf16[3,144,512]{2,1,0:T(8,128)(2,1)}, u32[]{:S(2)}, u32[]{:S(2)}) collective-permute-start(bf16[3,144,512]{2,1,0:T(8,128)(2,1)} %get-tuple-element.228), channel_id=1, source_target_pairs={{0,1},{1,0},{2,3},{3,2},{4,5},{5,4},{6,7},{7,6},{8,9},{9,8},{10,11... | collective-permute-start | bytes 1327112 | tf_op jit(solution)/shard_map/ppermute | solution.py:75
  174.3 81.4 %collective-permute-start.81 = (bf16[3,144,512]{2,1,0:T(8,128)(2,1)}, bf16[3,144,512]{2,1,0:T(8,128)(2,1)}, u32[]{:S(2)}, u32[]{:S(2)}) collective-permute-start(bf16[3,144,512]{2,1,0:T(8,128)(2,1)} %get-tuple-element.229), channel_id=1, source_target_pairs={{0,2},{1,3},{2,0},{3,1},{4,6},{5,7},{6,4},{7,5},{8,10},{9,11},{10,... | collective-permute-start | bytes 1327112 | tf_op jit(solution)/shard_map/ppermute | solution.py:75
  184.3 51.1 %collective-permute-start.29 = (bf16[8,128,512]{2,1,0:T(8,128)(2,1)}, bf16[8,128,512]{2,1,0:T(8,128)(2,1)S(1)}, u32[]{:S(2)}, u32[]{:S(2)}) collective-permute-start(bf16[8,128,512]{2,1,0:T(8,128)(2,1)} %constant_dynamic-update-slice_fusion.24.rest_0_), channel_id=1, source_target_pairs={{0,4},{1,5},{2,6},{3,7},{4,0},{5,1},{6,2},{7,3},{8,12},{9,13},{10,... | collective-permute-start | bytes 3145736 | tf_op jit(solution)/shard_map/ppermute | solution.py:75
  250.8 15.2 %all-to-all-start = ((bf16[32,8,512]{2,1,0:T(8,128)(2,1)}), bf16[32,8,512]{2,1,0:T(8,128)(2,1)S(1)}, u32[]{:S(2)}, u32[]{:S(2)}) async-start(bf16[32,8,512]{2,1,0:T(8,128)(2,1)} %bitcast.794), calls=%async_computation | async-start | bytes 524288 | tf_op jit(solution)/shard_map/all_to_all | solution.py:841
  258.1 22.7 %collective-permute-start.82 = (bf16[3,144,512]{2,1,0:T(8,128)(2,1)}, bf16[3,144,512]{2,1,0:T(8,128)(2,1)}, u32[]{:S(2)}, u32[]{:S(2)}) collective-permute-start(bf16[3,144,512]{2,1,0:T(8,128)(2,1)} %get-tuple-element.227), channel_id=1, source_target_pairs={{0,1},{1,0},{2,3},{3,2},{4,5},{5,4},{6,7},{7,6},{8,9},{9,8},{10,11... | collective-permute-start | bytes 1327112 | tf_op jit(solution)/shard_map/ppermute | solution.py:75
  290.4 16.3 %all-to-all-start.1 = ((bf16[32,8,512]{2,1,0:T(8,128)(2,1)}), bf16[32,8,512]{2,1,0:T(8,128)(2,1)}, u32[]{:S(2)}, u32[]{:S(2)}) async-start(bf16[32,8,512]{2,1,0:T(8,128)(2,1)} %bitcast.707), calls=%async_computation.1 | async-start | bytes 524288 | tf_op jit(solution)/shard_map/all_to_all | solution.py:857
  298.1 168.4 %collective-permute-start.83 = (bf16[3,2,144,512]{3,2,0,1:T(8,128)(2,1)}, bf16[3,2,144,512]{3,2,0,1:T(8,128)(2,1)}, u32[]{:S(2)}, u32[]{:S(2)}) collective-permute-start(bf16[3,2,144,512]{3,2,0,1:T(8,128)(2,1)} %pad_maximum_fusion.12), channel_id=1, source_target_pairs={{0,4},{1,5},{2,6},{3,7},{4,0},{5,1},{6,2},{7,3},{8,12},{9,13},{10,... | collective-permute-start | bytes 2654216 | tf_op jit(solution)/shard_map/ppermute | solution.py:75
  371.5 138.2 %collective-permute-start.60 = (bf16[4,2,544,512]{3,2,0,1:T(8,128)(2,1)}, bf16[4,2,544,512]{3,2,0,1:T(8,128)(2,1)}, u32[]{:S(2)}, u32[]{:S(2)}) collective-permute-start(bf16[4,2,544,512]{3,2,0,1:T(8,128)(2,1)} %pad_maximum_fusion.2), channel_id=1, source_target_pairs={{0,4},{1,5},{2,6},{3,7},{4,0},{5,1},{6,2},{7,3},{8,12},{9,13},{10,... | collective-permute-start | bytes 13369352 | tf_op jit(solution)/shard_map/ppermute | solution.py:75
  406.1 18.0 %collective-permute-start.32 = (bf16[4,2,128,512]{3,2,1,0:T(8,128)(2,1)S(1)}, bf16[4,2,128,512]{3,2,1,0:T(8,128)(2,1)S(1)}, u32[]{:S(2)}, u32[]{:S(2)}) collective-permute-start(bf16[4,2,128,512]{3,2,1,0:T(8,128)(2,1)S(1)} %dynamic-slice_bitcast_fusion.2), channel_id=1, source_target_pairs={{0,4},{1,5},{2,6},{3,7},{4,0},{5,1},{6,2},{7,3},{8,12},{9,13},{10,... | collective-permute-start | bytes 3145736 | tf_op jit(solution)/shard_map/ppermute | solution.py:75
  424.0 57.7 %collective-permute-start.46 = (bf16[4,2,416,512]{3,2,0,1:T(8,128)(2,1)}, bf16[4,2,416,512]{3,2,0,1:T(8,128)(2,1)}, u32[]{:S(2)}, u32[]{:S(2)}) collective-permute-start(bf16[4,2,416,512]{3,2,0,1:T(8,128)(2,1)} %pad_maximum_fusion.5), channel_id=1, source_target_pairs={{0,4},{1,5},{2,6},{3,7},{4,0},{5,1},{6,2},{7,3},{8,12},{9,13},{10,... | collective-permute-start | bytes 10223624 | tf_op jit(solution)/shard_map/ppermute | solution.py:75
  476.3 117.5 %collective-permute-start.78 = (f32[16,1024]{1,0:T(8,128)}, f32[16,1024]{1,0:T(8,128)}, u32[]{:S(2)}, u32[]{:S(2)}) collective-permute-start(f32[16,1024]{1,0:T(8,128)} %add.562), channel_id=1, source_target_pairs={{0,2},{1,3},{2,0},{3,1},{4,6},{5,7},{6,4},{7,5},{8,10},{9,11},{10,... | collective-permute-start | bytes 196616 | tf_op jit(solution)/shard_map/ppermute | solution.py:75
  485.4 21.9 %collective-permute-start.47 = (bf16[2,416,512]{2,1,0:T(8,128)(2,1)S(1)}, bf16[2,416,512]{2,1,0:T(8,128)(2,1)S(1)}, u32[]{:S(2)}, u32[]{:S(2)}) collective-permute-start(bf16[2,416,512]{2,1,0:T(8,128)(2,1)S(1)} %dynamic-slice_bitcast_fusion.4), channel_id=1, source_target_pairs={{0,1},{1,0},{2,3},{3,2},{4,5},{5,4},{6,7},{7,6},{8,9},{9,8},{10,11... | collective-permute-start | bytes 2555912 | tf_op jit(solution)/shard_map/ppermute | solution.py:75
  487.6 21.3 %collective-permute-start.49 = (bf16[2,416,512]{2,1,0:T(8,128)(2,1)S(1)}, bf16[2,416,512]{2,1,0:T(8,128)(2,1)S(1)}, u32[]{:S(2)}, u32[]{:S(2)}) collective-permute-start(bf16[2,416,512]{2,1,0:T(8,128)(2,1)S(1)} %dynamic-slice_bitcast_fusion.3), channel_id=1, source_target_pairs={{0,2},{1,3},{2,0},{3,1},{4,6},{5,7},{6,4},{7,5},{8,10},{9,11},{10,... | collective-permute-start | bytes 2555912 | tf_op jit(solution)/shard_map/ppermute | solution.py:75
  488.5 36.3 %collective-permute-start.41 = (bf16[1,144,512]{2,1,0:T(8,128)(2,1)S(1)}, bf16[1,144,512]{2,1,0:T(8,128)(2,1)S(1)}, u32[]{:S(2)}, u32[]{:S(2)}) collective-permute-start(bf16[1,144,512]{2,1,0:T(8,128)(2,1)S(1)} %get-tuple-element.248), channel_id=1, source_target_pairs={{0,1},{1,0},{2,3},{3,2},{4,5},{5,4},{6,7},{7,6},{8,9},{9,8},{10,11... | collective-permute-start | bytes 442376 | tf_op jit(solution)/shard_map/ppermute | solution.py:75
  507.2 17.6 %collective-permute-start.43 = (bf16[1,144,512]{2,1,0:T(8,128)(2,1)S(1)}, bf16[1,144,512]{2,1,0:T(8,128)(2,1)S(1)}, u32[]{:S(2)}, u32[]{:S(2)}) collective-permute-start(bf16[1,144,512]{2,1,0:T(8,128)(2,1)S(1)} %get-tuple-element.249), channel_id=1, source_target_pairs={{0,2},{1,3},{2,0},{3,1},{4,6},{5,7},{6,4},{7,5},{8,10},{9,11},{10,... | collective-permute-start | bytes 442376 | tf_op jit(solution)/shard_map/ppermute | solution.py:75
  523.3 46.3 %collective-permute-start.61 = (bf16[2,544,512]{2,1,0:T(8,128)(2,1)S(1)}, bf16[2,544,512]{2,1,0:T(8,128)(2,1)S(1)}, u32[]{:S(2)}, u32[]{:S(2)}) collective-permute-start(bf16[2,544,512]{2,1,0:T(8,128)(2,1)S(1)} %dynamic-slice_bitcast_fusion.1), channel_id=1, source_target_pairs={{0,1},{1,0},{2,3},{3,2},{4,5},{5,4},{6,7},{7,6},{8,9},{9,8},{10,11... | collective-permute-start | bytes 3342344 | tf_op jit(solution)/shard_map/ppermute | solution.py:75
  524.9 25.9 %collective-permute-start.44 = (bf16[1,144,512]{2,1,0:T(8,128)(2,1)S(1)}, bf16[1,144,512]{2,1,0:T(8,128)(2,1)S(1)}, u32[]{:S(2)}, u32[]{:S(2)}) collective-permute-start(bf16[1,144,512]{2,1,0:T(8,128)(2,1)S(1)} %get-tuple-element.247), channel_id=1, source_target_pairs={{0,1},{1,0},{2,3},{3,2},{4,5},{5,4},{6,7},{7,6},{8,9},{9,8},{10,11... | collective-permute-start | bytes 442376 | tf_op jit(solution)/shard_map/ppermute | solution.py:75
  525.5 26.1 %collective-permute-start.42 = (bf16[1,144,512]{2,1,0:T(8,128)(2,1)S(1)}, bf16[1,144,512]{2,1,0:T(8,128)(2,1)S(1)}, u32[]{:S(2)}, u32[]{:S(2)}) collective-permute-start(bf16[1,144,512]{2,1,0:T(8,128)(2,1)S(1)} %get-tuple-element.246), channel_id=1, source_target_pairs={{0,2},{1,3},{2,0},{3,1},{4,6},{5,7},{6,4},{7,5},{8,10},{9,11},{10,... | collective-permute-start | bytes 442376 | tf_op jit(solution)/shard_map/ppermute | solution.py:75
  531.3 39.0 %collective-permute-start.63 = (bf16[2,544,512]{2,1,0:T(8,128)(2,1)S(1)}, bf16[2,544,512]{2,1,0:T(8,128)(2,1)S(1)}, u32[]{:S(2)}, u32[]{:S(2)}) collective-permute-start(bf16[2,544,512]{2,1,0:T(8,128)(2,1)S(1)} %dynamic-slice_bitcast_fusion), channel_id=1, source_target_pairs={{0,2},{1,3},{2,0},{3,1},{4,6},{5,7},{6,4},{7,5},{8,10},{9,11},{10,... | collective-permute-start | bytes 3342344 | tf_op jit(solution)/shard_map/ppermute | solution.py:75
  550.8 18.6 %collective-permute-start.52 = (bf16[416,512]{1,0:T(8,128)(2,1)S(1)}, bf16[416,512]{1,0:T(8,128)(2,1)S(1)}, u32[]{:S(2)}, u32[]{:S(2)}) collective-permute-start(bf16[416,512]{1,0:T(8,128)(2,1)S(1)} %fusion.141), channel_id=1, source_target_pairs={{0,16},{1,17},{2,18},{3,19},{4,20},{5,21},{6,22},{7,23},{8,24},{9,... | collective-permute-start | bytes 1277960 | tf_op jit(solution)/shard_map/ppermute | solution.py:75
  552.4 43.6 %collective-permute-start.45 = (bf16[1,2,144,512]{3,2,1,0:T(8,128)(2,1)}, bf16[1,2,144,512]{3,2,1,0:T(8,128)(2,1)}, u32[]{:S(2)}, u32[]{:S(2)}) collective-permute-start(bf16[1,2,144,512]{3,2,1,0:T(8,128)(2,1)} %pad_maximum_fusion.32), channel_id=1, source_target_pairs={{0,4},{1,5},{2,6},{3,7},{4,0},{5,1},{6,2},{7,3},{8,12},{9,13},{10,... | collective-permute-start | bytes 884744 | tf_op jit(solution)/shard_map/ppermute | solution.py:75
  569.8 14.6 %collective-permute-start.62 = (bf16[544,512]{1,0:T(8,128)(2,1)S(1)}, bf16[544,512]{1,0:T(8,128)(2,1)S(1)}, u32[]{:S(2)}, u32[]{:S(2)}) collective-permute-start(bf16[544,512]{1,0:T(8,128)(2,1)S(1)} %dynamic-slice_bitcast_fusion.6), channel_id=1, source_target_pairs={{0,2},{1,3},{2,0},{3,1},{4,6},{5,7},{6,4},{7,5},{8,10},{9,11},{10,... | collective-permute-start | bytes 1671176 | tf_op jit(solution)/shard_map/ppermute | solution.py:75
  582.5 21.9 %collective-permute-start.54 = (bf16[2,416,512]{2,1,0:T(8,128)(2,1)}, bf16[2,416,512]{2,1,0:T(8,128)(2,1)}, u32[]{:S(2)}, u32[]{:S(2)}) collective-permute-start(bf16[2,416,512]{2,1,0:T(8,128)(2,1)} %pad_maximum_fusion.13), channel_id=1, source_target_pairs={{0,4},{1,5},{2,6},{3,7},{4,0},{5,1},{6,2},{7,3},{8,12},{9,13},{10,... | collective-permute-start | bytes 2555912 | tf_op jit(solution)/shard_map/ppermute | solution.py:75
  601.9 25.6 %collective-permute-start.66 = (bf16[544,512]{1,0:T(8,128)(2,1)}, bf16[544,512]{1,0:T(8,128)(2,1)}, u32[]{:S(2)}, u32[]{:S(2)}) collective-permute-start(bf16[544,512]{1,0:T(8,128)(2,1)} %fusion.108), channel_id=1, source_target_pairs={{0,16},{1,17},{2,18},{3,19},{4,20},{5,21},{6,22},{7,23},{8,24},{9,... | collective-permute-start | bytes 1671176 | tf_op jit(solution)/shard_map/ppermute | solution.py:75
  644.2 16.2 %collective-permute-start.68 = (bf16[2,544,512]{2,1,0:T(8,128)(2,1)}, bf16[2,544,512]{2,1,0:T(8,128)(2,1)}, u32[]{:S(2)}, u32[]{:S(2)}) collective-permute-start(bf16[2,544,512]{2,1,0:T(8,128)(2,1)} %pad_maximum_fusion.10), channel_id=1, source_target_pairs={{0,4},{1,5},{2,6},{3,7},{4,0},{5,1},{6,2},{7,3},{8,12},{9,13},{10,... | collective-permute-start | bytes 3342344 | tf_op jit(solution)/shard_map/ppermute | solution.py:75
  658.0 40.9 %collective-permute-start.58 = (bf16[2,144,512]{2,1,0:T(8,128)(2,1)}, bf16[2,144,512]{2,1,0:T(8,128)(2,1)}, u32[]{:S(2)}, u32[]{:S(2)}) collective-permute-start(bf16[2,144,512]{2,1,0:T(8,128)(2,1)} %get-tuple-element.237), channel_id=1, source_target_pairs={{0,1},{1,0},{2,3},{3,2},{4,5},{5,4},{6,7},{7,6},{8,9},{9,8},{10,11... | collective-permute-start | bytes 884744 | tf_op jit(solution)/shard_map/ppermute | solution.py:75
  658.8 41.2 %collective-permute-start.56 = (bf16[2,144,512]{2,1,0:T(8,128)(2,1)}, bf16[2,144,512]{2,1,0:T(8,128)(2,1)}, u32[]{:S(2)}, u32[]{:S(2)}) collective-permute-start(bf16[2,144,512]{2,1,0:T(8,128)(2,1)} %get-tuple-element.236), channel_id=1, source_target_pairs={{0,2},{1,3},{2,0},{3,1},{4,6},{5,7},{6,4},{7,5},{8,10},{9,11},{10,... | collective-permute-start | bytes 884744 | tf_op jit(solution)/shard_map/ppermute | solution.py:75
  (215 other events, 2336.7 us)

commit v2 on v1

v2 whole, which is shorter than its diff:
```python
import functools
import math

import jax
import jax.numpy as jnp
import numpy as np
from jax import lax
from jax.experimental import pallas as pl
from jax.experimental.pallas import tpu as pltpu
from jax.sharding import PartitionSpec as P

C = 2048
MID = 512
ACTIONS = 18
ATOMS = 51
GROUPS = 32
SIDE = 11
PIX = SIDE * SIDE
BLOCKS = 2
MB = 2
STEP = 10
SEG = 64
HPAD = ACTIONS * SEG
HOUT = ACTIONS * ATOMS

bf16 = jnp.bfloat16
f32 = jnp.float32

eps_norm = 1e-05
decay_moment = 0.5
beta_second = 0.95
adam_eps = 1e-08
rate_muon = 0.2
decay_muon = 0.01
rate_head = 0.02
decay_head = 0.01
rate_gain = 0.05
clip_limit = 0.01
cql_alpha = 0.05
value_max = 3.0
coef_a = 3.4445
coef_b = -4.775
coef_c = 2.0315

FROWS = 128
FPB = 2
BROWS = FPB * FROWS
TAPS = [(dr, dc) for dr in (-1, 0, 1) for dc in (-1, 0, 1)]
MIB = 1024 * 1024


def tap_masks():
    pixel = np.arange(FROWS)
    row, col = pixel // SIDE, pixel % SIDE
    masks = [
        (pixel < PIX) & (row + dr >= 0) & (row + dr < SIDE) & (col + dc >= 0) & (col + dc < SIDE)
        for dr, dc in TAPS
    ]
    return np.repeat(np.stack(masks).astype(np.float32).reshape(9 * FROWS, 1), 128, axis=1)


class Net:
    def __init__(self, dp, ns):
        self.dp, self.ns = dp, ns
        self.ns_bits = [1 << i for i in range(ns.bit_length() - 1)]
        self.dp_bits = [1 << i for i in range(dp.bit_length() - 1)]
        self.plain = not (dp == 8 and ns == 4)

    def swap(self, value, axis, bit):
        pairs = []
        for d in range(self.dp):
            for n in range(self.ns):
                partner = (d ^ bit) * self.ns + n if axis == "dp" else d * self.ns + (n ^ bit)
                pairs.append((d * self.ns + n, partner))
        return lax.ppermute(value, ("dp", "ns"), pairs)

    def add_all(self, value, axes=("dp", "ns")):
        for axis in axes:
            for bit in self.dp_bits if axis == "dp" else self.ns_bits:
                value = value + self.swap(value, axis, bit)
        return value


def pick(value, index, axis):
    return lax.dynamic_index_in_dim(value, index, axis, keepdims=False)


def bit_of(index, shift):
    return lax.rem(lax.div(index, 1 << shift), 2)


def after(value, *deps):
    return lax.optimization_barrier((value,) + deps)[0]


class Run:
    def __init__(self, steps):
        self.steps, self.deps, self.done, self.value = steps, None, False, None

    def step(self, *deps):
        if self.done:
            return ()
        try:
            sent = self.steps.send(deps if self.deps else None)
            self.deps = True
            return tuple(sent)
        except StopIteration as end:
            self.done, self.value = True, end.value
            return ()


class Shards:
    def __init__(self, arrays, pieces):
        self.arrays, self.pieces = arrays, pieces


def own_half(own):
    core = bit_of(lax.axis_index("dp"), 0)
    return pick(own.reshape(2, own.shape[0] // 2, MID), core, 0)


def gather_direct(net, shard):
    own = shard.astype(bf16)
    if net.plain:
        return Run(at_once([Shards((lax.all_gather(own, "ns", axis=0, tiled=True),), None)]))
    return Run(gather_direct_steps(net, own))


def at_once(value):
    if value is None:
        yield ()
    return value


def gather_direct_steps(net, own):
    half = own_half(own)
    n = half.shape[0]
    got = tuple(net.swap(half, "ns", rel) for rel in (1, 2, 3))
    deps = yield (got[0],)
    got = tuple(after(v, *deps) for v in got)
    other = tuple(net.swap(v, "dp", 1) for v in got)
    deps = yield got
    pieces = [(0, 0, (0, None, 0, 2 * n), 2 * n)]
    for core in range(2):
        for rel in (1, 2, 3):
            pieces.append((core * 3 + rel, 0, (rel, core, 0, 2 * n), n))
    return [Shards((own,) + got + other, pieces)]


def gather_two(net, shards, *deps):
    owns = [v.astype(bf16) for v in shards]
    if net.plain:
        return Run(
            at_once([Shards((lax.all_gather(v, "ns", axis=0, tiled=True),), None) for v in owns])
        )
    return Run(gather_two_steps(net, owns, deps))


def gather_two_steps(net, owns, deps):
    halves = [own_half(v) for v in owns]
    sizes = [v.shape[0] // 2 for v in halves]
    rows = sum(sizes)
    sent = jnp.concatenate(
        [v[:n] for v, n in zip(halves, sizes, strict=True)]
        + [v[n:] for v, n in zip(halves, sizes, strict=True)],
        axis=0,
    )
    sent = after(sent, *deps) if deps else sent
    got_x, got_y = net.swap(sent, "ns", 1), net.swap(sent, "ns", 2)
    deps = yield (sent,)
    got_x, got_y = after(got_x, *deps), after(got_y, *deps)
    sent = got_x[:rows], got_y[rows:]
    got_a, got_b = net.swap(sent[0], "ns", 2), net.swap(sent[1], "ns", 1)
    other = net.swap(got_x, "dp", 1), net.swap(got_y, "dp", 1)
    deps = yield sent
    got_a, got_b = after(got_a, *deps), after(got_b, *deps)
    got = (got_x, got_y, got_a, got_b)
    other = other + (net.swap(got_a, "dp", 1), net.swap(got_b, "dp", 1))
    yield got
    out, start = [], 0
    for own, n in zip(owns, sizes, strict=True):
        pieces = [(0, 0, (0, None, 0, 4 * n), 4 * n)]
        for core in range(2):
            at = 1 + 4 * core
            for rel, k in ((1, at), (2, at + 1)):
                pieces.append((k, start, (rel, core, 0, 4 * n), n))
                pieces.append((k, rows + start, (rel, core, n, 4 * n), n))
            pieces.append((at + 2, start, (3, core, 0, 4 * n), n))
            pieces.append((at + 3, start, (3, core, n, 4 * n), n))
        out.append(Shards((own,) + got + other, pieces))
        start += n
    return out


def export_rows(shard, buffer, full, sems):
    if full is None:
        return lambda: None
    copy = pltpu.make_async_copy(buffer, full, sems.at[13])
    pl.when(pl.program_id(0) == 0)(copy.start)
    return lambda: pl.when(pl.program_id(0) == pl.num_programs(0) - 1)(copy.wait)


def row_copies(shard, refs, pos_ref, buffer, sems):
    if shard.pieces is None:
        return [pltpu.make_async_copy(refs[0], buffer, sems.at[0])]
    here, my_core = pos_ref[0], pos_ref[1]
    copies = []
    for q, (k, row, (rel, core, offset, each), n) in enumerate(shard.pieces):
        if core is None:
            place = here * each
        else:
            place = (here ^ rel) * each + (my_core ^ core) * (each // 2) + offset
        copies.append(
            pltpu.make_async_copy(
                refs[k].at[pl.ds(row, n)],
                buffer.at[pl.ds(pl.multiple_of(place, 16), n)],
                sems.at[q],
            )
        )
    return copies


def load_rows(shard, refs, pos_ref, buffer, sems):
    copies = row_copies(shard, refs, pos_ref, buffer, sems)
    for copy in copies:
        copy.start()
    for copy in copies:
        copy.wait()


def place_rows(shard, refs, pos_ref, full, buffer, sems):
    copies = row_copies(shard, refs, pos_ref, buffer, sems)
    out = pltpu.make_async_copy(buffer, full, sems.at[13])
    step = pl.program_id(0)

    @pl.when(step == 0)
    def _():
        for copy in copies:
            copy.start()

    @pl.when(step == 1)
    def _():
        for copy in copies:
            copy.wait()
        out.start()

    @pl.when(step == pl.num_programs(0) - 1)
    def _():
        out.wait()


class Share:
    def __init__(self, arrays, pieces):
        self.arrays, self.pieces = arrays, pieces

    def copies(self, refs, pos, buffer, start, sems, first):
        out = []
        for q, (k, row, core, path, n) in enumerate(self.pieces):
            if core is None:
                place = start + path * n
            else:
                place = start + ((pos[1] ^ core) * 2 + (pos[5] ^ path)) * n
                place = pl.multiple_of(place, 16)
            out.append(
                pltpu.make_async_copy(
                    refs[k].at[pl.ds(row, n)], buffer.at[pl.ds(place, n)], sems.at[first + q]
                )
            )
        return out


def vmem_call(kernel, name, ins, outs):
    return pl.pallas_call(
        kernel,
        name=name,
        in_specs=[pl.BlockSpec(memory_space=pltpu.SMEM)]
        + [pl.BlockSpec(memory_space=pltpu.VMEM)] * (len(ins) - 1),
        out_shape=[jax.ShapeDtypeStruct(shape, bf16) for shape in outs],
        cost_estimate=pl.CostEstimate(flops=1024, bytes_accessed=1024, transcendentals=0),
        compiler_params=pltpu.CompilerParams(vmem_limit_bytes=24 * MIB),
    )(*ins)


def split_kernel(count, pos, *refs):
    grads, (got, send_a, send_b, keep_a, keep_b) = refs[:count], refs[count:]
    core, x, y = pos[1], pos[3], pos[4]
    start = 0
    for g in grads:
        rows = pl.ds(start, g.shape[4])
        start += g.shape[4]
        for j in range(2):
            send_a[j, rows] = g[j, 1 - x, core, 0] + got[j, 1 - x, 0, rows]
            keep_a[j, rows] = g[j, x, core, 0] + got[j, x, 0, rows]
            send_b[j, rows] = g[1 - y, j, core, 1] + got[1 - y, j, 1, rows]
            keep_b[j, rows] = g[y, j, core, 1] + got[y, j, 1, rows]


def turn_kernel(pos, keep_a, keep_b, got_a, got_b, send_a, send_b, rest_a, rest_b):
    x, y = pos[3], pos[4]
    send_a[...] = keep_a[1 - y] + got_a[1 - y]
    send_b[...] = keep_b[1 - x] + got_b[1 - x]
    rest_a[...] = keep_a[y] + got_a[y]
    rest_b[...] = keep_b[x] + got_b[x]


def half_kernel(pos, rest_a, rest_b, got_a, got_b, send, keep):
    @pl.when(pos[5] == 0)
    def _():
        send[...] = rest_b[...] + got_b[...]
        keep[...] = rest_a[...] + got_a[...]

    @pl.when(pos[5] == 1)
    def _():
        send[...] = rest_a[...] + got_a[...]
        keep[...] = rest_b[...] + got_b[...]


def reduce_steps(net, pos, grads):
    if net.plain:
        out = []
        for g in grads:
            share = lax.psum_scatter(g.astype(f32), "ns", scatter_dimension=0, tiled=True)
            out.append(Share((lax.psum(share, "dp").astype(bf16),), [(0, 0, None, 0, share.shape[0])]))
        return out
    core = pos[1]

    def half(some, which):
        parts = [pick(g, which, 2) for g in some]
        return jnp.concatenate(parts, axis=3) if len(parts) > 1 else parts[0]

    grads = [g.reshape(2, 2, 2, 2, g.shape[0] // 16, MID) for g in grads]
    sent = half(grads, 1 - core)
    got = net.swap(sent, "dp", 1)
    deps = yield (sent,)
    got = after(got, *deps)
    sizes = [g.shape[4] for g in grads]
    n = sum(sizes)
    two, one = (2, n, MID), (n, MID)
    send_a, send_b, keep_a, keep_b = vmem_call(
        functools.partial(split_kernel, len(grads)), "split_sum", [pos, *grads, got], [two] * 4
    )
    got_a, got_b = net.swap(send_a, "ns", 1), net.swap(send_b, "ns", 2)
    deps = yield send_a, send_b
    got_a, got_b = after(got_a, *deps), after(got_b, *deps)
    send_a, send_b, rest_a, rest_b = vmem_call(
        turn_kernel, "turn_sum", [pos, keep_a, keep_b, got_a, got_b], [one] * 4
    )
    got_a, got_b = net.swap(send_a, "ns", 2), net.swap(send_b, "ns", 1)
    deps = yield send_a, send_b
    got_a, got_b = after(got_a, *deps), after(got_b, *deps)
    sent, kept = vmem_call(half_kernel, "half_sum", [pos, rest_a, rest_b, got_a, got_b], [one] * 2)
    got = net.swap(sent, "dp", 2)
    deps = yield (sent,)
    kept = kept + after(got, *deps)
    got = net.swap(kept, "dp", 4)
    deps = yield (kept,)
    kept = kept + after(got, *deps)
    given, kept_other = net.swap(kept, "dp", 2), net.swap(kept, "dp", 1)
    deps = yield (kept,)
    given = after(given, *deps)
    given_other = net.swap(given, "dp", 1)
    deps = yield (given,)
    kept_other, given_other = after(kept_other, *deps), after(given_other, *deps)
    out, start = [], 0
    for size in sizes:
        out.append(
            Share(
                (kept, given, kept_other, given_other),
                [(k, start, k // 2, k % 2, size) for k in range(4)],
            )
        )
        start += size
    return out


HALF = MID // 2
PACK = HALF + 32
PATH = PACK // 2


def gram_steps(net, packs):
    first, second = packs
    if net.plain:
        first, second = (lax.psum(v.astype(f32), "ns").astype(bf16) for v in packs)
        return first, second, net.swap(first, "dp", 1), net.swap(second, "dp", 1)
    got_a, got_b = net.swap(first, "ns", 1), net.swap(second, "ns", 2)
    deps = yield first, second
    first, second = first + after(got_a, *deps), second + after(got_b, *deps)
    got_a, got_b = net.swap(first, "ns", 2), net.swap(second, "ns", 1)
    deps = yield first, second
    first, second = first + after(got_a, *deps), second + after(got_b, *deps)
    other = net.swap(first, "dp", 1), net.swap(second, "dp", 1)
    deps = yield first, second
    return first, second, after(other[0], *deps), after(other[1], *deps)


def add_steps(net, value):
    for axis, bits in (("dp", net.dp_bits), ("ns", net.ns_bits)):
        for bit in bits:
            got = net.swap(value, axis, bit)
            deps = yield (value,)
            value = value + after(got, *deps)
    return value


def sigmoid(v):
    return 0.5 * jnp.tanh(0.5 * v) + 0.5


def group_sum(t, size):
    tiles = t.shape[1] // 128
    u = jnp.concatenate([t[:, j * 128 : (j + 1) * 128] for j in range(tiles)], axis=0)
    lane = lax.broadcasted_iota(jnp.int32, u.shape, 1)
    step = 1
    while step < size:
        u = u + jnp.where(
            (lane & step) == 0, pltpu.roll(u, 128 - step, 1), pltpu.roll(u, step, 1)
        )
        step *= 2
    return jnp.concatenate([u[8 * j : 8 * j + 8] for j in range(tiles)], axis=1)


class Norm:
    def __init__(self, ref, layer, part):
        self.ref, self.row, self.base = ref, 2 * layer, (0, MID, 2 * MID)[part]

    def row_of(self, row, lanes):
        return self.ref[row : row + 1, self.base + lanes.start : self.base + lanes.stop]

    def gain(self, lanes):
        return self.row_of(self.row, lanes)

    def bias(self, lanes):
        return self.row_of(self.row + 1, lanes)


def live_rows():
    return lax.broadcasted_iota(jnp.int32, (FROWS, 128), 0) < PIX


def norm_stats(st, size):
    sums = group_sum(st[...], size) * (1.0 / (PIX * size))
    mean = sums[0:FPB]
    spread = jnp.maximum(sums[FPB : 2 * FPB] - mean * mean, 0.0)
    return mean, lax.rsqrt(spread + eps_norm)


def add_stats(st, f, lanes, v):
    st[f : f + 1, lanes] = jnp.sum(v, axis=0, keepdims=True)
    st[FPB + f : FPB + f + 1, lanes] = jnp.sum(v * v, axis=0, keepdims=True)


def units(width):
    for j in range(width // 128):
        for f in range(FPB):
            yield f, pl.ds(f * FROWS, FROWS), slice(j * 128, (j + 1) * 128)


def first_step(body):
    pl.when(pl.program_id(0) == 0)(body)


def reduce_kernel(shard, also, layer, pos, x, gains, *rest):
    gb = Norm(gains, layer, 0)
    n = len(shard.arrays)
    refs, rest = rest[:n], rest[n:]
    if also is not None:
        n = len(also.arrays)
        place_rows(also, rest[:n], pos, rest[n + 4], *rest[-2:])
        rest = rest[n : n + 4] + rest[n + 5 : -2]
    h, xh, rs, full, buf, sems, acc, st = rest

    @first_step
    def _():
        load_rows(shard, refs, pos, buf, sems)
        st[...] = jnp.zeros_like(st)

    finish = export_rows(shard, buf, full, sems)
    for j in range(MID // 256):
        lanes = slice(j * 256, (j + 1) * 256)
        a = jnp.dot(x[...], buf[:, lanes], preferred_element_type=f32)
        acc[:, lanes] = a
        for f in range(FPB):
            add_stats(st, f, lanes, a[f * FROWS : (f + 1) * FROWS])
    norm_out(acc, st, gb, h, xh, rs)
    finish()


def norm_out(acc, st, gb, h, xh, rs):
    mean, rstd = norm_stats(st, MID // GROUPS)
    rs[...] = jnp.zeros_like(rs)
    rs[0:FPB] = rstd
    live = live_rows()
    for f, rows, lanes in units(MID):
        v = jnp.where(live, (acc[rows, lanes] - mean[f : f + 1, lanes]) * rstd[f : f + 1, lanes], 0.0)
        xh[rows, lanes] = v.astype(bf16)
        v = v * gb.gain(lanes) + gb.bias(lanes)
        h[rows, lanes] = jnp.where(live, v * sigmoid(v), 0.0).astype(bf16)


def spread_taps(src, masks, taps):
    for f, rows, lanes in units(MID):
        v = src[rows, lanes].astype(f32)
        for k, (dr, dc) in enumerate(TAPS):
            shift = -(dr * SIDE + dc)
            t = v if shift == 0 else pltpu.roll(v, shift % FROWS, 0)
            t = t * masks[k * FROWS : (k + 1) * FROWS]
            taps[rows, k * MID + lanes.start : k * MID + lanes.stop] = t.astype(bf16)


def conv_kernel(shard, also, layer, pos, src, masks, gains, *rest):
    gb = Norm(gains, layer, 1)
    n = len(shard.arrays)
    refs, rest = rest[:n], rest[n:]
    if also is not None:
        n = len(also.arrays)
        place_rows(also, rest[:n], pos, rest[n + 5], *rest[-2:])
        rest = rest[n : n + 5] + rest[n + 6 : -2]
    taps, u2, xh, rs, full, buf, sems, acc, st = rest

    @first_step
    def _():
        load_rows(shard, refs, pos, buf, sems)
        st[...] = jnp.zeros_like(st)

    finish = export_rows(shard, buf, full, sems)
    spread_taps(src, masks, taps)
    for j in range(MID // 256):
        lanes = slice(j * 256, (j + 1) * 256)
        a = jnp.dot(taps[...], buf[:, lanes], preferred_element_type=f32)
        acc[:, lanes] = a
        for f in range(FPB):
            add_stats(st, f, lanes, a[f * FROWS : (f + 1) * FROWS])
    norm_out(acc, st, gb, u2, xh, rs)
    finish()


def expand_kernel(shard, layer, last, pos, u2, x, gains, *rest):
    gb = Norm(gains, layer, 2)
    n = len(shard.arrays)
    refs, (xh, rs, out, full, buf, sems, acc, st) = rest[:n], rest[n:]

    @first_step
    def _():
        load_rows(shard, refs, pos, buf, sems)
        st[...] = jnp.zeros_like(st)

    finish = export_rows(shard, buf, full, sems)
    for j in range(C // 256):
        lanes = slice(j * 256, (j + 1) * 256)
        a = lax.dot_general(
            u2[...], buf[lanes, :], (((1,), (1,)), ((), ())), preferred_element_type=f32
        )
        acc[:, lanes] = a
        for f in range(FPB):
            add_stats(st, f, lanes, a[f * FROWS : (f + 1) * FROWS])
    mean, rstd = norm_stats(st, C // GROUPS)
    rs[...] = jnp.zeros_like(rs)
    rs[0:FPB] = rstd
    if last:
        out[...] = jnp.zeros_like(out)
    live = live_rows()
    for f, rows, lanes in units(C):
        v = jnp.where(live, (acc[rows, lanes] - mean[f : f + 1, lanes]) * rstd[f : f + 1, lanes], 0.0)
        xh[rows, lanes] = v.astype(bf16)
        v = x[rows, lanes].astype(f32) + (v * gb.gain(lanes) + gb.bias(lanes))
        v = jnp.where(live, v * sigmoid(v), 0.0)
        if last:
            out[f : f + 1, lanes] = jnp.sum(v, axis=0, keepdims=True) * (1.0 / PIX)
        else:
            out[rows, lanes] = v.astype(bf16)
    finish()


def back_sums(st, f, lanes, dv, xhat, gain, gacc):
    by_gain = jnp.sum(dv * xhat, axis=0, keepdims=True)
    by_bias = jnp.sum(dv, axis=0, keepdims=True)
    st[f : f + 1, lanes] = by_bias * gain
    st[FPB + f : FPB + f + 1, lanes] = by_gain * gain
    gacc[0:1, lanes] += by_gain
    gacc[1:2, lanes] += by_bias


def back_norm(st, size):
    sums = group_sum(st[...], size) * (1.0 / (PIX * size))
    return sums[0:FPB], sums[FPB : 2 * FPB]


def act_back(acc, st, xh, rs, gb, gacc, out):
    live = live_rows()
    for f, rows, lanes in units(MID):
        xhat = xh[rows, lanes].astype(f32)
        v = xhat * gb.gain(lanes) + gb.bias(lanes)
        s = sigmoid(v)
        dv = jnp.where(live, acc[rows, lanes] * (s + v * s * (1.0 - s)), 0.0)
        acc[rows, lanes] = dv
        back_sums(st, f, lanes, dv, xhat, gb.gain(lanes), gacc)
    m1, m2 = back_norm(st, MID // GROUPS)
    for f, rows, lanes in units(MID):
        xhat = xh[rows, lanes].astype(f32)
        da = rs[f : f + 1, lanes] * (
            acc[rows, lanes] * gb.gain(lanes) - m1[f : f + 1, lanes] - xhat * m2[f : f + 1, lanes]
        )
        out[rows, lanes] = jnp.where(live, da, 0.0).astype(bf16)


def tail_back_kernel(shard, layer, last, pos, d, x, xh3, rs3, xh2, rs2, gains, *rest):
    gb3, gb2 = Norm(gains, layer, 2), Norm(gains, layer, 1)
    n = len(shard.arrays)
    refs, (r, da3, da2, gacc3, gacc2, buf, sems, acc, st, acc2, st2) = rest[:n], rest[n:]

    @first_step
    def _():
        load_rows(shard, refs, pos, buf, sems)
        st[...] = jnp.zeros_like(st)
        st2[...] = jnp.zeros_like(st2)
        gacc3[...] = jnp.zeros_like(gacc3)
        gacc2[...] = jnp.zeros_like(gacc2)

    live = live_rows()
    for f, rows, lanes in units(C):
        xhat = xh3[rows, lanes].astype(f32)
        v = x[rows, lanes].astype(f32) + (xhat * gb3.gain(lanes) + gb3.bias(lanes))
        s = sigmoid(v)
        grad = d[f : f + 1, lanes] if last else d[rows, lanes].astype(f32)
        dv = jnp.where(live, grad * (s + v * s * (1.0 - s)), 0.0)
        acc[rows, lanes] = dv
        r[rows, lanes] = dv.astype(bf16)
        back_sums(st, f, lanes, dv, xhat, gb3.gain(lanes), gacc3)
    m1, m2 = back_norm(st, C // GROUPS)
    for f, rows, lanes in units(C):
        xhat = xh3[rows, lanes].astype(f32)
        da = rs3[f : f + 1, lanes] * (
            acc[rows, lanes] * gb3.gain(lanes) - m1[f : f + 1, lanes] - xhat * m2[f : f + 1, lanes]
        )
        da3[rows, lanes] = jnp.where(live, da, 0.0).astype(bf16)
    for j in range(MID // 256):
        lanes = slice(j * 256, (j + 1) * 256)
        acc2[:, lanes] = jnp.dot(da3[...], buf[:, lanes], preferred_element_type=f32)
    act_back(acc2, st2, xh2, rs2, gb2, gacc2, da2)


def conv_back_kernel(shard, shard_one, layer, pos, da2, masks, xh1, rs1, gains, *rest):
    gb1 = Norm(gains, layer, 0)
    n = len(shard.arrays)
    refs, rest = rest[:n], rest[n:]
    if shard_one is not None:
        n = len(shard_one.arrays)
        refs_one, (r, da1, gacc1, d, buf, sems, taps, acc, st, buf_one, sems_one) = rest[:n], rest[n:]
    else:
        da1, gacc1, buf, sems, taps, acc, st = rest

    @first_step
    def _():
        load_rows(shard, refs, pos, buf, sems)
        if shard_one is not None:
            load_rows(shard_one, refs_one, pos, buf_one, sems_one)
        st[...] = jnp.zeros_like(st)
        gacc1[...] = jnp.zeros_like(gacc1)

    spread_taps(da2, masks, taps)
    for j in range(MID // 256):
        total = None
        for k in range(9):
            part = lax.dot_general(
                taps[:, (8 - k) * MID : (9 - k) * MID],
                buf[k * MID + j * 256 : k * MID + (j + 1) * 256, :],
                (((1,), (1,)), ((), ())),
                preferred_element_type=f32,
            )
            total = part if total is None else total + part
        acc[:, j * 256 : (j + 1) * 256] = total
    act_back(acc, st, xh1, rs1, gb1, gacc1, da1)
    if shard_one is not None:
        for j in range(C // 256):
            lanes = slice(j * 256, (j + 1) * 256)
            a = lax.dot_general(
                da1[...], buf_one[lanes, :], (((1,), (1,)), ((), ())), preferred_element_type=f32
            )
            d[:, lanes] = (r[:, lanes].astype(f32) + a).astype(bf16)


def rows_spec(width):
    return pl.BlockSpec((BROWS, width), lambda i: (i, 0))


def eight_spec(width):
    return pl.BlockSpec((8, width), lambda i: (i, 0))


def gains_spec():
    return whole_spec(2 * BLOCKS, 2 * MID + C)


def whole_spec(rows, width):
    return pl.BlockSpec((rows, width), lambda i: (0, 0))


HBM = pl.BlockSpec(memory_space=pltpu.HBM)
ANY = pl.BlockSpec(memory_space=pl.ANY)
SMEM = pl.BlockSpec(memory_space=pltpu.SMEM)


def kept_sds(rows, width, dtype):
    return pltpu.HBM((rows, width), dtype)


def sds(rows, width, dtype):
    return jax.ShapeDtypeStruct((rows, width), dtype)


def call(kernel, name, rows, in_specs, outs, scratch, limit=48):
    return pl.pallas_call(
        kernel,
        name=name,
        grid=(rows // BROWS,),
        in_specs=in_specs,
        out_specs=[spec for _, spec in outs],
        out_shape=[shape for shape, _ in outs],
        scratch_shapes=scratch,
        cost_estimate=pl.CostEstimate(flops=1024, bytes_accessed=1024, transcendentals=0),
        compiler_params=pltpu.CompilerParams(
            vmem_limit_bytes=limit * MIB, dimension_semantics=("arbitrary",)
        ),
    )


def row_sems():
    return pltpu.SemaphoreType.DMA((14,))


def run_reduce(pos, x, shard, gains, layer, also=None):
    rows = x.shape[0]
    more = also.arrays if also else ()
    eights = rows // BROWS * 8
    return call(
        functools.partial(reduce_kernel, shard, also, layer),
        "reduce_norm",
        rows,
        [SMEM, rows_spec(C), gains_spec()] + [ANY] * (len(shard.arrays) + len(more)),
        [
            (sds(rows, MID, bf16), rows_spec(MID)),
            (kept_sds(rows, MID, bf16), rows_spec(MID)),
            (kept_sds(eights, MID, f32), eight_spec(MID)),
            (kept_sds(C, MID, bf16), HBM),
        ]
        + ([(kept_sds(9 * MID, MID, bf16), HBM)] if also else []),
        [
            pltpu.VMEM((C, MID), bf16),
            row_sems(),
            pltpu.VMEM((BROWS, MID), f32),
            pltpu.VMEM((8, MID), f32),
        ]
        + ([pltpu.VMEM((9 * MID, MID), bf16), row_sems()] if also else []),
    )(pos, x, gains, *shard.arrays, *more)


def run_conv(pos, h, masks, shard, gains, layer, also=None):
    rows = h.shape[0]
    more = also.arrays if also else ()
    eights = rows // BROWS * 8
    return call(
        functools.partial(conv_kernel, shard, also, layer),
        "conv_norm",
        rows,
        [SMEM, rows_spec(MID), whole_spec(9 * FROWS, 128), gains_spec()]
        + [ANY] * (len(shard.arrays) + len(more)),
        [
            (kept_sds(rows, 9 * MID, bf16), rows_spec(9 * MID)),
            (sds(rows, MID, bf16), rows_spec(MID)),
            (kept_sds(rows, MID, bf16), rows_spec(MID)),
            (kept_sds(eights, MID, f32), eight_spec(MID)),
            (kept_sds(9 * MID, MID, bf16), HBM),
        ]
        + ([(kept_sds(C, MID, bf16), HBM)] if also else []),
        [
            pltpu.VMEM((9 * MID, MID), bf16),
            row_sems(),
            pltpu.VMEM((BROWS, MID), f32),
            pltpu.VMEM((8, MID), f32),
        ]
        + ([pltpu.VMEM((C, MID), bf16), row_sems()] if also else []),
    )(pos, h, masks, gains, *shard.arrays, *more)


def run_expand(pos, u2, x, shard, gains, layer, last):
    rows = x.shape[0]
    eights = rows // BROWS * 8
    return call(
        functools.partial(expand_kernel, shard, layer, last),
        "expand_norm",
        rows,
        [SMEM, rows_spec(MID), rows_spec(C), gains_spec()] + [ANY] * len(shard.arrays),
        [
            (kept_sds(rows, C, bf16), rows_spec(C)),
            (kept_sds(eights, C, f32), eight_spec(C)),
            (sds(eights, C, f32), eight_spec(C)) if last else (sds(rows, C, bf16), rows_spec(C)),
            (kept_sds(C, MID, bf16), HBM),
        ],
        [
            pltpu.VMEM((C, MID), bf16),
            row_sems(),
            pltpu.VMEM((BROWS, C), f32),
            pltpu.VMEM((8, C), f32),
        ],
    )(pos, u2, x, gains, *shard.arrays)


def run_tail_back(pos, d, x, xh3, rs3, xh2, rs2, gains, shard, layer, last):
    rows = x.shape[0]
    return call(
        functools.partial(tail_back_kernel, shard, layer, last),
        "tail_back",
        rows,
        [
            SMEM,
            eight_spec(C) if last else rows_spec(C),
            rows_spec(C),
            rows_spec(C),
            eight_spec(C),
            rows_spec(MID),
            eight_spec(MID),
            gains_spec(),
        ]
        + [HBM] * len(shard.arrays),
        [
            (sds(rows, C, bf16), rows_spec(C)),
            (sds(rows, C, bf16), rows_spec(C)),
            (sds(rows, MID, bf16), rows_spec(MID)),
            (sds(8, C, f32), whole_spec(8, C)),
            (sds(8, MID, f32), whole_spec(8, MID)),
        ],
        [
            pltpu.VMEM((C, MID), bf16),
            row_sems(),
            pltpu.VMEM((BROWS, C), f32),
            pltpu.VMEM((8, C), f32),
            pltpu.VMEM((BROWS, MID), f32),
            pltpu.VMEM((8, MID), f32),
        ],
    )(pos, d, x, xh3, rs3, xh2, rs2, gains, *shard.arrays)


def run_conv_back(pos, da2, masks, xh1, rs1, gains, shard, shard_one, r, layer):
    rows = da2.shape[0]
    more = shard_one is not None
    extra = shard_one.arrays if more else ()
    return call(
        functools.partial(conv_back_kernel, shard, shard_one, layer),
        "conv_back",
        rows,
        [
            SMEM,
            rows_spec(MID),
            whole_spec(9 * FROWS, 128),
            rows_spec(MID),
            eight_spec(MID),
            gains_spec(),
        ]
        + [HBM] * (len(shard.arrays) + len(extra))
        + ([rows_spec(C)] if more else []),
        [
            (sds(rows, MID, bf16), rows_spec(MID)),
            (sds(8, MID, f32), whole_spec(8, MID)),
        ]
        + ([(sds(rows, C, bf16), rows_spec(C))] if more else []),
        [
            pltpu.VMEM((9 * MID, MID), bf16),
            row_sems(),
            pltpu.VMEM((BROWS, 9 * MID), bf16),
            pltpu.VMEM((BROWS, MID), f32),
            pltpu.VMEM((8, MID), f32),
        ]
        + ([pltpu.VMEM((C, MID), bf16), row_sems()] if more else []),
        28,
    )(pos, da2, masks, xh1, rs1, gains, *shard.arrays, *extra, *([r] if more else []))


def head_in_kernel(width, pos, feats, head, rows_out, logits, meta_out, select_out):
    everyone, slots = feats.shape[0], rows_out.shape[0]
    meta = feats[:, width : width + 128]
    match = meta[:, 2:3].astype(f32) == pos[2].astype(f32)
    ones = jnp.where(match, 1.0, 0.0)
    row = lax.broadcasted_iota(jnp.int32, (everyone, everyone), 0)
    col = lax.broadcasted_iota(jnp.int32, (everyone, everyone), 1)
    earlier = jnp.where(col < row, 1.0, 0.0).astype(bf16)
    place = jnp.dot(
        earlier,
        jnp.broadcast_to(ones, (everyone, 128)).astype(bf16),
        preferred_element_type=f32,
    )[:, 0:1]
    slot = lax.broadcasted_iota(jnp.int32, (everyone, slots), 1).astype(f32)
    select = jnp.where((slot == place) & match, 1.0, 0.0).astype(bf16)
    select_out[...] = select
    turn = (((0,), (0,)), ((), ()))
    rows = lax.dot_general(select, feats[:, :width], turn, preferred_element_type=f32).astype(bf16)
    rows_out[...] = rows
    meta_out[...] = lax.dot_general(select, meta, turn, preferred_element_type=f32)
    logits[...] = jnp.dot(rows, head[...], preferred_element_type=f32)


def head_loss_kernel(logits, meta, head, select, grad_out, back, loss, probs):
    count = logits.shape[0]
    lane = lax.broadcasted_iota(jnp.int32, (count, 128), 1)
    spot = lane & (SEG - 1)
    level = value_max * (spot.astype(f32) * (2.0 / (ATOMS - 1)) - 1.0)
    values = jnp.zeros((count, 128), f32)
    columns = []
    for a in range(ACTIONS):
        chunk = slice(a // 2 * 128, a // 2 * 128 + 128)
        inside = (lane >= (a % 2) * SEG) & (lane < (a % 2) * SEG + ATOMS)
        v = logits[:, chunk]
        top = jnp.max(jnp.where(inside, v, -3.0e38), axis=1, keepdims=True)
        e = jnp.where(inside, jnp.exp(jnp.minimum(v - top, 0.0)), 0.0)
        p = e / jnp.sum(e, axis=1, keepdims=True)
        q = jnp.sum(p * level, axis=1, keepdims=True)
        columns.append(q)
        values = jnp.where(lane == a, q, values)
        if a % 2 == 0:
            probs[:, chunk] = p
        else:
            probs[:, chunk] += p
    target, weight, action = meta[:, 0:1], meta[:, 1:2], meta[:, 3:4]
    real = lane < ACTIONS
    hot = (lane.astype(f32) == action).astype(f32)
    chosen = jnp.sum(values * hot, axis=1, keepdims=True)
    top = jnp.max(jnp.where(real, values, -3.0e38), axis=1, keepdims=True)
    e = jnp.where(real, jnp.exp(jnp.minimum(values - top, 0.0)), 0.0)
    total = jnp.sum(e, axis=1, keepdims=True)
    soft_top = top + jnp.log(total)
    row_loss = weight * ((chosen - target) * (chosen - target) + cql_alpha * (soft_top - chosen))
    loss[...] = jnp.zeros(loss.shape, f32) + jnp.sum(row_loss, axis=0, keepdims=True)
    slope = weight * (2.0 * (chosen - target) * hot + cql_alpha * (e / total - hot))
    for j in range(ACTIONS // 2):
        chunk = slice(j * 128, j * 128 + 128)
        low = lane < SEG
        q = jnp.where(low, columns[2 * j], columns[2 * j + 1])
        s = jnp.where(low, slope[:, 2 * j : 2 * j + 1], slope[:, 2 * j + 1 : 2 * j + 2])
        grad_out[:, chunk] = (s * probs[:, chunk] * (level - q)).astype(bf16)
    feat = lax.dot_general(
        grad_out[...], head[...], (((1,), (1,)), ((), ())), preferred_element_type=f32
    ).astype(bf16)
    back[...] = jnp.dot(select[...], feat, preferred_element_type=f32).astype(bf16)


def plain_call(kernel, name, outs, scratch, limit=48):
    return pl.pallas_call(
        kernel,
        name=name,
        out_shape=outs,
        scratch_shapes=scratch,
        compiler_params=pltpu.CompilerParams(vmem_limit_bytes=limit * MIB),
    )


def adam_step(weight, first, second, grad_in, rate, decay):
    first_new = decay_moment * first + (1.0 - decay_moment) * grad_in
    second_new = beta_second * second + (1.0 - beta_second) * grad_in * grad_in
    normed = (
        first_new
        / (1.0 - decay_moment**STEP)
        / (jnp.sqrt(second_new / (1.0 - beta_second**STEP)) + adam_eps)
    )
    return (weight - rate * (normed + decay * weight), first_new, second_new)


def heads_kernel(factor, weight, first, second, grad, *outs):
    values = adam_step(
        weight[...], first[...], second[...], factor[0] * grad[...], rate_head, decay_head
    )
    for out, value in zip(outs, values, strict=True):
        out[...] = value


def heads_step(factor, arrays):
    width = arrays[0].shape[2]
    spec = pl.BlockSpec((HOUT // 6, 1, width), lambda i: (i, 0, 0))
    return pl.pallas_call(
        heads_kernel,
        name="heads",
        grid=(6,),
        in_specs=[SMEM] + [spec] * 4,
        out_specs=[spec] * 3,
        out_shape=[jax.ShapeDtypeStruct((HOUT, 1, width), f32)] * 3,
        compiler_params=pltpu.CompilerParams(vmem_limit_bytes=63 * MIB),
    )(factor.reshape(1), *arrays)


def gram(a, b):
    return jnp.einsum("ri,rj->ij", a, b, preferred_element_type=f32)


def weight_grad(a, b):
    return jnp.einsum("ri,rj->ij", a, b, preferred_element_type=f32).astype(bf16)


TURN = (((0,), (0,)), ((), ()))


def turned_dot(a, b):
    return lax.dot_general(a, b, TURN, preferred_element_type=f32)


def pack_to(out_a, out_b, slot, core, upper, lower):
    row = lax.broadcasted_iota(jnp.int32, (HALF, MID), 0) + core * HALF
    col = lax.broadcasted_iota(jnp.int32, (HALF, MID), 1)
    body = jnp.where(row < col, upper, lower).astype(bf16)
    diag = jnp.sum(jnp.where(row == col, upper, 0.0), axis=0, keepdims=True)
    out_a[slot] = body[:PATH]
    out_b[slot, : HALF - PATH] = body[PATH:]
    out_b[slot, HALF - PATH :] = jnp.broadcast_to(diag, (PACK - HALF, MID)).astype(bf16)


def rows_of(ref, k):
    n = ref.shape[0] // 4 if k < 4 else ref.shape[0] // 2
    return ref.at[pl.ds((k if k < 4 else k - 4) * n, n)], n


def core_columns(core):
    return pl.ds(pl.multiple_of(core * HALF, HALF), HALF)


def old_gram_kernel(pos, pair, spatial, out_a, out_b, buf, low, sems):
    core = pos[1]
    mine = core_columns(core)
    copies, spans, at = [], [], 0
    for k in range(6):
        src, n = rows_of(pair if k < 4 else spatial, k)
        spans.append(slice(at, at + n))
        copies.append(pltpu.make_async_copy(src, buf.at[pl.ds(at, n)], sems.at[k]))
        at += n
    for copy in copies:
        copy.start()
    for k in range(6):
        copies[k].wait()
        low[spans[k]] = buf[spans[k]].astype(bf16)
    for p in range(3):
        upper, lower = (turned_dot(low[spans[k], mine], low[spans[k]]) for k in (2 * p, 2 * p + 1))
        pack_to(out_a, out_b, p, core, upper, lower)


def cross_gram_kernel(shares, pos, pair, spatial, *rest):
    refs, (out_a, out_b, full, buf, share, low, sems) = rest[:-7], rest[-7:]
    core = pos[1]
    mine = core_columns(core)
    copies, spans, at, used = [], [], 0, 0
    for s, (k, got) in enumerate(shares.items()):
        src, n = rows_of(pair if k < 4 else spatial, k)
        spans.append(slice(at, at + n))
        group = [pltpu.make_async_copy(src, buf.at[pl.ds(at, n)], sems.at[5 * s])]
        here = refs[used : used + len(got.arrays)]
        used += len(got.arrays)
        group += got.copies(here, pos, share, at, sems, 5 * s + 1)
        copies.append(group)
        at += n
    for group in copies:
        for copy in group:
            copy.start()
    for s, span in enumerate(spans):
        for copy in copies[s]:
            copy.wait()
        if s == len(spans) - 1:
            export = pltpu.make_async_copy(share, full, sems.at[5 * len(spans)])
            export.start()
        low[span] = buf[span].astype(bf16)
        upper = turned_dot(low[span, mine], share[span]) + turned_dot(share[span, mine], low[span])
        pack_to(out_a, out_b, s, core, upper, turned_dot(share[span, mine], share[span]))
    export.wait()


def gram_call(kernel, name, pos, moms, arrays, rows, count, scratch, sems, outs=()):
    return pl.pallas_call(
        kernel,
        name=name,
        in_specs=[SMEM, HBM, HBM] + [ANY] * len(arrays),
        out_specs=[pl.BlockSpec(memory_space=pltpu.VMEM)] * 2 + [HBM] * len(outs),
        out_shape=[jax.ShapeDtypeStruct((count, PATH, MID), bf16)] * 2 + list(outs),
        scratch_shapes=[pltpu.VMEM((rows, MID), f32)]
        + [pltpu.VMEM((rows, MID), bf16)] * scratch
        + [pltpu.SemaphoreType.DMA((sems,))],
        cost_estimate=pl.CostEstimate(flops=1024, bytes_accessed=1024, transcendentals=0),
        compiler_params=pltpu.CompilerParams(vmem_limit_bytes=28 * MIB),
    )(pos, *moms, *arrays)


def old_grams(pos, moms):
    rows = moms[0].shape[0] + moms[1].shape[0]
    return gram_call(old_gram_kernel, "old_gram", pos, moms, [], rows, 3, 1, 6)


def cross_grams(pos, moms, shares):
    rows = sum(moms[0].shape[0] // 4 if k < 4 else moms[1].shape[0] // 2 for k in shares)
    return gram_call(
        functools.partial(cross_gram_kernel, shares),
        "cross_gram",
        pos,
        moms,
        [v for share in shares.values() for v in share.arrays],
        rows,
        len(shares),
        2,
        5 * len(shares) + 1,
        [kept_sds(rows, MID, bf16)],
    )


def newton_kernel(groups, pos, facts, *rest):
    counts, order = tuple(len(g) for g in groups), [k for g in groups for k in g]
    n = 4 * (1 + len(counts))
    packs, rest = rest[:n], rest[n:]
    weights, moms, rest = rest[0:2], rest[2:4], rest[4:]
    shares, rest = rest[: len(groups)], rest[len(groups) :]
    news, moments, report, rest = rest[0:2], rest[2:4], rest[4], rest[5:]
    olds, crosses, w_buf, m_buf, g_buf, poly, sems, big_sems, share_sems, out_sems = rest
    pair_rows, rows = weights[0].shape[0], w_buf.shape[0]
    core = pos[1]
    spans, at = [], 0
    for k in range(6):
        count = pair_rows // 4 if k < 4 else (rows - pair_rows) // 2
        spans.append((at, count))
        at += count

    small = []
    at = 0
    for q, count in enumerate((3,) + counts):
        buffer = olds if q == 0 else crosses
        for j in range(4):
            side = core if j < 2 else 1 - core
            small.append(
                pltpu.make_async_copy(
                    packs[4 * q + j],
                    buffer.at[side, pl.ds(at, count), pl.ds(j % 2 * PATH, PATH)],
                    sems.at[4 * q + j],
                )
            )
        at = 0 if q == 0 else at + count
    big = []
    for q, (src, dst) in enumerate(((weights, w_buf), (moms, m_buf))):
        big.append(pltpu.make_async_copy(src[0], dst.at[pl.ds(0, pair_rows)], big_sems.at[2 * q]))
        big.append(
            pltpu.make_async_copy(
                src[1], dst.at[pl.ds(pair_rows, rows - pair_rows)], big_sems.at[2 * q + 1]
            )
        )
    for ids, share in zip(groups, shares, strict=True):
        at = 0
        for k in ids:
            start, n = spans[k]
            big.append(
                pltpu.make_async_copy(
                    share.at[pl.ds(at, n)], g_buf.at[pl.ds(start, n)], share_sems.at[k]
                )
            )
            at += n
    for copy in small:
        copy.start()
    for copy in small:
        copy.wait()
    for copy in big:
        copy.start()

    row = lax.broadcasted_iota(jnp.int32, (MID, MID), 0)
    col = lax.broadcasted_iota(jnp.int32, (MID, MID), 1)
    above, on = row < col, row == col

    def total(v):
        return jnp.sum(jnp.sum(v, axis=0, keepdims=True), axis=1, keepdims=True)

    def pack_of(buffer, p):
        body = jnp.concatenate([buffer[0, p, 0:HALF], buffer[1, p, 0:HALF]], axis=0).astype(f32)
        diag = (
            buffer[0, p, HALF : HALF + 16].astype(f32) + buffer[1, p, HALF : HALF + 16].astype(f32)
        )
        return body, diag[0:1]

    def diag_of(body):
        return jnp.sum(jnp.where(on, body, 0.0), axis=0, keepdims=True)

    squares = jnp.zeros((1, 1), f32)
    for p in range(6):
        squares = squares + total(jnp.where(on, pack_of(crosses, p)[0], 0.0))
    weight_total = jnp.zeros((1, 1), f32) + facts[1]
    grad_norm = jnp.sqrt(squares + facts[0]) / weight_total
    factor = jnp.minimum(1.0, clip_limit / grad_norm) / weight_total
    lane = lax.broadcasted_iota(jnp.int32, report.shape, 1)
    report[...] = jnp.where(lane == 0, grad_norm, factor)

    def low_dot(a, b):
        return jnp.dot(a.astype(bf16), b.astype(bf16), preferred_element_type=f32)

    scales = []
    for k in range(6):
        old, old_diag = pack_of(olds, k // 2)
        body, cross_diag = pack_of(crosses, order.index(k))
        quarter, half_factor = decay_moment * decay_moment, decay_moment * factor
        if k % 2 == 0:
            part = jnp.where(above, quarter * old + half_factor * body, (factor * factor) * body)
        else:
            old_diag = diag_of(old)
            part = jnp.where(above, half_factor * body, quarter * old + (factor * factor) * body)
        diag = quarter * old_diag + half_factor * cross_diag + (factor * factor) * diag_of(body)
        part = jnp.where(on, 0.5 * diag, part)
        g = part + part.T
        frob = jnp.sqrt(jnp.maximum(jnp.sum(diag, axis=1, keepdims=True), 0.0))
        scale = 1.0 / (frob + 1e-07)
        scales.append(scale)
        g0 = g * (scale * scale)
        e1 = coef_b * g0 + coef_c * low_dot(g0, g0)
        h = coef_a * g0 + low_dot(g0, e1)
        g1 = coef_a * h + low_dot(h, e1)
        e2 = coef_b * g1 + coef_c * low_dot(g1, g1)
        poly[k] = (coef_a * (e1 + e2) + low_dot(e1, e2)).astype(bf16)

    for copy in big:
        copy.wait()
    outs = []
    for k in range(6):
        start, count = spans[k]
        gain = 0.2 * math.sqrt(C if k < 4 else 9 * MID)
        chunk = 256 if count % 256 == 0 else 128 if count % 128 == 0 else 32
        for j in range(count // chunk):
            here = slice(start + j * chunk, start + (j + 1) * chunk)
            moment = decay_moment * m_buf[here] + factor * g_buf[here].astype(f32)
            m_buf[here] = moment
            current = moment * scales[k]
            ortho = (coef_a * coef_a) * current + jnp.dot(
                current.astype(bf16), poly[k], preferred_element_type=f32
            )
            w_buf[here] = (1.0 - rate_muon * decay_muon) * w_buf[here] - (rate_muon * gain) * ortho
        which, base = (0, 0) if k < 4 else (1, pair_rows)
        for q, (buf, dst) in enumerate(((w_buf, news), (m_buf, moments))):
            copy = pltpu.make_async_copy(
                buf.at[pl.ds(start, count)],
                dst[which].at[pl.ds(start - base, count)],
                out_sems.at[2 * k + q],
            )
            copy.start()
            outs.append(copy)
    for copy in outs:
        copy.wait()


def newton(pos, facts, olds, groups, crosses, weights, moms, shares):
    rows = weights[0].shape[0] + weights[1].shape[0]
    packs = [v for group in (olds, *crosses) for v in group]
    return pl.pallas_call(
        functools.partial(newton_kernel, groups),
        name="newton",
        in_specs=[SMEM, SMEM]
        + [HBM] * len(packs)
        + [HBM] * (4 + len(shares)),
        out_specs=[HBM] * 4 + [pl.BlockSpec(memory_space=pltpu.VMEM)],
        out_shape=[jax.ShapeDtypeStruct(w.shape, f32) for w in weights] * 2 + [sds(8, 128, f32)],
        scratch_shapes=[
            pltpu.VMEM((2, 3, PACK, MID), bf16),
            pltpu.VMEM((2, 6, PACK, MID), bf16),
            pltpu.VMEM((rows, MID), f32),
            pltpu.VMEM((rows, MID), f32),
            pltpu.VMEM((rows, MID), bf16),
            pltpu.VMEM((6, MID, MID), bf16),
            pltpu.SemaphoreType.DMA((len(packs),)),
            pltpu.SemaphoreType.DMA((4,)),
            pltpu.SemaphoreType.DMA((6,)),
            pltpu.SemaphoreType.DMA((12,)),
        ],
        compiler_params=pltpu.CompilerParams(vmem_limit_bytes=63 * MIB),
    )(pos, facts, *packs, *weights, *moms, *shares)


def local(
    net,
    frames,
    game_ids,
    actions,
    groups,
    targets,
    w_pair,
    w_spatial,
    mom_pair,
    mom_spatial,
    head_table,
    head_first,
    head_second,
    norm_params,
    norm_first,
    norm_second,
):
    dp_idx, ns_idx = lax.axis_index("dp"), lax.axis_index("ns")
    pos = jnp.stack(
        [ns_idx, bit_of(dp_idx, 0), dp_idx, bit_of(ns_idx, 0), bit_of(ns_idx, 1), bit_of(dp_idx, 1)]
    ).astype(jnp.int32)
    dev_rows = frames.shape[1]
    samples = MB * dev_rows
    rows = samples * FROWS
    devices = net.dp * net.ns
    everyone = devices * samples
    slots = MB * net.dp * (2 * net.ns * dev_rows // net.dp)
    col_width = C // net.ns

    get_a = gather_direct(net, w_pair[0, 0])
    get_a.step()

    masks = jnp.asarray(tap_masks())
    stream = jnp.pad(
        frames.reshape(samples, PIX, C), ((0, 0), (0, FROWS - PIX), (0, 0))
    ).reshape(rows, C)
    gains = norm_params.reshape(2 * BLOCKS, 2 * MID + C)
    x0 = stream
    got = get_a.step()
    get_b = gather_two(net, [w_spatial[0], w_pair[0, 1]], *got)
    sent = get_b.step()
    get_a.step()
    h, xh1, rs1, one = run_reduce(pos, after(x0, *sent), get_a.value[0], gains, 0)
    sent = get_b.step(h)

    out_col = jnp.arange(HOUT, dtype=jnp.int32)
    widen = (
        (out_col // ATOMS * SEG + out_col % ATOMS)[:, None] == jnp.arange(HPAD, dtype=jnp.int32)
    ).astype(bf16)
    head = jnp.dot(after(head_table, *sent)[0].astype(bf16), widen, preferred_element_type=f32).astype(bf16)

    moms = [mom_pair.reshape(-1, MID), mom_spatial.reshape(-1, MID)]
    old = old_grams(after(pos, *sent), moms)

    get_c = gather_two(net, [w_pair[1, 0], w_spatial[1]], *sent)
    sent = get_c.step()
    h = after(h, *old, head)
    get_b.step(*sent)
    get_b.step()
    kept = [(x0, xh1, rs1)]
    ones, mids, lasts = [one], [], []
    taps, u2, xh2, rs2, mid, last = run_conv(
        pos, h, masks, get_b.value[0], gains, 0, get_b.value[1]
    )
    sent = get_c.step(u2)
    get_d = gather_two(net, [w_pair[1, 1]], *sent)
    sent = get_d.step()
    xh3, rs3, x1, _ = run_expand(
        pos, after(u2, *sent), x0, Shards((last,), None), gains, 0, False
    )
    kept[0] = kept[0] + (taps, u2, xh2, rs2, xh3, rs3)
    mids.append(mid)
    lasts.append(last)
    get_c.step(x1)
    get_c.step()
    sent = get_d.step(x1)
    h, xh1, rs1, one, mid = run_reduce(
        pos, after(x1, *sent), get_c.value[0], gains, 1, get_c.value[1]
    )
    taps, u2, xh2, rs2, _ = run_conv(pos, h, masks, Shards((mid,), None), gains, 1)
    get_d.step(h)
    get_d.step()
    xh3, rs3, stream, last = run_expand(pos, u2, x1, get_d.value[0], gains, 1, True)
    kept.append((x1, xh1, rs1, taps, u2, xh2, rs2, xh3, rs3))
    ones, mids, lasts = [
        [Shards((v,), None) for v in pair]
        for pair in ((ones[0], one), (mids[0], mid), (lasts[0], last))
    ]
    pooled = stream.reshape(-1, 8, C)[:, :FPB].reshape(samples, C).astype(bf16)

    meta = jnp.stack(
        [
            targets.astype(f32),
            0.25 + 0.75 * groups.astype(f32),
            game_ids[:, :, 0].astype(f32),
            actions.astype(f32),
        ],
        axis=2,
    ).reshape(samples, 4)
    meta = jnp.pad(meta, ((0, 0), (0, 124))).astype(bf16)
    sent = jnp.swapaxes(pooled.reshape(samples, net.ns, col_width), 0, 1)
    sent = jnp.concatenate([sent, jnp.broadcast_to(meta[None], (net.ns, samples, 128))], axis=2)
    sent = jnp.broadcast_to(sent[None], (net.dp,) + sent.shape)
    feats = lax.all_to_all(
        sent.reshape(devices, samples, col_width + 128), ("dp", "ns"), 0, 0, tiled=True
    ).reshape(everyone, col_width + 128)
    feat_rows, logits, meta_slots, select = pl.pallas_call(
        functools.partial(head_in_kernel, col_width),
        name="head_in",
        in_specs=[SMEM] + [pl.BlockSpec(memory_space=pltpu.VMEM)] * 2,
        out_shape=[
            sds(slots, col_width, bf16),
            sds(slots, HPAD, f32),
            sds(slots, 128, f32),
            sds(everyone, slots, bf16),
        ],
        compiler_params=pltpu.CompilerParams(vmem_limit_bytes=48 * MIB),
    )(pos, feats, head)
    weight_total = jnp.sum(feats[:, col_width + 1].astype(f32))
    logits = net.add_all(logits, ("ns",))
    grad_low, back, loss = plain_call(
        head_loss_kernel,
        "head_loss",
        [sds(slots, HPAD, bf16), sds(everyone, col_width, bf16), sds(8, 128, f32)],
        [pltpu.VMEM((slots, HPAD), f32)],
    )(logits, meta_slots, head, select)
    returned = lax.all_to_all(
        back.reshape(devices, samples, col_width), ("dp", "ns"), 0, 0, tiled=True
    ).reshape(net.dp, net.ns, samples, col_width)
    grad_pooled = jnp.sum(returned.astype(f32), axis=0)
    grad_pooled = jnp.swapaxes(grad_pooled, 0, 1).reshape(samples // FPB, FPB, C) * (1.0 / PIX)
    grad_stream = jnp.pad(grad_pooled, ((0, 0), (0, 8 - FPB), (0, 0))).reshape(-1, C)

    def tail_back(layer, grad):
        x, xh1, rs1, taps, u2, xh2, rs2, xh3, rs3 = kept[layer]
        return run_tail_back(
            pos, grad, x, xh3, rs3, xh2, rs2, gains, lasts[layer], layer, layer == BLOCKS - 1
        )

    def conv_back(layer, da2, r):
        xh1, rs1 = kept[layer][1:3]
        one = ones[layer] if layer > 0 else None
        return run_conv_back(pos, da2, masks, xh1, rs1, gains, mids[layer], one, r, layer)

    shares, grams = {}, []

    def reduce_and_gram(ids, grads):
        got = yield from reduce_steps(net, pos, grads)
        got = dict(zip(ids, got, strict=True))
        *packs, share = cross_grams(pos, moms, got)
        shares[tuple(ids)] = share
        grams.append((tuple(ids), (yield from gram_steps(net, packs))))

    r, da3, da2, gacc3, gacc2 = tail_back(1, grad_stream)
    sum_a = Run(reduce_and_gram((5,), [weight_grad(kept[1][3], da2)]))
    sum_o = Run(gram_steps(net, old))
    sent = sum_a.step()
    da1, gacc1, grad_stream = conv_back(1, after(da2, *sent), r)
    gains_1 = jnp.concatenate([gacc1[:2], gacc2[:2], gacc3[:2]], axis=1)
    sent = sum_a.step(da1)
    grad_one, grad_last = weight_grad(x1, after(da1, *sent)), weight_grad(da3, kept[1][4])
    sum_b = Run(reduce_and_gram((2, 3), [grad_one, grad_last]))
    sent = sent + sum_b.step()
    r, da3, da2, gacc3, gacc2 = tail_back(0, after(grad_stream, *sent))
    sent = sum_b.step(da2) + sum_a.step(da2)
    sum_c = Run(reduce_and_gram((4,), [weight_grad(after(kept[0][3], *sent), da2)]))
    sent = sum_c.step() + sum_o.step()
    da1, gacc1 = conv_back(0, after(da2, *sent), None)

    grad_low = lax.dot_general(
        widen, after(grad_low, da1), (((1,), (1,)), ((), ())), preferred_element_type=f32
    ).astype(bf16)
    head_grad = jnp.dot(grad_low, feat_rows, preferred_element_type=f32)
    head_sq = jnp.sum(jnp.square(head_grad))
    head_grad = head_grad.reshape(HOUT, 1, col_width)
    loss_part = jnp.where(ns_idx == 0, loss[0, 0], 0.0)
    gains_0 = jnp.concatenate([gacc1[:2], gacc2[:2], gacc3[:2]], axis=1)
    small = jnp.stack([gains_0, gains_1]).reshape(-1, 1024)
    tail = jnp.zeros((16 - small.shape[0], 1024), f32)
    lane = jnp.arange(1024, dtype=jnp.int32)[None, :]
    tail = tail + jnp.where(lane == 0, loss_part, 0.0) + jnp.where(lane == 1, head_sq, 0.0)
    sum_s = Run(add_steps(net, jnp.concatenate([small, tail], axis=0)))

    sent = sum_c.step(da1) + sum_b.step(da1) + sum_a.step(da1)
    grad_one, grad_last = weight_grad(x0, after(da1, *sent)), weight_grad(after(da3, da1), kept[0][4])
    sum_d = Run(reduce_and_gram((0, 1), [grad_one, grad_last]))

    runs = (sum_d, sum_c, sum_b, sum_a, sum_s, sum_o)
    deps = (grad_one, grad_last)
    while not all(run.done for run in runs):
        sent = ()
        for run in runs:
            sent = sent + run.step(*deps)
        if sum_s.done:
            sent = sent + (sum_s.value,)
        deps = sent

    groups = tuple(ids for ids, _ in grams)
    gain_sum = sum_s.value[:12].reshape(BLOCKS, 2, 2 * MID + C)
    loss_sum, head_total = sum_s.value[12, 0], sum_s.value[12, 1]

    facts = jnp.stack([head_total + jnp.sum(jnp.square(gain_sum)), weight_total])
    pair_new, spatial_new, pair_moment, spatial_moment, report = newton(
        pos,
        facts,
        sum_o.value,
        groups,
        [got for _, got in grams],
        [w_pair.reshape(-1, MID), w_spatial.reshape(-1, MID)],
        moms,
        [shares[ids] for ids in groups],
    )
    grad_norm, factor = report[0, 0], report[0, 1]

    heads = heads_step(
        factor,
        [jnp.transpose(v, (2, 0, 1)) for v in (head_table, head_first, head_second)] + [head_grad],
    )
    heads = [jnp.transpose(v, (1, 2, 0)) for v in heads]
    norm_new, norm_first_new, norm_second_new = adam_step(
        norm_params, norm_first, norm_second, factor * gain_sum, rate_gain, 0.0
    )

    return (
        pair_new.reshape(w_pair.shape),
        spatial_new.reshape(w_spatial.shape),
        pair_moment.reshape(w_pair.shape),
        spatial_moment.reshape(w_spatial.shape),
        *heads,
        norm_new,
        norm_first_new,
        norm_second_new,
        grad_norm,
        loss_sum,
        weight_total,
    )


def solution(mesh):
    net = Net(mesh.shape["dp"], mesh.shape["ns"])
    samples = P(None, ("dp", "ns"))
    heads = P("dp", "ns", None)
    pairs, spatial = P(None, None, "ns", None), P(None, "ns", None)
    in_specs = (
        P(None, ("dp", "ns"), None, None),
        P(None, ("dp", "ns"), None),
        samples,
        samples,
        samples,
        pairs,
        spatial,
        pairs,
        spatial,
        heads,
        heads,
        heads,
        P(),
        P(),
        P(),
    )
    out_specs = (pairs, spatial, pairs, spatial, heads, heads, heads) + (P(),) * 6
    return jax.shard_map(
        functools.partial(local, net),
        mesh=mesh,
        in_specs=in_specs,
        out_specs=out_specs,
        check_vma=False,
    )
```

time: 893 us -> 536 us (0.60)
  other arithmetic: 137 us -> 18 us
  local copies, waits for them, and re-layouts: 155 us -> 56.2 us
  matrix products: 133 us -> 39.3 us
  waiting for transfers between devices: 215 us -> 128 us
  Pallas kernels: 142 us -> 191 us
  blocking collectives: 0 us -> 17.1 us
  starting transfers between devices: 90.6 us -> 76.1 us
    dot_general x33 -> x2, matrix products: 105 us -> 7.09 us  [the longest x1 4.26 us: local(): head_grad = jnp.dot(grad_low, feat_rows, preferred_element_type=f32)]
    ppermute x84 -> x107, waiting for transfers between devices: 207 us -> 117 us  [swap(): return lax.ppermute(value, ('dp', 'ns'), pairs)]
    unnamed x391 -> x216, local copies, waits for them, and re-layouts: 80.3 us -> 28.4 us
    pallas_call x11 -> x30, Pallas kernels: 140 us -> 189 us  [the longest x2 34.4 us: run_tail_back(): call(functools.partial(tail_back_kernel, shard, layer, last), 'tail_back'...]
    another operation x53 -> x8, other arithmetic: 36.5 us -> 1.33 us  [the longest x1 1.23 us: local(): jnp.stack([head_total + jnp.sum(jnp.square(gain_sum)), weight_total])]
    reduce_sum x10 -> x1, other arithmetic: 22.9 us -> 0.7 us  [local(): weight_total = jnp.sum(feats[:, col_width + 1].astype(f32))]
    add x23 -> x33, other arithmetic: 24.7 us -> 4.05 us  [the longest x20 3.42 us: gram_steps(): first, second = (first + after(got_a, *deps), second + after(got_b, *deps))]
    all_to_all x0 -> x1, blocking collectives: none -> 17.1 us  [local(): lax.all_to_all(sent.reshape(devices, samples, col_width + 128), ('dp', 'n...]
  transfers between devices with their start and end apart: 86 -> 108, of which waited for: 37 -> 29; matrix products, arithmetic and copies ran while one was open for 28% -> 10% of each run, Pallas kernels for 16% -> 23%
where the time goes in v2:
time: 536 us; the launch traced here: 531 us
  Pallas kernels  191 us (36%)
  waiting for transfers between devices  128 us (24%)
  starting transfers between devices  76.1 us (14%)
  local copies, waits for them, and re-layouts  56.2 us (10%)
  matrix products  39.3 us (7%)
  other arithmetic  18 us (3%)
  blocking collectives  17.1 us (3%)
    ppermute x107, waiting for transfers between devices, swap(): return lax.ppermute(value, ('dp', 'ns'), pairs)  117 us
    ppermute x107, starting transfers between devices, swap(): return lax.ppermute(value, ('dp', 'ns'), pairs)  72.7 us
    pallas_call x2, Pallas kernels, run_tail_back(): call(functools.partial(tail_back_kernel, shard, layer, last), 'tail_back'...  34.4 us
    dot_general x6, matrix products, weight_grad(): jnp.einsum('ri,rj->ij', a, b, preferred_element_type=f32).astype(bf16)  32.2 us
    unnamed x216, local copies, waits for them, and re-layouts  28.4 us
    pallas_call x2, Pallas kernels, run_conv(): call(functools.partial(conv_kernel, shard, also, layer), 'conv_norm', row...  27.1 us
    pallas_call x2, Pallas kernels, run_expand(): call(functools.partial(expand_kernel, shard, layer, last), 'expand_norm',...  26.1 us
    pallas_call x1, Pallas kernels, newton(): pl.pallas_call(functools.partial(newton_kernel, groups), name='newton', i...  22.9 us
  transfers between devices with their start and end apart: 108, of which 29 were waited for; matrix products, arithmetic and copies ran while one was open for 10% of the time, Pallas kernels for 23%

profile of v2, /device:TPU:0, one launch (start us, length us, event | category | flops | bytes accessed | tf_op | source)
XLA Modules:
  0.0 530.8 jit_solution(12833054187988022296)
XLA Ops:
  0.7 3.2 fusion.22
  4.6 2.9 collective-permute-start
  9.1 3.7 fusion.21
  12.8 2.5 dynamic-slice_bitcast_fusion.7
  17.3 3.9 collective-permute-done.1.rest_2_
  23.8 6.3 %copy.37 = bf16[2,4,121,2048]{3,2,1,0:T(8,128)(2,1)} copy(bf16[2,4,121,2048]{3,1,2,0:T(4,128)(2,1)} %param.16) | data formatting | bytes 7929856 | tf_op args[0]
  30.1 4.9 pad.13
  35.2 9.5 %reduce_norm.2 = (bf16[1024,512]{1,0:T(8,128)(2,1)S(1)}, bf16[1024,512]{1,0:T(8,128)(2,1)}, f32[32,512]{1,0:T(8,128)}, bf16[2048,512]{1,0:T(8,128)(2,1)}) custom-call(s32[6]{0:T(128)S(1)} %stack.60.pos, bf16[1024,2048]{1,0:T(8,128)(2,1)} %bitcast.158, f32[4,3072]{1,0:T(4,128)S(1)} %reshape.197.gains, bf16[512,512]{1,0:T(8,128)(2,1)S(1)} %bitcast.150, ...), custom_call_target="tpu_custom_call" | custom-call | flops 1024 | bytes 1024 | tf_op jit(solution)/shard_map/reduce_norm/pallas_call | solution.py:736
  50.0 7.2 %collective-permute-done.8.rest_3_.rest_12_ = bf16[416,512]{1,0:T(8,128)(2,1)S(1)} collective-permute-done((bf16[416,512]{1,0:T(8,128)(2,1)S(1)}, bf16[416,512]{1,0:T(8,128)(2,1)S(1)}, u32[]{:S(2)}, u32[]{:S(2)}) %collective-permute-start.8) | collective-permute-done | bytes 426016 | tf_op jit(solution)/shard_map/ppermute | solution.py:75
  60.2 3.1 old_gram.1
  64.7 2.8 fusion.2.head
  68.5 14.6 %conv_norm.2 = (bf16[1024,4608]{1,0:T(8,128)(2,1)}, bf16[1024,512]{1,0:T(8,128)(2,1)}, bf16[1024,512]{1,0:T(8,128)(2,1)}, f32[32,512]{1,0:T(8,128)}, bf16[4608,5...) custom-call(s32[6]{0:T(128)S(1)} %stack.60.pos, bf16[1024,512]{1,0:T(8,128)(2,1)} %copy-done.25, f32[1152,128]{1,0:T(8,128)S(1)} %copy-done.2, ...), custom_call_target="tpu_custom_call" | custom-call | flops 1024 | bytes 1024 | tf_op jit(solution)/shard_map/conv_norm/pallas_call | solution.py:762
  87.7 12.4 %expand_norm.2 = (bf16[1024,2048]{1,0:T(8,128)(2,1)}, f32[32,2048]{1,0:T(8,128)}, bf16[1024,2048]{1,0:T(8,128)(2,1)}, bf16[2048,512]{1,0:T(8,128)(2,1)}) custom-call(s32[6]{0:T(128)S(1)} %stack.60.pos, bf16[1024,512]{1,0:T(8,128)(2,1)S(1)} %copy-done.20, bf16[1024,2048]{1,0:T(8,128)(2,1)} %bitcast.159, f32[4,3072]{1,0:T(4,128)S(1)} %reshape.197.gains, ...), custom_call_target="tpu_custom_call" | custom-call | flops 1024 | bytes 1024 | tf_op jit(solution)/shard_map/expand_norm/pallas_call | solution.py:789
  102.0 7.0 %collective-permute-done.17.rest_2_ = bf16[256,512]{1,0:T(8,128)(2,1)} collective-permute-done((bf16[256,512]{1,0:T(8,128)(2,1)S(1)}, bf16[256,512]{1,0:T(8,128)(2,1)}, u32[]{:S(2)}, u32[]{:S(2)}) %collective-permute-start.17) | collective-permute-done | bytes 262176 | tf_op jit(solution)/shard_map/ppermute | solution.py:75
  112.5 12.1 %reduce_norm.3 = (bf16[1024,512]{1,0:T(8,128)(2,1)}, bf16[1024,512]{1,0:T(8,128)(2,1)}, f32[32,512]{1,0:T(8,128)}, bf16[2048,512]{1,0:T(8,128)(2,1)}, bf16[4608,512]{1,0:T(8,128)(2,1)}) custom-call(s32[6]{0:T(128)S(1)} %stack.60.pos, bf16[1024,2048]{1,0:T(8,128)(2,1)} %get-tuple-element.247.x, f32[4,3072]{1,0:T(4,128)S(1)} %reshape.197.gains, ...), custom_call_target="tpu_custom_call" | custom-call | flops 1024 | bytes 1024 | tf_op jit(solution)/shard_map/reduce_norm/pallas_call | solution.py:736
  126.9 12.4 %conv_norm.3 = (bf16[1024,4608]{1,0:T(8,128)(2,1)}, bf16[1024,512]{1,0:T(8,128)(2,1)S(1)}, bf16[1024,512]{1,0:T(8,128)(2,1)}, f32[32,512]{1,0:T(8,128)}, bf16[4608,512]{1,0:T(8,128)(2,1)}) custom-call(s32[6]{0:T(128)S(1)} %stack.60.pos, bf16[1024,512]{1,0:T(8,128)(2,1)S(1)} %copy-done.18, f32[1152,128]{1,0:T(8,128)S(1)} %copy-done.2, ...), custom_call_target="tpu_custom_call" | custom-call | flops 1024 | bytes 1024 | tf_op jit(solution)/shard_map/conv_norm/pallas_call | solution.py:762
  139.5 13.7 %expand_norm.3 = (bf16[1024,2048]{1,0:T(8,128)(2,1)}, f32[32,2048]{1,0:T(8,128)}, f32[32,2048]{1,0:T(8,128)S(1)}, bf16[2048,512]{1,0:T(8,128)(2,1)}) custom-call(s32[6]{0:T(128)S(1)} %stack.60.pos, bf16[1024,512]{1,0:T(8,128)(2,1)S(1)} %get-tuple-element.252.u2, bf16[1024,2048]{1,0:T(8,128)(2,1)} %get-tuple-element.247.x, f32[4,3072]{1,0:T(4,128)S(1)} %reshape.197.gains, ...), custom_call_target="tpu_custom_call" | custom-call | flops 1024 | bytes 1024 | tf_op jit(solution)/shard_map/expand_norm/pallas_call | solution.py:789
  153.3 17.1 %all_to_all.10 = bf16[32,8,640]{2,1,0:T(8,128)(2,1)S(1)} all-to-all(bf16[32,8,640]{2,1,0:T(8,128)(2,1)S(1)} %bitcast.172), channel_id=1, replica_groups=mesh['dp'=8,'ns'=4] {'dp','ns'}, dimensions={0} | all-to-all | bytes 655360 | tf_op jit(solution)/shard_map/all_to_all | solution.py:1374
  173.1 7.9 %collective-permute-done.30 = f32[64,1152]{1,0:T(8,128)S(1)} collective-permute-done((f32[64,1152]{1,0:T(8,128)S(1)}, f32[64,1152]{1,0:T(8,128)S(1)}, u32[]{:S(2)}, u32[]{:S(2)}) %collective-permute-start.30) | collective-permute-done | bytes 294944 | tf_op jit(solution)/shard_map/ppermute | solution.py:75
  182.7 7.0 %collective-permute-done.31 = f32[64,1152]{1,0:T(8,128)S(1)} collective-permute-done((f32[64,1152]{1,0:T(8,128)S(1)}, f32[64,1152]{1,0:T(8,128)S(1)}, u32[]{:S(2)}, u32[]{:S(2)}) %collective-permute-start.31) | collective-permute-done | bytes 294944 | tf_op jit(solution)/shard_map/ppermute | solution.py:75
  192.7 3.5 all-to-all-start.1
  196.1 10.9 %all-to-all-done.1 = bf16[32,8,512]{2,1,0:T(8,128)(2,1)} async-done(((bf16[32,8,512]{2,1,0:T(8,128)(2,1)}), bf16[32,8,512]{2,1,0:T(8,128)(2,1)}, u32[]{:S(2)}, u32[]{:S(2)}) %all-to-all-start.1) | async-done | bytes 262176 | tf_op jit(solution)/shard_map/all_to_all | solution.py:1397
  212.5 16.5 %tail_back.2 = (bf16[1024,2048]{1,0:T(8,128)(2,1)}, bf16[1024,2048]{1,0:T(8,128)(2,1)}, bf16[1024,512]{1,0:T(8,128)(2,1)S(1)}, f32[8,2048]{1,0:T(8,128)S(1)}, f32[8,512]{1,0:T(8,128)S(1)}) custom-call(s32[6]{0:T(128)S(1)} %stack.60.pos, f32[32,2048]{1,0:T(8,128)S(1)} %pad_bitcast_fusion.d, bf16[1024,2048]{1,0:T(8,128)(2,1)} %get-tuple-element.247.x, ...), custom_call_target="tpu_custom_call" | custom-call | flops 1024 | bytes 1024 | tf_op jit(solution)/shard_map/tail_back/pallas_call | solution.py:811
  229.0 9.2 %convolution_convert_fusion.1 = bf16[4608,512]{1,0:T(8,128)(2,1)S(1)} fusion(bf16[1024,4608]{1,0:T(8,128)(2,1)} %get-tuple-element.266, bf16[1024,512]{1,0:T(8,128)(2,1)S(1)} %get-tuple-element.267.da2), kind=kOutput, calls=%fused_computation.1 | convolution fusion | flops 4834197504 | bytes 15204352 | tf_op jit(solution)/shard_map/ri,rj->ij/dot_general | solution.py:994
  240.5 12.2 %conv_back.2 = (bf16[1024,512]{1,0:T(8,128)(2,1)S(1)}, f32[8,512]{1,0:T(8,128)S(1)}, bf16[1024,2048]{1,0:T(8,128)(2,1)S(1)}) custom-call(s32[6]{0:T(128)S(1)} %stack.60.pos, bf16[1024,512]{1,0:T(8,128)(2,1)S(1)} %get-tuple-element.267.da2, f32[1152,128]{1,0:T(8,128)S(1)} %copy-done.2, bf16[1024,512]{1,0:T(8,128)(2,1)S(1)} %copy-done.22, ...), custom_call_target="tpu_custom_call" | custom-call | flops 1024 | bytes 1024 | tf_op jit(solution)/shard_map/conv_back/pallas_call | solution.py:848
  252.7 6.1 %convolution_convert_fusion.4 = bf16[2048,512]{1,0:T(8,128)(2,1)S(1)} fusion(bf16[1024,2048]{1,0:T(8,128)(2,1)} %get-tuple-element.278, bf16[1024,512]{1,0:T(8,128)(2,1)S(1)} %copy-done.24), kind=kOutput, calls=%fused_computation.7 | convolution fusion | flops 2148532224 | bytes 7340032 | tf_op jit(solution)/shard_map/ri,rj->ij/dot_general | solution.py:994
  266.6 18.0 %tail_back.3 = (bf16[1024,2048]{1,0:T(8,128)(2,1)}, bf16[1024,2048]{1,0:T(8,128)(2,1)}, bf16[1024,512]{1,0:T(8,128)(2,1)S(1)}, f32[8,2048]{1,0:T(8,128)S(1)}, f32[8,512]{1,0:T(8,128)S(1)}) custom-call(s32[6]{0:T(128)S(1)} %stack.60.pos, bf16[1024,2048]{1,0:T(8,128)(2,1)} %copy-done.9, bf16[1024,2048]{1,0:T(8,128)(2,1)} %bitcast.160, ...), custom_call_target="tpu_custom_call" | custom-call | flops 1024 | bytes 1024 | tf_op jit(solution)/shard_map/tail_back/pallas_call | solution.py:811
  286.1 9.6 %convolution_convert_fusion = bf16[4608,512]{1,0:T(8,128)(2,1)S(1)} fusion(bf16[1024,4608]{1,0:T(8,128)(2,1)} %get-tuple-element.295, bf16[1024,512]{1,0:T(8,128)(2,1)S(1)} %get-tuple-element.296.da2), kind=kOutput, calls=%fused_computation | convolution fusion | flops 4834197504 | bytes 15204352 | tf_op jit(solution)/shard_map/ri,rj->ij/dot_general | solution.py:994
  300.1 9.0 %conv_back.3 = (bf16[1024,512]{1,0:T(8,128)(2,1)S(1)}, f32[8,512]{1,0:T(8,128)S(1)}) custom-call(s32[6]{0:T(128)S(1)} %stack.60.pos, bf16[1024,512]{1,0:T(8,128)(2,1)S(1)} %get-tuple-element.296.da2, f32[1152,128]{1,0:T(8,128)S(1)} %copy-done.2, bf16[1024,512]{1,0:T(8,128)(2,1)S(1)} %copy-done.19, f32[32,512]{1,0:T(8,128)S(1)} %copy-done.44, ...), custom_call_target="tpu_custom_call" | custom-call | flops 1024 | bytes 1024 | tf_op jit(solution)/shard_map/conv_back/pallas_call | solution.py:848
  312.5 4.8 collective-permute-done.38.got_a
  321.5 2.4 convolution_convert_fusion.3
  335.5 6.0 %collective-permute-done.44.got_a = bf16[256,512]{1,0:T(8,128)(2,1)S(1)} collective-permute-done((bf16[256,512]{1,0:T(8,128)(2,1)}, bf16[256,512]{1,0:T(8,128)(2,1)S(1)}, u32[]{:S(2)}, u32[]{:S(2)}) %collective-permute-start.44) | collective-permute-done | bytes 262176 | tf_op jit(solution)/shard_map/ppermute | solution.py:75
  346.9 4.3 multiply_reduce_fusion
  362.3 4.5 collective-permute-done.48
  379.6 7.4 %collective-permute-done.54 = bf16[288,512]{1,0:T(8,128)(2,1)S(1)} collective-permute-done((bf16[288,512]{1,0:T(8,128)(2,1)S(1)}, bf16[288,512]{1,0:T(8,128)(2,1)S(1)}, u32[]{:S(2)}, u32[]{:S(2)}) %collective-permute-start.54) | collective-permute-done | bytes 294944 | tf_op jit(solution)/shard_map/ppermute | solution.py:75
  389.3 5.9 %collective-permute-done.58.got_a = bf16[2,256,512]{2,1,0:T(8,128)(2,1)S(1)} collective-permute-done((bf16[2,256,512]{2,1,0:T(8,128)(2,1)S(1)}, bf16[2,256,512]{2,1,0:T(8,128)(2,1)S(1)}, u32[]{:S(2)}, u32[]{:S(2)}) %collective-permute-start.58) | collective-permute-done | bytes 524320 | tf_op jit(solution)/shard_map/ppermute | solution.py:75
  398.5 3.9 collective-permute-done.60
  403.1 10.7 %collective-permute-done.49 = f32[16,1024]{1,0:T(8,128)S(1)} collective-permute-done((f32[16,1024]{1,0:T(8,128)S(1)}, f32[16,1024]{1,0:T(8,128)S(1)}, u32[]{:S(2)}, u32[]{:S(2)}) %collective-permute-start.49) | collective-permute-done | bytes 65568 | tf_op jit(solution)/shard_map/ppermute | solution.py:75
  417.0 6.0 %collective-permute-done.67.rest_1_.rest_5_ = bf16[256,512]{1,0:T(8,128)(2,1)S(1)} collective-permute-done((bf16[256,512]{1,0:T(8,128)(2,1)S(1)}, bf16[256,512]{1,0:T(8,128)(2,1)S(1)}, u32[]{:S(2)}, u32[]{:S(2)}) %collective-permute-start.67) | collective-permute-done | bytes 262176 | tf_op jit(solution)/shard_map/ppermute | solution.py:75
  424.2 2.7 collective-permute-start.72
  434.5 3.8 cross_gram.5
  440.6 7.6 %collective-permute-done.82 = bf16[256,512]{1,0:T(8,128)(2,1)S(1)} collective-permute-done((bf16[256,512]{1,0:T(8,128)(2,1)S(1)}, bf16[256,512]{1,0:T(8,128)(2,1)S(1)}, u32[]{:S(2)}, u32[]{:S(2)}) %collective-permute-start.82) | collective-permute-done | bytes 262176 | tf_op jit(solution)/shard_map/ppermute | solution.py:75
  459.1 7.7 %collective-permute-done.93 = bf16[1,144,512]{2,1,0:T(8,128)(2,1)S(1)} collective-permute-done((bf16[1,144,512]{2,1,0:T(8,128)(2,1)S(1)}, bf16[1,144,512]{2,1,0:T(8,128)(2,1)S(1)}, u32[]{:S(2)}, u32[]{:S(2)}) %collective-permute-start.93) | collective-permute-done | bytes 147488 | tf_op jit(solution)/shard_map/ppermute | solution.py:75
  467.7 4.0 cross_gram.7
  475.9 6.0 %collective-permute-done.96 = bf16[1,144,512]{2,1,0:T(8,128)(2,1)S(1)} collective-permute-done((bf16[1,144,512]{2,1,0:T(8,128)(2,1)S(1)}, bf16[1,144,512]{2,1,0:T(8,128)(2,1)S(1)}, u32[]{:S(2)}, u32[]{:S(2)}) %collective-permute-start.96) | collective-permute-done | bytes 147488 | tf_op jit(solution)/shard_map/ppermute | solution.py:75
  485.5 2.5 reshape.218.grad
  496.5 22.9 %newton.1 = (f32[2048,512]{1,0:T(8,128)}, f32[2304,512]{1,0:T(8,128)}, f32[2048,512]{1,0:T(8,128)}, f32[2304,512]{1,0:T(8,128)}, f32[8,128]{1,0:T(8,128)}) custom-call(s32[6]{0:T(128)} %copy-done.28, f32[2]{0:T(128)} %pad_maximum_fusion.9.facts, bf16[3,144,512]{2,1,0:T(8,128)(2,1)} %copy-done.65, bf16[3,144,512]{2,1,0:T(8,128)(2,1)} %copy-done.66, ...), custom_call_target="tpu_custom_call" | custom-call | tf_op jit(solution)/shard_map/newton/pallas_call | solution.py:1246
  522.3 8.3 %heads.1 = (f32[918,1,512]{2,1,0:T(1,128)}, f32[918,1,512]{2,1,0:T(1,128)}, f32[918,1,512]{2,1,0:T(1,128)}) custom-call(f32[1]{0:T(128)} %bitcast.65.factor, f32[918,1,512]{2,1,0:T(1,128)} %bitcast.165, f32[918,1,512]{2,1,0:T(1,128)} %bitcast.170, f32[918,1,512]{2,1,0:T(1,128)} %bitcast.171, f32[918,1,512]{2,1,0:T(1,128)} %reshape.218.grad), custom_call_target="tpu_custom_call" | custom-call | tf_op jit(solution)/shard_map/heads/pallas_call | solution.py:978
  (535 shorter events, 154.8 us)
Async XLA Ops:
  7.6 13.6 %collective-permute-start.1 = (bf16[256,512]{1,0:T(8,128)(2,1)}, bf16[256,512]{1,0:T(8,128)(2,1)S(1)}, u32[]{:S(2)}, u32[]{:S(2)}) collective-permute-start(bf16[256,512]{1,0:T(8,128)(2,1)} %dynamic-slice_bitcast_fusion.10), channel_id=1, source_target_pairs={{0,2},{1,3},{2,0},{3,1},{4,6},{5,7},{6,4},{7,5},{8,10},{9,11},{10,... | collective-permute-start | bytes 786440 | tf_op jit(solution)/shard_map/ppermute | solution.py:75
  21.2 23.6 %collective-permute-start.6 = (bf16[832,512]{1,0:T(8,128)(2,1)}, bf16[832,512]{1,0:T(8,128)(2,1)S(1)}, u32[]{:S(2)}, u32[]{:S(2)}) collective-permute-start(bf16[832,512]{1,0:T(8,128)(2,1)} %pad_maximum_fusion.2), channel_id=1, source_target_pairs={{0,1},{1,0},{2,3},{3,2},{4,5},{5,4},{6,7},{7,6},{8,9},{9,8},{10,11... | collective-permute-start | bytes 2555912 | tf_op jit(solution)/shard_map/ppermute | solution.py:75
  22.5 24.3 %collective-permute-start.7 = (bf16[832,512]{1,0:T(8,128)(2,1)}, bf16[832,512]{1,0:T(8,128)(2,1)S(1)}, u32[]{:S(2)}, u32[]{:S(2)}) collective-permute-start(bf16[832,512]{1,0:T(8,128)(2,1)} %pad_maximum_fusion.2), channel_id=1, source_target_pairs={{0,2},{1,3},{2,0},{3,1},{4,6},{5,7},{6,4},{7,5},{8,10},{9,11},{10,... | collective-permute-start | bytes 2555912 | tf_op jit(solution)/shard_map/ppermute | solution.py:75
  44.8 14.8 %collective-permute-start.10 = (bf16[832,512]{1,0:T(8,128)(2,1)S(1)}, bf16[832,512]{1,0:T(8,128)(2,1)S(1)}, u32[]{:S(2)}, u32[]{:S(2)}) collective-permute-start(bf16[832,512]{1,0:T(8,128)(2,1)S(1)} %collective-permute-done.6.rest_1_.rest_10_), channel_id=1, source_target_pairs={{0,4},{1,5},{2,6},{3,7},{4,0},{5,1},{6,2},{7,3},{8,12},{9,13},{10,... | collective-permute-start | bytes 2555912 | tf_op jit(solution)/shard_map/ppermute | solution.py:75
  46.9 20.6 %collective-permute-start.11 = (bf16[832,512]{1,0:T(8,128)(2,1)S(1)}, bf16[832,512]{1,0:T(8,128)(2,1)S(1)}, u32[]{:S(2)}, u32[]{:S(2)}) collective-permute-start(bf16[832,512]{1,0:T(8,128)(2,1)S(1)} %collective-permute-done.7.rest_2_.rest_11_), channel_id=1, source_target_pairs={{0,4},{1,5},{2,6},{3,7},{4,0},{5,1},{6,2},{7,3},{8,12},{9,13},{10,... | collective-permute-start | bytes 2555912 | tf_op jit(solution)/shard_map/ppermute | solution.py:75
  48.7 34.4 %collective-permute-start.14 = (bf16[832,512]{1,0:T(8,128)(2,1)}, bf16[832,512]{1,0:T(8,128)(2,1)S(1)}, u32[]{:S(2)}, u32[]{:S(2)}) collective-permute-start(bf16[832,512]{1,0:T(8,128)(2,1)} %pad_maximum_fusion.3), channel_id=1, source_target_pairs={{0,1},{1,0},{2,3},{3,2},{4,5},{5,4},{6,7},{7,6},{8,9},{9,8},{10,11... | collective-permute-start | bytes 2555912 | tf_op jit(solution)/shard_map/ppermute | solution.py:75
  57.2 26.8 %collective-permute-start.15 = (bf16[832,512]{1,0:T(8,128)(2,1)}, bf16[832,512]{1,0:T(8,128)(2,1)S(1)}, u32[]{:S(2)}, u32[]{:S(2)}) collective-permute-start(bf16[832,512]{1,0:T(8,128)(2,1)} %pad_maximum_fusion.3), channel_id=1, source_target_pairs={{0,2},{1,3},{2,0},{3,1},{4,6},{5,7},{6,4},{7,5},{8,10},{9,11},{10,... | collective-permute-start | bytes 2555912 | tf_op jit(solution)/shard_map/ppermute | solution.py:75
  83.2 26.8 %collective-permute-start.20 = (bf16[832,512]{1,0:T(8,128)(2,1)S(1)}, bf16[832,512]{1,0:T(8,128)(2,1)S(1)}, u32[]{:S(2)}, u32[]{:S(2)}) collective-permute-start(bf16[832,512]{1,0:T(8,128)(2,1)S(1)} %collective-permute-done.14.rest_1_.rest_10_), channel_id=1, source_target_pairs={{0,4},{1,5},{2,6},{3,7},{4,0},{5,1},{6,2},{7,3},{8,12},{9,13},{10,... | collective-permute-start | bytes 2555912 | tf_op jit(solution)/shard_map/ppermute | solution.py:75
  83.4 16.7 %collective-permute-start.18 = (bf16[416,512]{1,0:T(8,128)(2,1)S(1)}, bf16[416,512]{1,0:T(8,128)(2,1)S(1)}, u32[]{:S(2)}, u32[]{:S(2)}) collective-permute-start(bf16[416,512]{1,0:T(8,128)(2,1)S(1)} %slice.167), channel_id=1, source_target_pairs={{0,2},{1,3},{2,0},{3,1},{4,6},{5,7},{6,4},{7,5},{8,10},{9,11},{10,... | collective-permute-start | bytes 1277960 | tf_op jit(solution)/shard_map/ppermute | solution.py:75
  84.0 26.5 %collective-permute-start.21 = (bf16[832,512]{1,0:T(8,128)(2,1)S(1)}, bf16[832,512]{1,0:T(8,128)(2,1)S(1)}, u32[]{:S(2)}, u32[]{:S(2)}) collective-permute-start(bf16[832,512]{1,0:T(8,128)(2,1)S(1)} %collective-permute-done.15.rest_2_.rest_11_), channel_id=1, source_target_pairs={{0,4},{1,5},{2,6},{3,7},{4,0},{5,1},{6,2},{7,3},{8,12},{9,13},{10,... | collective-permute-start | bytes 2555912 | tf_op jit(solution)/shard_map/ppermute | solution.py:75
  84.2 15.9 %collective-permute-start.19 = (bf16[416,512]{1,0:T(8,128)(2,1)S(1)}, bf16[416,512]{1,0:T(8,128)(2,1)S(1)}, u32[]{:S(2)}, u32[]{:S(2)}) collective-permute-start(bf16[416,512]{1,0:T(8,128)(2,1)S(1)} %slice.168), channel_id=1, source_target_pairs={{0,1},{1,0},{2,3},{3,2},{4,5},{5,4},{6,7},{7,6},{8,9},{9,8},{10,11... | collective-permute-start | bytes 1277960 | tf_op jit(solution)/shard_map/ppermute | solution.py:75
  85.8 16.2 %collective-permute-start.16 = (bf16[256,512]{1,0:T(8,128)(2,1)S(1)}, bf16[256,512]{1,0:T(8,128)(2,1)S(1)}, u32[]{:S(2)}, u32[]{:S(2)}) collective-permute-start(bf16[256,512]{1,0:T(8,128)(2,1)S(1)} %pad_maximum_fusion.4), channel_id=1, source_target_pairs={{0,1},{1,0},{2,3},{3,2},{4,5},{5,4},{6,7},{7,6},{8,9},{9,8},{10,11... | collective-permute-start | bytes 786440 | tf_op jit(solution)/shard_map/ppermute | solution.py:75
  109.0 30.4 %collective-permute-start.26 = (bf16[256,512]{1,0:T(8,128)(2,1)S(1)}, bf16[256,512]{1,0:T(8,128)(2,1)}, u32[]{:S(2)}, u32[]{:S(2)}) collective-permute-start(bf16[256,512]{1,0:T(8,128)(2,1)S(1)} %collective-permute-done.16.rest_1_), channel_id=1, source_target_pairs={{0,4},{1,5},{2,6},{3,7},{4,0},{5,1},{6,2},{7,3},{8,12},{9,13},{10,... | collective-permute-start | bytes 786440 | tf_op jit(solution)/shard_map/ppermute | solution.py:75
  109.9 29.5 %collective-permute-start.27 = (bf16[256,512]{1,0:T(8,128)(2,1)}, bf16[256,512]{1,0:T(8,128)(2,1)}, u32[]{:S(2)}, u32[]{:S(2)}) collective-permute-start(bf16[256,512]{1,0:T(8,128)(2,1)} %collective-permute-done.17.rest_2_), channel_id=1, source_target_pairs={{0,4},{1,5},{2,6},{3,7},{4,0},{5,1},{6,2},{7,3},{8,12},{9,13},{10,... | collective-permute-start | bytes 786440 | tf_op jit(solution)/shard_map/ppermute | solution.py:75
  110.5 14.1 %collective-permute-start.24 = (bf16[128,512]{1,0:T(8,128)(2,1)S(1)}, bf16[128,512]{1,0:T(8,128)(2,1)}, u32[]{:S(2)}, u32[]{:S(2)}) collective-permute-start(bf16[128,512]{1,0:T(8,128)(2,1)S(1)} %slice.169), channel_id=1, source_target_pairs={{0,2},{1,3},{2,0},{3,1},{4,6},{5,7},{6,4},{7,5},{8,10},{9,11},{10,... | collective-permute-start | bytes 393224 | tf_op jit(solution)/shard_map/ppermute | solution.py:75
  124.7 14.8 %collective-permute-start.28 = (bf16[128,512]{1,0:T(8,128)(2,1)}, bf16[128,512]{1,0:T(8,128)(2,1)S(1)}, u32[]{:S(2)}, u32[]{:S(2)}) collective-permute-start(bf16[128,512]{1,0:T(8,128)(2,1)} %collective-permute-done.24.rest_3_), channel_id=1, source_target_pairs={{0,4},{1,5},{2,6},{3,7},{4,0},{5,1},{6,2},{7,3},{8,12},{9,13},{10,... | collective-permute-start | bytes 393224 | tf_op jit(solution)/shard_map/ppermute | solution.py:75
  124.7 14.7 %collective-permute-start.29 = (bf16[128,512]{1,0:T(8,128)(2,1)}, bf16[128,512]{1,0:T(8,128)(2,1)S(1)}, u32[]{:S(2)}, u32[]{:S(2)}) collective-permute-start(bf16[128,512]{1,0:T(8,128)(2,1)} %collective-permute-done.25.rest_4_), channel_id=1, source_target_pairs={{0,4},{1,5},{2,6},{3,7},{4,0},{5,1},{6,2},{7,3},{8,12},{9,13},{10,... | collective-permute-start | bytes 393224 | tf_op jit(solution)/shard_map/ppermute | solution.py:75
  192.7 14.4 %all-to-all-start.1 = ((bf16[32,8,512]{2,1,0:T(8,128)(2,1)}), bf16[32,8,512]{2,1,0:T(8,128)(2,1)}, u32[]{:S(2)}, u32[]{:S(2)}) async-start(bf16[32,8,512]{2,1,0:T(8,128)(2,1)} %bitcast.157), calls=%async_computation.1 | async-start | bytes 524288 | tf_op jit(solution)/shard_map/all_to_all | solution.py:1397
  238.5 20.5 %collective-permute-start.32 = (bf16[2,2,2,288,512]{4,3,2,1,0:T(8,128)(2,1)S(1)}, bf16[2,2,2,288,512]{4,3,2,1,0:T(8,128)(2,1)S(1)}, u32[]{:S(2)}, u32[]{:S(2)}) collective-permute-start(bf16[2,2,2,288,512]{4,3,2,1,0:T(8,128)(2,1)S(1)} %dynamic-slice_bitcast_fusion.1), channel_id=1, source_target_pairs={{0,4},{1,5},{2,6},{3,7},{4,0},{5,1},{6,2},{7,3},{8,12},{9,13},{10,... | collective-permute-start | bytes 7077896 | tf_op jit(solution)/shard_map/ppermute | solution.py:75
  265.2 20.1 %collective-permute-start.33 = (bf16[2,2,2,256,512]{4,3,2,1,0:T(8,128)(2,1)}, bf16[2,2,2,256,512]{4,3,2,1,0:T(8,128)(2,1)S(1)}, u32[]{:S(2)}, u32[]{:S(2)}) collective-permute-start(bf16[2,2,2,256,512]{4,3,2,1,0:T(8,128)(2,1)} %pad_maximum_fusion), channel_id=1, source_target_pairs={{0,4},{1,5},{2,6},{3,7},{4,0},{5,1},{6,2},{7,3},{8,12},{9,13},{10,... | collective-permute-start | bytes 6291464 | tf_op jit(solution)/shard_map/ppermute | solution.py:75
  265.2 19.4 %collective-permute-start.34 = (bf16[2,288,512]{2,1,0:T(8,128)(2,1)S(1)}, bf16[2,288,512]{2,1,0:T(8,128)(2,1)S(1)}, u32[]{:S(2)}, u32[]{:S(2)}) collective-permute-start(bf16[2,288,512]{2,1,0:T(8,128)(2,1)S(1)} %get-tuple-element.275), channel_id=1, source_target_pairs={{0,1},{1,0},{2,3},{3,2},{4,5},{5,4},{6,7},{7,6},{8,9},{9,8},{10,11... | collective-permute-start | bytes 1769480 | tf_op jit(solution)/shard_map/ppermute | solution.py:75
  265.5 19.1 %collective-permute-start.35 = (bf16[2,288,512]{2,1,0:T(8,128)(2,1)S(1)}, bf16[2,288,512]{2,1,0:T(8,128)(2,1)S(1)}, u32[]{:S(2)}, u32[]{:S(2)}) collective-permute-start(bf16[2,288,512]{2,1,0:T(8,128)(2,1)S(1)} %get-tuple-element.276), channel_id=1, source_target_pairs={{0,2},{1,3},{2,0},{3,1},{4,6},{5,7},{6,4},{7,5},{8,10},{9,11},{10,... | collective-permute-start | bytes 1769480 | tf_op jit(solution)/shard_map/ppermute | solution.py:75
  295.9 22.8 %collective-permute-start.37 = (bf16[2,2,2,288,512]{4,3,2,1,0:T(8,128)(2,1)S(1)}, bf16[2,2,2,288,512]{4,3,2,1,0:T(8,128)(2,1)S(1)}, u32[]{:S(2)}, u32[]{:S(2)}) collective-permute-start(bf16[2,2,2,288,512]{4,3,2,1,0:T(8,128)(2,1)S(1)} %dynamic-slice_bitcast_fusion), channel_id=1, source_target_pairs={{0,4},{1,5},{2,6},{3,7},{4,0},{5,1},{6,2},{7,3},{8,12},{9,13},{10,... | collective-permute-start | bytes 7077896 | tf_op jit(solution)/shard_map/ppermute | solution.py:75
  298.7 18.6 %collective-permute-start.38 = (bf16[2,256,512]{2,1,0:T(8,128)(2,1)S(1)}, bf16[2,256,512]{2,1,0:T(8,128)(2,1)S(1)}, u32[]{:S(2)}, u32[]{:S(2)}) collective-permute-start(bf16[2,256,512]{2,1,0:T(8,128)(2,1)S(1)} %get-tuple-element.287), channel_id=1, source_target_pairs={{0,1},{1,0},{2,3},{3,2},{4,5},{5,4},{6,7},{7,6},{8,9},{9,8},{10,11... | collective-permute-start | bytes 1572872 | tf_op jit(solution)/shard_map/ppermute | solution.py:75
  299.0 18.3 %collective-permute-start.39 = (bf16[2,256,512]{2,1,0:T(8,128)(2,1)S(1)}, bf16[2,256,512]{2,1,0:T(8,128)(2,1)S(1)}, u32[]{:S(2)}, u32[]{:S(2)}) collective-permute-start(bf16[2,256,512]{2,1,0:T(8,128)(2,1)S(1)} %get-tuple-element.288), channel_id=1, source_target_pairs={{0,2},{1,3},{2,0},{3,1},{4,6},{5,7},{6,4},{7,5},{8,10},{9,11},{10,... | collective-permute-start | bytes 1572872 | tf_op jit(solution)/shard_map/ppermute | solution.py:75
  326.8 46.4 %collective-permute-start.50 = (bf16[2,2,2,256,512]{4,3,2,1,0:T(8,128)(2,1)}, bf16[2,2,2,256,512]{4,3,2,1,0:T(8,128)(2,1)}, u32[]{:S(2)}, u32[]{:S(2)}) collective-permute-start(bf16[2,2,2,256,512]{4,3,2,1,0:T(8,128)(2,1)} %pad_maximum_fusion.1), channel_id=1, source_target_pairs={{0,4},{1,5},{2,6},{3,7},{4,0},{5,1},{6,2},{7,3},{8,12},{9,13},{10,... | collective-permute-start | bytes 6291464 | tf_op jit(solution)/shard_map/ppermute | solution.py:75
  326.9 28.9 %collective-permute-start.47 = (bf16[3,144,512]{2,1,0:T(8,128)(2,1)}, bf16[3,144,512]{2,1,0:T(8,128)(2,1)}, u32[]{:S(2)}, u32[]{:S(2)}) collective-permute-start(bf16[3,144,512]{2,1,0:T(8,128)(2,1)} %copy-done.31), channel_id=1, source_target_pairs={{0,1},{1,0},{2,3},{3,2},{4,5},{5,4},{6,7},{7,6},{8,9},{9,8},{10,11... | collective-permute-start | bytes 1327112 | tf_op jit(solution)/shard_map/ppermute | solution.py:75
  334.4 23.6 %collective-permute-start.42 = (bf16[2,288,512]{2,1,0:T(8,128)(2,1)}, bf16[2,288,512]{2,1,0:T(8,128)(2,1)}, u32[]{:S(2)}, u32[]{:S(2)}) collective-permute-start(bf16[2,288,512]{2,1,0:T(8,128)(2,1)} %copy-done.53), channel_id=1, source_target_pairs={{0,1},{1,0},{2,3},{3,2},{4,5},{5,4},{6,7},{7,6},{8,9},{9,8},{10,11... | collective-permute-start | bytes 1769480 | tf_op jit(solution)/shard_map/ppermute | solution.py:75
  342.3 17.4 %collective-permute-start.43 = (bf16[2,288,512]{2,1,0:T(8,128)(2,1)}, bf16[2,288,512]{2,1,0:T(8,128)(2,1)}, u32[]{:S(2)}, u32[]{:S(2)}) collective-permute-start(bf16[2,288,512]{2,1,0:T(8,128)(2,1)} %copy-done.52), channel_id=1, source_target_pairs={{0,2},{1,3},{2,0},{3,1},{4,6},{5,7},{6,4},{7,5},{8,10},{9,11},{10,... | collective-permute-start | bytes 1769480 | tf_op jit(solution)/shard_map/ppermute | solution.py:75
  345.8 21.1 %collective-permute-start.48 = (bf16[3,144,512]{2,1,0:T(8,128)(2,1)S(1)}, bf16[3,144,512]{2,1,0:T(8,128)(2,1)}, u32[]{:S(2)}, u32[]{:S(2)}) collective-permute-start(bf16[3,144,512]{2,1,0:T(8,128)(2,1)S(1)} %copy-done.30), channel_id=1, source_target_pairs={{0,2},{1,3},{2,0},{3,1},{4,6},{5,7},{6,4},{7,5},{8,10},{9,11},{10,... | collective-permute-start | bytes 1327112 | tf_op jit(solution)/shard_map/ppermute | solution.py:75
  355.7 14.7 %collective-permute-start.46 = (bf16[288,512]{1,0:T(8,128)(2,1)}, bf16[288,512]{1,0:T(8,128)(2,1)S(1)}, u32[]{:S(2)}, u32[]{:S(2)}) collective-permute-start(bf16[288,512]{1,0:T(8,128)(2,1)} %copy-done.54), channel_id=1, source_target_pairs={{0,8},{1,9},{2,10},{3,11},{4,12},{5,13},{6,14},{7,15},{8,0},{9,1},... | collective-permute-start | bytes 884744 | tf_op jit(solution)/shard_map/ppermute | solution.py:75
  370.5 16.7 %collective-permute-start.55 = (bf16[3,144,512]{2,1,0:T(8,128)(2,1)S(1)}, bf16[3,144,512]{2,1,0:T(8,128)(2,1)S(1)}, u32[]{:S(2)}, u32[]{:S(2)}) collective-permute-start(bf16[3,144,512]{2,1,0:T(8,128)(2,1)S(1)} %add.202), channel_id=1, source_target_pairs={{0,2},{1,3},{2,0},{3,1},{4,6},{5,7},{6,4},{7,5},{8,10},{9,11},{10,... | collective-permute-start | bytes 1327112 | tf_op jit(solution)/shard_map/ppermute | solution.py:75
  371.5 17.5 %collective-permute-start.56 = (bf16[3,144,512]{2,1,0:T(8,128)(2,1)S(1)}, bf16[3,144,512]{2,1,0:T(8,128)(2,1)S(1)}, u32[]{:S(2)}, u32[]{:S(2)}) collective-permute-start(bf16[3,144,512]{2,1,0:T(8,128)(2,1)S(1)} %add.203), channel_id=1, source_target_pairs={{0,1},{1,0},{2,3},{3,2},{4,5},{5,4},{6,7},{7,6},{8,9},{9,8},{10,11... | collective-permute-start | bytes 1327112 | tf_op jit(solution)/shard_map/ppermute | solution.py:75
  373.3 13.7 %collective-permute-start.54 = (bf16[288,512]{1,0:T(8,128)(2,1)S(1)}, bf16[288,512]{1,0:T(8,128)(2,1)S(1)}, u32[]{:S(2)}, u32[]{:S(2)}) collective-permute-start(bf16[288,512]{1,0:T(8,128)(2,1)S(1)} %add.201), channel_id=1, source_target_pairs={{0,16},{1,17},{2,18},{3,19},{4,20},{5,21},{6,22},{7,23},{8,24},{9,... | collective-permute-start | bytes 884744 | tf_op jit(solution)/shard_map/ppermute | solution.py:75
  376.8 18.5 %collective-permute-start.58 = (bf16[2,256,512]{2,1,0:T(8,128)(2,1)S(1)}, bf16[2,256,512]{2,1,0:T(8,128)(2,1)S(1)}, u32[]{:S(2)}, u32[]{:S(2)}) collective-permute-start(bf16[2,256,512]{2,1,0:T(8,128)(2,1)S(1)} %get-tuple-element.345), channel_id=1, source_target_pairs={{0,1},{1,0},{2,3},{3,2},{4,5},{5,4},{6,7},{7,6},{8,9},{9,8},{10,11... | collective-permute-start | bytes 1572872 | tf_op jit(solution)/shard_map/ppermute | solution.py:75
  377.3 18.8 %collective-permute-start.59 = (bf16[2,256,512]{2,1,0:T(8,128)(2,1)S(1)}, bf16[2,256,512]{2,1,0:T(8,128)(2,1)S(1)}, u32[]{:S(2)}, u32[]{:S(2)}) collective-permute-start(bf16[2,256,512]{2,1,0:T(8,128)(2,1)S(1)} %get-tuple-element.346), channel_id=1, source_target_pairs={{0,2},{1,3},{2,0},{3,1},{4,6},{5,7},{6,4},{7,5},{8,10},{9,11},{10,... | collective-permute-start | bytes 1572872 | tf_op jit(solution)/shard_map/ppermute | solution.py:75
  387.0 15.5 %collective-permute-start.60 = (bf16[288,512]{1,0:T(8,128)(2,1)S(1)}, bf16[288,512]{1,0:T(8,128)(2,1)S(1)}, u32[]{:S(2)}, u32[]{:S(2)}) collective-permute-start(bf16[288,512]{1,0:T(8,128)(2,1)S(1)} %get-tuple-element.351), channel_id=1, source_target_pairs={{0,8},{1,9},{2,10},{3,11},{4,12},{5,13},{6,14},{7,15},{8,0},{9,1},... | collective-permute-start | bytes 884744 | tf_op jit(solution)/shard_map/ppermute | solution.py:75
  387.2 15.5 %collective-permute-start.61 = (bf16[256,512]{1,0:T(8,128)(2,1)S(1)}, bf16[256,512]{1,0:T(8,128)(2,1)S(1)}, u32[]{:S(2)}, u32[]{:S(2)}) collective-permute-start(bf16[256,512]{1,0:T(8,128)(2,1)S(1)} %add.205), channel_id=1, source_target_pairs={{0,16},{1,17},{2,18},{3,19},{4,20},{5,21},{6,22},{7,23},{8,24},{9,... | collective-permute-start | bytes 786440 | tf_op jit(solution)/shard_map/ppermute | solution.py:75
  389.0 24.7 %collective-permute-start.62 = (bf16[288,512]{1,0:T(8,128)(2,1)S(1)}, bf16[288,512]{1,0:T(8,128)(2,1)S(1)}, u32[]{:S(2)}, u32[]{:S(2)}) collective-permute-start(bf16[288,512]{1,0:T(8,128)(2,1)S(1)} %add.206.rest_0_), channel_id=1, source_target_pairs={{0,8},{1,9},{2,10},{3,11},{4,12},{5,13},{6,14},{7,15},{8,0},{9,1},... | collective-permute-start | bytes 884744 | tf_op jit(solution)/shard_map/ppermute | solution.py:75
  395.3 18.4 %collective-permute-start.49 = (f32[16,1024]{1,0:T(8,128)S(1)}, f32[16,1024]{1,0:T(8,128)S(1)}, u32[]{:S(2)}, u32[]{:S(2)}) collective-permute-start(f32[16,1024]{1,0:T(8,128)S(1)} %fusion.19), channel_id=1, source_target_pairs={{0,8},{1,9},{2,10},{3,11},{4,12},{5,13},{6,14},{7,15},{8,0},{9,1},... | collective-permute-start | bytes 196616 | tf_op jit(solution)/shard_map/ppermute | solution.py:75
  396.7 17.0 %collective-permute-start.64 = (bf16[256,512]{1,0:T(8,128)(2,1)S(1)}, bf16[256,512]{1,0:T(8,128)(2,1)S(1)}, u32[]{:S(2)}, u32[]{:S(2)}) collective-permute-start(bf16[256,512]{1,0:T(8,128)(2,1)S(1)} %get-tuple-element.362), channel_id=1, source_target_pairs={{0,2},{1,3},{2,0},{3,1},{4,6},{5,7},{6,4},{7,5},{8,10},{9,11},{10,... | collective-permute-start | bytes 786440 | tf_op jit(solution)/shard_map/ppermute | solution.py:75
  402.6 21.6 %collective-permute-start.66 = (bf16[288,512]{1,0:T(8,128)(2,1)S(1)}, bf16[288,512]{1,0:T(8,128)(2,1)S(1)}, u32[]{:S(2)}, u32[]{:S(2)}) collective-permute-start(bf16[288,512]{1,0:T(8,128)(2,1)S(1)} %add.210), channel_id=1, source_target_pairs={{0,16},{1,17},{2,18},{3,19},{4,20},{5,21},{6,22},{7,23},{8,24},{9,... | collective-permute-start | bytes 884744 | tf_op jit(solution)/shard_map/ppermute | solution.py:75
  413.8 15.2 %collective-permute-start.69 = (bf16[288,512]{1,0:T(8,128)(2,1)S(1)}, bf16[288,512]{1,0:T(8,128)(2,1)S(1)}, u32[]{:S(2)}, u32[]{:S(2)}) collective-permute-start(bf16[288,512]{1,0:T(8,128)(2,1)S(1)} %collective-permute-done.62.rest_1_), channel_id=1, source_target_pairs={{0,4},{1,5},{2,6},{3,7},{4,0},{5,1},{6,2},{7,3},{8,12},{9,13},{10,... | collective-permute-start | bytes 884744 | tf_op jit(solution)/shard_map/ppermute | solution.py:75
  414.9 16.8 %collective-permute-start.71 = (bf16[256,512]{1,0:T(8,128)(2,1)S(1)}, bf16[256,512]{1,0:T(8,128)(2,1)S(1)}, u32[]{:S(2)}, u32[]{:S(2)}) collective-permute-start(bf16[256,512]{1,0:T(8,128)(2,1)S(1)} %get-tuple-element.373), channel_id=1, source_target_pairs={{0,8},{1,9},{2,10},{3,11},{4,12},{5,13},{6,14},{7,15},{8,0},{9,1},... | collective-permute-start | bytes 786440 | tf_op jit(solution)/shard_map/ppermute | solution.py:75
  424.2 14.1 %collective-permute-start.72 = (bf16[288,512]{1,0:T(8,128)(2,1)S(1)}, bf16[288,512]{1,0:T(8,128)(2,1)S(1)}, u32[]{:S(2)}, u32[]{:S(2)}) collective-permute-start(bf16[288,512]{1,0:T(8,128)(2,1)S(1)} %add.213.rest_0_), channel_id=1, source_target_pairs={{0,8},{1,9},{2,10},{3,11},{4,12},{5,13},{6,14},{7,15},{8,0},{9,1},... | collective-permute-start | bytes 884744 | tf_op jit(solution)/shard_map/ppermute | solution.py:75
  433.5 14.7 %collective-permute-start.82 = (bf16[256,512]{1,0:T(8,128)(2,1)S(1)}, bf16[256,512]{1,0:T(8,128)(2,1)S(1)}, u32[]{:S(2)}, u32[]{:S(2)}) collective-permute-start(bf16[256,512]{1,0:T(8,128)(2,1)S(1)} %add.215), channel_id=1, source_target_pairs={{0,16},{1,17},{2,18},{3,19},{4,20},{5,21},{6,22},{7,23},{8,24},{9,... | collective-permute-start | bytes 786440 | tf_op jit(solution)/shard_map/ppermute | solution.py:75
  434.5 13.8 %collective-permute-start.83 = (bf16[288,512]{1,0:T(8,128)(2,1)S(1)}, bf16[288,512]{1,0:T(8,128)(2,1)S(1)}, u32[]{:S(2)}, u32[]{:S(2)}) collective-permute-start(bf16[288,512]{1,0:T(8,128)(2,1)S(1)} %add.213.rest_0_), channel_id=1, source_target_pairs={{0,4},{1,5},{2,6},{3,7},{4,0},{5,1},{6,2},{7,3},{8,12},{9,13},{10,... | collective-permute-start | bytes 884744 | tf_op jit(solution)/shard_map/ppermute | solution.py:75
  439.4 13.6 %collective-permute-start.86 = (bf16[2,144,512]{2,1,0:T(8,128)(2,1)S(1)}, bf16[2,144,512]{2,1,0:T(8,128)(2,1)S(1)}, u32[]{:S(2)}, u32[]{:S(2)}) collective-permute-start(bf16[2,144,512]{2,1,0:T(8,128)(2,1)S(1)} %get-tuple-element.387), channel_id=1, source_target_pairs={{0,2},{1,3},{2,0},{3,1},{4,6},{5,7},{6,4},{7,5},{8,10},{9,11},{10,... | collective-permute-start | bytes 884744 | tf_op jit(solution)/shard_map/ppermute | solution.py:75
  (167 other events, 2221.7 us)

commit v3 on v2

--- a/solution.py
+++ b/solution.py
@@ -269,6 +269,9 @@
         return out
 
 
+SMALL = pl.CostEstimate(flops=1024, bytes_accessed=1024, transcendentals=0)
+
+
 def vmem_call(kernel, name, ins, outs):
     return pl.pallas_call(
         kernel,
@@ -276,23 +279,23 @@
         in_specs=[pl.BlockSpec(memory_space=pltpu.SMEM)]
         + [pl.BlockSpec(memory_space=pltpu.VMEM)] * (len(ins) - 1),
         out_shape=[jax.ShapeDtypeStruct(shape, bf16) for shape in outs],
-        cost_estimate=pl.CostEstimate(flops=1024, bytes_accessed=1024, transcendentals=0),
+        cost_estimate=SMALL,
         compiler_params=pltpu.CompilerParams(vmem_limit_bytes=24 * MIB),
     )(*ins)
 
 
 def split_kernel(count, pos, *refs):
-    grads, (got, send_a, send_b, keep_a, keep_b) = refs[:count], refs[count:]
+    grads, gots, (send_a, send_b, keep_a, keep_b) = refs[:count], refs[count : 2 * count], refs[2 * count :]
     core, x, y = pos[1], pos[3], pos[4]
     start = 0
-    for g in grads:
+    for g, got in zip(grads, gots, strict=True):
         rows = pl.ds(start, g.shape[4])
         start += g.shape[4]
         for j in range(2):
-            send_a[j, rows] = g[j, 1 - x, core, 0] + got[j, 1 - x, 0, rows]
-            keep_a[j, rows] = g[j, x, core, 0] + got[j, x, 0, rows]
-            send_b[j, rows] = g[1 - y, j, core, 1] + got[1 - y, j, 1, rows]
-            keep_b[j, rows] = g[y, j, core, 1] + got[y, j, 1, rows]
+            send_a[j, rows] = g[j, 1 - x, core, 0] + got[j, 1 - x, 0]
+            keep_a[j, rows] = g[j, x, core, 0] + got[j, x, 0]
+            send_b[j, rows] = g[1 - y, j, core, 1] + got[1 - y, j, 1]
+            keep_b[j, rows] = g[y, j, core, 1] + got[y, j, 1]
 
 
 def turn_kernel(pos, keep_a, keep_b, got_a, got_b, send_a, send_b, rest_a, rest_b):
@@ -315,29 +318,31 @@
         keep[...] = rest_b[...] + got_b[...]
 
 
-def reduce_steps(net, pos, grads):
+def reduce_steps(net, pos, grads, late=()):
     if net.plain:
+        yield ()
         out = []
-        for g in grads:
+        for g in [*grads, *late]:
             share = lax.psum_scatter(g.astype(f32), "ns", scatter_dimension=0, tiled=True)
             out.append(Share((lax.psum(share, "dp").astype(bf16),), [(0, 0, None, 0, share.shape[0])]))
         return out
     core = pos[1]
 
-    def half(some, which):
-        parts = [pick(g, which, 2) for g in some]
-        return jnp.concatenate(parts, axis=3) if len(parts) > 1 else parts[0]
-
-    grads = [g.reshape(2, 2, 2, 2, g.shape[0] // 16, MID) for g in grads]
-    sent = half(grads, 1 - core)
-    got = net.swap(sent, "dp", 1)
-    deps = yield (sent,)
-    got = after(got, *deps)
+    def start(some):
+        some = [g.reshape(2, 2, 2, 2, g.shape[0] // 16, MID) for g in some]
+        sent = [pick(g, 1 - core, 2) for g in some]
+        return some, sent, [net.swap(v, "dp", 1) for v in sent]
+
+    grads, sent, gots = start(grads)
+    deps = yield tuple(sent)
+    gots = [after(v, *deps) for v in gots]
+    more, _, got_more = start(late)
+    grads, gots = grads + more, gots + got_more
     sizes = [g.shape[4] for g in grads]
     n = sum(sizes)
     two, one = (2, n, MID), (n, MID)
     send_a, send_b, keep_a, keep_b = vmem_call(
-        functools.partial(split_kernel, len(grads)), "split_sum", [pos, *grads, got], [two] * 4
+        functools.partial(split_kernel, len(grads)), "split_sum", [pos, *grads, *gots], [two] * 4
     )
     got_a, got_b = net.swap(send_a, "ns", 1), net.swap(send_b, "ns", 2)
     deps = yield send_a, send_b
@@ -460,10 +465,16 @@
     pl.when(pl.program_id(0) == 0)(body)
 
 
-def reduce_kernel(shard, also, layer, pos, x, gains, *rest):
+def reduce_kernel(shard, also, layer, raw, pos, x, gains, *rest):
     gb = Norm(gains, layer, 0)
     n = len(shard.arrays)
     refs, rest = rest[:n], rest[n:]
+    if raw:
+        frames, x, rest = x, rest[0], rest[1:]
+        for f in range(FPB):
+            last = (f + 1) * FROWS
+            x[last - 16 : last] = jnp.zeros((16, C), bf16)
+            x[f * FROWS : f * FROWS + PIX] = frames[f]
     if also is not None:
         n = len(also.arrays)
         place_rows(also, rest[:n], pos, rest[n + 4], *rest[-2:])
@@ -718,7 +729,7 @@
         out_specs=[spec for _, spec in outs],
         out_shape=[shape for shape, _ in outs],
         scratch_shapes=scratch,
-        cost_estimate=pl.CostEstimate(flops=1024, bytes_accessed=1024, transcendentals=0),
+        cost_estimate=SMALL,
         compiler_params=pltpu.CompilerParams(
             vmem_limit_bytes=limit * MIB, dimension_semantics=("arbitrary",)
         ),
@@ -730,15 +741,18 @@
 
 
 def run_reduce(pos, x, shard, gains, layer, also=None):
-    rows = x.shape[0]
+    raw = x.ndim == 3
+    rows = x.shape[0] * FROWS if raw else x.shape[0]
     more = also.arrays if also else ()
     eights = rows // BROWS * 8
     return call(
-        functools.partial(reduce_kernel, shard, also, layer),
+        functools.partial(reduce_kernel, shard, also, layer, raw),
         "reduce_norm",
         rows,
-        [SMEM, rows_spec(C), gains_spec()] + [ANY] * (len(shard.arrays) + len(more)),
-        [
+        [SMEM, pl.BlockSpec((FPB, PIX, C), lambda i: (i, 0, 0)) if raw else rows_spec(C), gains_spec()]
+        + [ANY] * (len(shard.arrays) + len(more)),
+        ([(kept_sds(rows, C, bf16), rows_spec(C))] if raw else [])
+        + [
             (sds(rows, MID, bf16), rows_spec(MID)),
             (kept_sds(rows, MID, bf16), rows_spec(MID)),
             (kept_sds(eights, MID, f32), eight_spec(MID)),
@@ -1078,8 +1092,8 @@
         scratch_shapes=[pltpu.VMEM((rows, MID), f32)]
         + [pltpu.VMEM((rows, MID), bf16)] * scratch
         + [pltpu.SemaphoreType.DMA((sems,))],
-        cost_estimate=pl.CostEstimate(flops=1024, bytes_accessed=1024, transcendentals=0),
-        compiler_params=pltpu.CompilerParams(vmem_limit_bytes=28 * MIB),
+        cost_estimate=SMALL,
+        compiler_params=pltpu.CompilerParams(vmem_limit_bytes=63 * MIB),
     )(pos, *moms, *arrays)
 
 
@@ -1301,16 +1315,13 @@
     get_a.step()
 
     masks = jnp.asarray(tap_masks())
-    stream = jnp.pad(
-        frames.reshape(samples, PIX, C), ((0, 0), (0, FROWS - PIX), (0, 0))
-    ).reshape(rows, C)
+    frames = frames.reshape(samples, PIX, C)
     gains = norm_params.reshape(2 * BLOCKS, 2 * MID + C)
-    x0 = stream
     got = get_a.step()
     get_b = gather_two(net, [w_spatial[0], w_pair[0, 1]], *got)
     sent = get_b.step()
     get_a.step()
-    h, xh1, rs1, one = run_reduce(pos, after(x0, *sent), get_a.value[0], gains, 0)
+    x0, h, xh1, rs1, one = run_reduce(pos, after(frames, *sent), get_a.value[0], gains, 0)
     sent = get_b.step(h)
 
     out_col = jnp.arange(HOUT, dtype=jnp.int32)
@@ -1322,9 +1333,9 @@
     moms = [mom_pair.reshape(-1, MID), mom_spatial.reshape(-1, MID)]
     old = old_grams(after(pos, *sent), moms)
 
+    sent = sent + (*old, head)
     get_c = gather_two(net, [w_pair[1, 0], w_spatial[1]], *sent)
-    sent = get_c.step()
-    h = after(h, *old, head)
+    sent = sent + get_c.step()
     get_b.step(*sent)
     get_b.step()
     kept = [(x0, xh1, rs1)]
@@ -1414,31 +1425,39 @@
 
     shares, grams = {}, []
 
-    def reduce_and_gram(ids, grads):
-        got = yield from reduce_steps(net, pos, grads)
+    def reduce_and_gram(ids, grads, late):
+        got = yield from reduce_steps(net, pos, grads, late)
         got = dict(zip(ids, got, strict=True))
         *packs, share = cross_grams(pos, moms, got)
         shares[tuple(ids)] = share
         grams.append((tuple(ids), (yield from gram_steps(net, packs))))
 
-    r, da3, da2, gacc3, gacc2 = tail_back(1, grad_stream)
-    sum_a = Run(reduce_and_gram((5,), [weight_grad(kept[1][3], da2)]))
-    sum_o = Run(gram_steps(net, old))
+    sum_o = Run(gram_steps(net, [after(v, grad_stream) for v in old]))
+    r, da3, da2, gacc3, gacc2 = tail_back(1, after(grad_stream, *sum_o.step()))
+    da2 = after(da2, *sum_o.step(da2))
+    late_a, late_b = [], []
+    grad_mid, grad_last = weight_grad(kept[1][3], da2), weight_grad(da3, kept[1][4])
+    sum_a = Run(reduce_and_gram((5, 3, 2), [grad_mid, grad_last], late_a))
     sent = sum_a.step()
+    sent = sent + sum_o.step(*sent)
     da1, gacc1, grad_stream = conv_back(1, after(da2, *sent), r)
+    sum_o.step(da1)
     gains_1 = jnp.concatenate([gacc1[:2], gacc2[:2], gacc3[:2]], axis=1)
+    late_a.append(weight_grad(x1, da1))
     sent = sum_a.step(da1)
-    grad_one, grad_last = weight_grad(x1, after(da1, *sent)), weight_grad(da3, kept[1][4])
-    sum_b = Run(reduce_and_gram((2, 3), [grad_one, grad_last]))
-    sent = sent + sum_b.step()
     r, da3, da2, gacc3, gacc2 = tail_back(0, after(grad_stream, *sent))
-    sent = sum_b.step(da2) + sum_a.step(da2)
-    sum_c = Run(reduce_and_gram((4,), [weight_grad(after(kept[0][3], *sent), da2)]))
-    sent = sum_c.step() + sum_o.step()
+    sent = sum_a.step(da2)
+    grad_mid, grad_last = weight_grad(after(kept[0][3], *sent), da2), weight_grad(da3, kept[0][4])
+    sum_b = Run(reduce_and_gram((4, 1, 0), [grad_mid, grad_last], late_b))
+    sent = sum_b.step()
+    sent = sent + sum_a.step(grad_mid, grad_last, *sent)
     da1, gacc1 = conv_back(0, after(da2, *sent), None)
+    sent = sum_a.step(da1)
+    late_b.append(weight_grad(x0, after(da1, *sent)))
+    sent_b = sum_b.step(*sent, late_b[0])
 
     grad_low = lax.dot_general(
-        widen, after(grad_low, da1), (((1,), (1,)), ((), ())), preferred_element_type=f32
+        widen, after(grad_low, *sent_b), (((1,), (1,)), ((), ())), preferred_element_type=f32
     ).astype(bf16)
     head_grad = jnp.dot(grad_low, feat_rows, preferred_element_type=f32)
     head_sq = jnp.sum(jnp.square(head_grad))
@@ -1449,27 +1468,28 @@
     tail = jnp.zeros((16 - small.shape[0], 1024), f32)
     lane = jnp.arange(1024, dtype=jnp.int32)[None, :]
     tail = tail + jnp.where(lane == 0, loss_part, 0.0) + jnp.where(lane == 1, head_sq, 0.0)
-    sum_s = Run(add_steps(net, jnp.concatenate([small, tail], axis=0)))
-
-    sent = sum_c.step(da1) + sum_b.step(da1) + sum_a.step(da1)
-    grad_one, grad_last = weight_grad(x0, after(da1, *sent)), weight_grad(after(da3, da1), kept[0][4])
-    sum_d = Run(reduce_and_gram((0, 1), [grad_one, grad_last]))
-
-    runs = (sum_d, sum_c, sum_b, sum_a, sum_s, sum_o)
-    deps = (grad_one, grad_last)
-    while not all(run.done for run in runs):
-        sent = ()
-        for run in runs:
-            sent = sent + run.step(*deps)
-        if sum_s.done:
-            sent = sent + (sum_s.value,)
-        deps = sent
+    small = after(jnp.concatenate([small, tail], axis=0), head_grad, weight_total)
+    sum_s = Run(add_steps(net, small))
+
+    runs = {"a": sum_a, "b": sum_b, "s": sum_s}
+    sent = sent + sent_b
+    def read_sums(value):
+        gain_sum = value[:12].reshape(BLOCKS, 2, 2 * MID + C)
+        facts = jnp.stack([value[12, 1] + jnp.sum(jnp.square(gain_sum)), weight_total])
+        return gain_sum, value[12, 0], facts
+
+    sums = None
+    for name in "assbabasbasbasbasbbbb":
+        sent = runs[name].step(*sent) or sent
+        if sum_s.done and sums is None:
+            sums = read_sums(sum_s.value)
+            sent = sent + (sums[2],)
+    while not all(run.done for run in runs.values()):
+        for run in runs.values():
+            sent = run.step(*sent) or sent
+    gain_sum, loss_sum, facts = sums or read_sums(sum_s.value)
 
     groups = tuple(ids for ids, _ in grams)
-    gain_sum = sum_s.value[:12].reshape(BLOCKS, 2, 2 * MID + C)
-    loss_sum, head_total = sum_s.value[12, 0], sum_s.value[12, 1]
-
-    facts = jnp.stack([head_total + jnp.sum(jnp.square(gain_sum)), weight_total])
     pair_new, spatial_new, pair_moment, spatial_moment, report = newton(
         pos,
         facts,

time: 536 us -> 547 us (1.021)
  starting transfers between devices: 76.1 us -> 52.8 us
  blocking collectives: 17.1 us -> 31.2 us
  local copies, waits for them, and re-layouts: 56.2 us -> 65 us
    ppermute x107 -> x79, starting transfers between devices: 72.7 us -> 52.8 us  [swap(): return lax.ppermute(value, ('dp', 'ns'), pairs)]
    ppermute x107 -> x79, waiting for transfers between devices: 117 us -> 133 us  [swap(): return lax.ppermute(value, ('dp', 'ns'), pairs)]
    all_to_all x0 -> x1, blocking collectives: none -> 14 us  [local(): lax.all_to_all(back.reshape(devices, samples, col_width), ('dp', 'ns'), 0...]
    all_to_all x1 -> x0, waiting for transfers between devices: 10.9 us -> none  [local(): lax.all_to_all(back.reshape(devices, samples, col_width), ('dp', 'ns'), 0...]
    add x20 -> x12, other arithmetic: 3.42 us -> 9.69 us  [gram_steps(): first, second = (first + after(got_a, *deps), second + after(got_b, *deps))]
    squeeze x7, local copies, waits for them, and re-layouts: 1.39 us -> 7.2 us  [pick(): return lax.dynamic_index_in_dim(value, index, axis, keepdims=False)]
    pallas_call x5 -> x3, Pallas kernels: 15.4 us -> 21 us  [gram_call(): pl.pallas_call(kernel, name=name, in_specs=[SMEM, HBM, HBM] + [ANY] * len...]
    unnamed x216 -> x182, local copies, waits for them, and re-layouts: 28.4 us -> 32.3 us
  transfers between devices with their start and end apart: 108 -> 79, of which waited for: 29 -> 27; matrix products, arithmetic and copies ran while one was open for 10% -> 16% of each run, Pallas kernels for 23% -> 25%
where the time goes in v3:
time: 547 us; the launch traced here: 541 us
  Pallas kernels  195 us (36%)
  waiting for transfers between devices  133 us (24%)
  local copies, waits for them, and re-layouts  65 us (12%)
  starting transfers between devices  52.8 us (10%)
  matrix products  36.3 us (7%)
  blocking collectives  31.2 us (6%)
  other arithmetic  22.6 us (4%)
    ppermute x79, waiting for transfers between devices, swap(): return lax.ppermute(value, ('dp', 'ns'), pairs)  133 us
    ppermute x79, starting transfers between devices, swap(): return lax.ppermute(value, ('dp', 'ns'), pairs)  52.8 us
    pallas_call x2, Pallas kernels, run_tail_back(): call(functools.partial(tail_back_kernel, shard, layer, last), 'tail_back'...  34.7 us
    unnamed x182, local copies, waits for them, and re-layouts  32.3 us
    dot_general x6, matrix products, weight_grad(): jnp.einsum('ri,rj->ij', a, b, preferred_element_type=f32).astype(bf16)  30.1 us
    pallas_call x2, Pallas kernels, run_conv(): call(functools.partial(conv_kernel, shard, also, layer), 'conv_norm', row...  26.4 us
    pallas_call x2, Pallas kernels, run_expand(): call(functools.partial(expand_kernel, shard, layer, last), 'expand_norm',...  26.3 us
    pallas_call x1, Pallas kernels, newton(): pl.pallas_call(functools.partial(newton_kernel, groups), name='newton', i...  22.6 us
  transfers between devices with their start and end apart: 79, of which 27 were waited for; matrix products, arithmetic and copies ran while one was open for 16% of the time, Pallas kernels for 25%

profile of v3, /device:TPU:0, one launch (start us, length us, event | category | flops | bytes accessed | tf_op | source)
XLA Modules:
  0.0 540.8 jit_solution(14324123325946987997)
XLA Ops:
  0.7 2.4 fusion.21
  3.9 2.9 collective-permute-start
  8.4 4.1 fusion.20
  15.6 4.9 collective-permute-done.1.rest_2_
  23.0 6.3 %copy.35 = bf16[2,4,121,2048]{3,2,1,0:T(8,128)(2,1)} copy(bf16[2,4,121,2048]{3,1,2,0:T(4,128)(2,1)} %param.16) | data formatting | bytes 7929856 | tf_op args[0]
  34.0 8.6 %reduce_norm.2 = (bf16[1024,2048]{1,0:T(8,128)(2,1)}, bf16[1024,512]{1,0:T(8,128)(2,1)S(1)}, bf16[1024,512]{1,0:T(8,128)(2,1)}, f32[32,512]{1,0:T(8,128)}, bf16[2048,512]{1,0:T(8,128)(2,1)}) custom-call(s32[6]{0:T(128)S(1)} %stack.60.pos, bf16[8,121,2048]{2,1,0:T(8,128)(2,1)} %bitcast.149, f32[4,3072]{1,0:T(4,128)S(1)} %reshape.193.gains, ...), custom_call_target="tpu_custom_call" | custom-call | flops 1024 | bytes 1024 | tf_op jit(solution)/shard_map/reduce_norm/pallas_call | solution.py:748
  50.4 2.8 fusion.2.head
  53.2 6.9 %old_gram.1 = (bf16[3,144,512]{2,1,0:T(8,128)(2,1)}, bf16[3,144,512]{2,1,0:T(8,128)(2,1)}) custom-call(s32[6]{0:T(128)} %copy-done.36, f32[2048,512]{1,0:T(8,128)} %bitcast.145, f32[2304,512]{1,0:T(8,128)} %bitcast.141), custom_call_target="tpu_custom_call" | custom-call | flops 1024 | bytes 1024 | tf_op jit(solution)/shard_map/old_gram/pallas_call | solution.py:1086
  65.9 13.8 %conv_norm.2 = (bf16[1024,4608]{1,0:T(8,128)(2,1)}, bf16[1024,512]{1,0:T(8,128)(2,1)}, bf16[1024,512]{1,0:T(8,128)(2,1)}, f32[32,512]{1,0:T(8,128)}, bf16[4608,5...) custom-call(s32[6]{0:T(128)S(1)} %copy-done.37, bf16[1024,512]{1,0:T(8,128)(2,1)} %copy-done.29, f32[1152,128]{1,0:T(8,128)S(1)} %copy-done.2, ...), custom_call_target="tpu_custom_call" | custom-call | flops 1024 | bytes 1024 | tf_op jit(solution)/shard_map/conv_norm/pallas_call | solution.py:776
  87.1 12.5 %expand_norm.2 = (bf16[1024,2048]{1,0:T(8,128)(2,1)}, f32[32,2048]{1,0:T(8,128)}, bf16[1024,2048]{1,0:T(8,128)(2,1)}, bf16[2048,512]{1,0:T(8,128)(2,1)}) custom-call(s32[6]{0:T(128)S(1)} %copy-done.37, bf16[1024,512]{1,0:T(8,128)(2,1)S(1)} %copy-done.24, bf16[1024,2048]{1,0:T(8,128)(2,1)} %get-tuple-element.189.x, f32[4,3072]{1,0:T(4,128)S(1)} %reshape.193.gains, ...), custom_call_target="tpu_custom_call" | custom-call | flops 1024 | bytes 1024 | tf_op jit(solution)/shard_map/expand_norm/pallas_call | solution.py:803
  101.4 7.1 %collective-permute-done.17.rest_2_ = bf16[256,512]{1,0:T(8,128)(2,1)} collective-permute-done((bf16[256,512]{1,0:T(8,128)(2,1)S(1)}, bf16[256,512]{1,0:T(8,128)(2,1)}, u32[]{:S(2)}, u32[]{:S(2)}) %collective-permute-start.17) | collective-permute-done | bytes 262176 | tf_op jit(solution)/shard_map/ppermute | solution.py:75
  111.8 11.8 %reduce_norm.3 = (bf16[1024,512]{1,0:T(8,128)(2,1)}, bf16[1024,512]{1,0:T(8,128)(2,1)}, f32[32,512]{1,0:T(8,128)}, bf16[2048,512]{1,0:T(8,128)(2,1)}, bf16[4608,512]{1,0:T(8,128)(2,1)}) custom-call(s32[6]{0:T(128)S(1)} %copy-done.37, bf16[1024,2048]{1,0:T(8,128)(2,1)} %get-tuple-element.194.x, f32[4,3072]{1,0:T(4,128)S(1)} %reshape.193.gains, ...), custom_call_target="tpu_custom_call" | custom-call | flops 1024 | bytes 1024 | tf_op jit(solution)/shard_map/reduce_norm/pallas_call | solution.py:748
  126.0 12.7 %conv_norm.3 = (bf16[1024,4608]{1,0:T(8,128)(2,1)}, bf16[1024,512]{1,0:T(8,128)(2,1)S(1)}, bf16[1024,512]{1,0:T(8,128)(2,1)}, f32[32,512]{1,0:T(8,128)}, bf16[4608,512]{1,0:T(8,128)(2,1)}) custom-call(s32[6]{0:T(128)S(1)} %copy-done.37, bf16[1024,512]{1,0:T(8,128)(2,1)S(1)} %copy-done.22, f32[1152,128]{1,0:T(8,128)S(1)} %copy-done.2, ...), custom_call_target="tpu_custom_call" | custom-call | flops 1024 | bytes 1024 | tf_op jit(solution)/shard_map/conv_norm/pallas_call | solution.py:776
  138.7 13.8 %expand_norm.3 = (bf16[1024,2048]{1,0:T(8,128)(2,1)}, f32[32,2048]{1,0:T(8,128)}, f32[32,2048]{1,0:T(8,128)S(1)}, bf16[2048,512]{1,0:T(8,128)(2,1)}) custom-call(s32[6]{0:T(128)S(1)} %copy-done.37, bf16[1024,512]{1,0:T(8,128)(2,1)S(1)} %get-tuple-element.199.u2, bf16[1024,2048]{1,0:T(8,128)(2,1)} %get-tuple-element.194.x, f32[4,3072]{1,0:T(4,128)S(1)} %reshape.193.gains, ...), custom_call_target="tpu_custom_call" | custom-call | flops 1024 | bytes 1024 | tf_op jit(solution)/shard_map/expand_norm/pallas_call | solution.py:803
  152.7 17.2 %all_to_all.10 = bf16[32,8,640]{2,1,0:T(8,128)(2,1)S(1)} all-to-all(bf16[32,8,640]{2,1,0:T(8,128)(2,1)S(1)} %bitcast.159), channel_id=1, replica_groups=mesh['dp'=8,'ns'=4] {'dp','ns'}, dimensions={0} | all-to-all | bytes 655360 | tf_op jit(solution)/shard_map/all_to_all | solution.py:1385
  173.2 7.9 %collective-permute-done.30 = f32[64,1152]{1,0:T(8,128)S(1)} collective-permute-done((f32[64,1152]{1,0:T(8,128)S(1)}, f32[64,1152]{1,0:T(8,128)S(1)}, u32[]{:S(2)}, u32[]{:S(2)}) %collective-permute-start.30) | collective-permute-done | bytes 294944 | tf_op jit(solution)/shard_map/ppermute | solution.py:75
  182.8 7.0 %collective-permute-done.31 = f32[64,1152]{1,0:T(8,128)S(1)} collective-permute-done((f32[64,1152]{1,0:T(8,128)S(1)}, f32[64,1152]{1,0:T(8,128)S(1)}, u32[]{:S(2)}, u32[]{:S(2)}) %collective-permute-start.31) | collective-permute-done | bytes 294944 | tf_op jit(solution)/shard_map/ppermute | solution.py:75
  191.4 14.0 %all_to_all.11 = bf16[32,8,512]{2,1,0:T(8,128)(2,1)S(1)} all-to-all(bf16[32,8,512]{2,1,0:T(8,128)(2,1)S(1)} %bitcast.140), channel_id=1, replica_groups=mesh['dp'=8,'ns'=4] {'dp','ns'}, dimensions={0} | all-to-all | bytes 524288 | tf_op jit(solution)/shard_map/all_to_all | solution.py:1408
  210.8 16.7 %tail_back.2 = (bf16[1024,2048]{1,0:T(8,128)(2,1)}, bf16[1024,2048]{1,0:T(8,128)(2,1)}, bf16[1024,512]{1,0:T(8,128)(2,1)S(1)}, f32[8,2048]{1,0:T(8,128)S(1)}, f32[8,512]{1,0:T(8,128)S(1)}) custom-call(s32[6]{0:T(128)S(1)} %copy-done.37, f32[32,2048]{1,0:T(8,128)S(1)} %pad_bitcast_fusion.d, bf16[1024,2048]{1,0:T(8,128)(2,1)} %get-tuple-element.194.x, ...), custom_call_target="tpu_custom_call" | custom-call | flops 1024 | bytes 1024 | tf_op jit(solution)/shard_map/tail_back/pallas_call | solution.py:825
  232.6 9.2 %convolution_convert_fusion.1 = bf16[4608,512]{1,0:T(8,128)(2,1)S(1)} fusion(bf16[1024,4608]{1,0:T(8,128)(2,1)} %get-tuple-element.219, bf16[1024,512]{1,0:T(8,128)(2,1)S(1)} %get-tuple-element.223.da2), kind=kOutput, calls=%fused_computation.1 | convolution fusion | flops 4834197504 | bytes 15204352 | tf_op jit(solution)/shard_map/ri,rj->ij/dot_general | solution.py:1008
  243.5 2.4 convolution_convert_fusion.5
  249.3 12.2 %conv_back.2 = (bf16[1024,512]{1,0:T(8,128)(2,1)S(1)}, f32[8,512]{1,0:T(8,128)S(1)}, bf16[1024,2048]{1,0:T(8,128)(2,1)S(1)}) custom-call(s32[6]{0:T(128)S(1)} %copy-done.37, bf16[1024,512]{1,0:T(8,128)(2,1)S(1)} %get-tuple-element.223.da2, f32[1152,128]{1,0:T(8,128)S(1)} %copy-done.2, bf16[1024,512]{1,0:T(8,128)(2,1)S(1)} %copy-done.26, ...), custom_call_target="tpu_custom_call" | custom-call | flops 1024 | bytes 1024 | tf_op jit(solution)/shard_map/conv_back/pallas_call | solution.py:862
  263.5 2.4 convolution_convert_fusion.4
  266.2 2.6 collective-permute-done.38.refs_5_
  272.3 18.1 %tail_back.3 = (bf16[1024,2048]{1,0:T(8,128)(2,1)}, bf16[1024,2048]{1,0:T(8,128)(2,1)}, bf16[1024,512]{1,0:T(8,128)(2,1)S(1)}, f32[8,2048]{1,0:T(8,128)S(1)}, f32[8,512]{1,0:T(8,128)S(1)}) custom-call(s32[6]{0:T(128)S(1)} %copy-done.37, bf16[1024,2048]{1,0:T(8,128)(2,1)} %copy-done.9, bf16[1024,2048]{1,0:T(8,128)(2,1)} %get-tuple-element.189.x, ...), custom_call_target="tpu_custom_call" | custom-call | flops 1024 | bytes 1024 | tf_op jit(solution)/shard_map/tail_back/pallas_call | solution.py:825
  290.4 4.6 convolution_convert_fusion.3
  295.0 2.4 collective-permute-done.39.got_a
  300.5 9.1 %convolution_convert_fusion = bf16[4608,512]{1,0:T(8,128)(2,1)S(1)} fusion(bf16[1024,4608]{1,0:T(8,128)(2,1)} %get-tuple-element.247, bf16[1024,512]{1,0:T(8,128)(2,1)S(1)} %get-tuple-element.254.da2), kind=kOutput, calls=%fused_computation | convolution fusion | flops 4834197504 | bytes 15204352 | tf_op jit(solution)/shard_map/ri,rj->ij/dot_general | solution.py:1008
  316.2 9.3 %conv_back.3 = (bf16[1024,512]{1,0:T(8,128)(2,1)S(1)}, f32[8,512]{1,0:T(8,128)S(1)}) custom-call(s32[6]{0:T(128)S(1)} %copy-done.37, bf16[1024,512]{1,0:T(8,128)(2,1)S(1)} %get-tuple-element.254.da2, f32[1152,128]{1,0:T(8,128)S(1)} %copy-done.2, bf16[1024,512]{1,0:T(8,128)(2,1)S(1)} %copy-done.23, f32[32,512]{1,0:T(8,128)S(1)} %copy-done.38, ...), custom_call_target="tpu_custom_call" | custom-call | flops 1024 | bytes 1024 | tf_op jit(solution)/shard_map/conv_back/pallas_call | solution.py:862
  325.5 4.7 collective-permute-done.43
  331.2 2.5 convolution_convert_fusion.2
  342.7 2.3 copy-done.1
  347.8 3.8 split_sum.3
  355.5 3.4 multiply_reduce_fusion
  358.9 4.2 reshape.208.grad
  363.9 18.5 %collective-permute-done.49 = bf16[544,512]{1,0:T(8,128)(2,1)} collective-permute-done((bf16[544,512]{1,0:T(8,128)(2,1)}, bf16[544,512]{1,0:T(8,128)(2,1)}, u32[]{:S(2)}, u32[]{:S(2)}) %collective-permute-start.49) | collective-permute-done | bytes 557088 | tf_op jit(solution)/shard_map/ppermute | solution.py:75
  387.5 10.6 %collective-permute-done.50.rest_1_.rest_5_.rest_9_ = bf16[544,512]{1,0:T(8,128)(2,1)S(1)} collective-permute-done((bf16[544,512]{1,0:T(8,128)(2,1)S(1)}, bf16[544,512]{1,0:T(8,128)(2,1)S(1)}, u32[]{:S(2)}, u32[]{:S(2)}) %collective-permute-start.50) | collective-permute-done | bytes 557088 | tf_op jit(solution)/shard_map/ppermute | solution.py:75
  405.4 7.0 %cross_gram.2 = (bf16[3,144,512]{2,1,0:T(8,128)(2,1)}, bf16[3,144,512]{2,1,0:T(8,128)(2,1)}, bf16[2176,512]{1,0:T(8,128)(2,1)}) custom-call(s32[6]{0:T(128)} %copy-done.36, f32[2048,512]{1,0:T(8,128)} %bitcast.146, f32[2304,512]{1,0:T(8,128)} %bitcast.142, bf16[544,512]{1,0:T(8,128)(2,1)} %copy-done.53, bf16[544,512]{1,0:T(8,128)(2,1)} %copy-done.56, ...), custom_call_target="tpu_custom_call" | custom-call | flops 1024 | bytes 1024 | tf_op jit(solution)/shard_map/cross_gram/pallas_call | solution.py:1086
  412.4 5.1 collective-permute-done.48
  424.2 5.7 %collective-permute-done.58 = bf16[3,144,512]{2,1,0:T(8,128)(2,1)S(1)} collective-permute-done((bf16[3,144,512]{2,1,0:T(8,128)(2,1)}, bf16[3,144,512]{2,1,0:T(8,128)(2,1)S(1)}, u32[]{:S(2)}, u32[]{:S(2)}) %collective-permute-start.58) | collective-permute-done | bytes 442400 | tf_op jit(solution)/shard_map/ppermute | solution.py:75
  431.3 15.8 %collective-permute-done.57 = f32[16,1024]{1,0:T(8,128)S(1)} collective-permute-done((f32[16,1024]{1,0:T(8,128)S(1)}, f32[16,1024]{1,0:T(8,128)S(1)}, u32[]{:S(2)}, u32[]{:S(2)}) %collective-permute-start.57) | collective-permute-done | bytes 65568 | tf_op jit(solution)/shard_map/ppermute | solution.py:75
  449.9 9.0 %collective-permute-done.62 = bf16[3,144,512]{2,1,0:T(8,128)(2,1)S(1)} collective-permute-done((bf16[3,144,512]{2,1,0:T(8,128)(2,1)S(1)}, bf16[3,144,512]{2,1,0:T(8,128)(2,1)S(1)}, u32[]{:S(2)}, u32[]{:S(2)}) %collective-permute-start.62) | collective-permute-done | bytes 442400 | tf_op jit(solution)/shard_map/ppermute | solution.py:75
  462.5 3.4 collective-permute-done.65
  470.4 7.0 %cross_gram.3 = (bf16[3,144,512]{2,1,0:T(8,128)(2,1)}, bf16[3,144,512]{2,1,0:T(8,128)(2,1)}, bf16[2176,512]{1,0:T(8,128)(2,1)}) custom-call(s32[6]{0:T(128)} %copy-done.36, f32[2048,512]{1,0:T(8,128)} %bitcast.147, f32[2304,512]{1,0:T(8,128)} %bitcast.143, bf16[544,512]{1,0:T(8,128)(2,1)} %copy-done.54, bf16[544,512]{1,0:T(8,128)(2,1)} %copy-done.57, ...), custom_call_target="tpu_custom_call" | custom-call | flops 1024 | bytes 1024 | tf_op jit(solution)/shard_map/cross_gram/pallas_call | solution.py:1086
  479.8 9.7 %collective-permute-done.73 = bf16[3,144,512]{2,1,0:T(8,128)(2,1)S(1)} collective-permute-done((bf16[3,144,512]{2,1,0:T(8,128)(2,1)}, bf16[3,144,512]{2,1,0:T(8,128)(2,1)S(1)}, u32[]{:S(2)}, u32[]{:S(2)}) %collective-permute-start.73) | collective-permute-done | bytes 442400 | tf_op jit(solution)/shard_map/ppermute | solution.py:75
  494.7 6.8 %collective-permute-done.74 = bf16[3,144,512]{2,1,0:T(8,128)(2,1)S(1)} collective-permute-done((bf16[3,144,512]{2,1,0:T(8,128)(2,1)S(1)}, bf16[3,144,512]{2,1,0:T(8,128)(2,1)S(1)}, u32[]{:S(2)}, u32[]{:S(2)}) %collective-permute-start.74) | collective-permute-done | bytes 442400 | tf_op jit(solution)/shard_map/ppermute | solution.py:75
  506.6 22.6 %newton.1 = (f32[2048,512]{1,0:T(8,128)}, f32[2304,512]{1,0:T(8,128)}, f32[2048,512]{1,0:T(8,128)}, f32[2304,512]{1,0:T(8,128)}, f32[8,128]{1,0:T(8,128)}) custom-call(s32[6]{0:T(128)} %copy-done.36, f32[2]{0:T(128)} %pad_maximum_fusion.7.facts, bf16[3,144,512]{2,1,0:T(8,128)(2,1)} %add.163.rest_0_, bf16[3,144,512]{2,1,0:T(8,128)(2,1)} %add.164.rest_1_, ...), custom_call_target="tpu_custom_call" | custom-call | tf_op jit(solution)/shard_map/newton/pallas_call | solution.py:1260
  532.3 8.4 %heads.1 = (f32[918,1,512]{2,1,0:T(1,128)}, f32[918,1,512]{2,1,0:T(1,128)}, f32[918,1,512]{2,1,0:T(1,128)}) custom-call(f32[1]{0:T(128)} %bitcast.64.factor, f32[918,1,512]{2,1,0:T(1,128)} %bitcast.152, f32[918,1,512]{2,1,0:T(1,128)} %bitcast.157, f32[918,1,512]{2,1,0:T(1,128)} %bitcast.158, f32[918,1,512]{2,1,0:T(1,128)} %reshape.208.grad), custom_call_target="tpu_custom_call" | custom-call | tf_op jit(solution)/shard_map/heads/pallas_call | solution.py:992
  (419 shorter events, 140.2 us)
Async XLA Ops:
  6.9 13.6 %collective-permute-start.1 = (bf16[256,512]{1,0:T(8,128)(2,1)}, bf16[256,512]{1,0:T(8,128)(2,1)S(1)}, u32[]{:S(2)}, u32[]{:S(2)}) collective-permute-start(bf16[256,512]{1,0:T(8,128)(2,1)} %dynamic-slice_bitcast_fusion.10), channel_id=1, source_target_pairs={{0,2},{1,3},{2,0},{3,1},{4,6},{5,7},{6,4},{7,5},{8,10},{9,11},{10,... | collective-permute-start | bytes 786440 | tf_op jit(solution)/shard_map/ppermute | solution.py:75
  20.5 22.1 %collective-permute-start.6 = (bf16[832,512]{1,0:T(8,128)(2,1)}, bf16[832,512]{1,0:T(8,128)(2,1)}, u32[]{:S(2)}, u32[]{:S(2)}) collective-permute-start(bf16[832,512]{1,0:T(8,128)(2,1)} %pad_maximum_fusion), channel_id=1, source_target_pairs={{0,1},{1,0},{2,3},{3,2},{4,5},{5,4},{6,7},{7,6},{8,9},{9,8},{10,11... | collective-permute-start | bytes 2555912 | tf_op jit(solution)/shard_map/ppermute | solution.py:75
  21.7 24.7 %collective-permute-start.7 = (bf16[832,512]{1,0:T(8,128)(2,1)}, bf16[832,512]{1,0:T(8,128)(2,1)}, u32[]{:S(2)}, u32[]{:S(2)}) collective-permute-start(bf16[832,512]{1,0:T(8,128)(2,1)} %pad_maximum_fusion), channel_id=1, source_target_pairs={{0,2},{1,3},{2,0},{3,1},{4,6},{5,7},{6,4},{7,5},{8,10},{9,11},{10,... | collective-permute-start | bytes 2555912 | tf_op jit(solution)/shard_map/ppermute | solution.py:75
  44.7 17.5 %collective-permute-start.10 = (bf16[832,512]{1,0:T(8,128)(2,1)}, bf16[832,512]{1,0:T(8,128)(2,1)}, u32[]{:S(2)}, u32[]{:S(2)}) collective-permute-start(bf16[832,512]{1,0:T(8,128)(2,1)} %collective-permute-done.6.rest_1_.rest_10_), channel_id=1, source_target_pairs={{0,4},{1,5},{2,6},{3,7},{4,0},{5,1},{6,2},{7,3},{8,12},{9,13},{10,... | collective-permute-start | bytes 2555912 | tf_op jit(solution)/shard_map/ppermute | solution.py:75
  45.2 16.2 %collective-permute-start.8 = (bf16[416,512]{1,0:T(8,128)(2,1)}, bf16[416,512]{1,0:T(8,128)(2,1)}, u32[]{:S(2)}, u32[]{:S(2)}) collective-permute-start(bf16[416,512]{1,0:T(8,128)(2,1)} %slice.150), channel_id=1, source_target_pairs={{0,2},{1,3},{2,0},{3,1},{4,6},{5,7},{6,4},{7,5},{8,10},{9,11},{10,... | collective-permute-start | bytes 1277960 | tf_op jit(solution)/shard_map/ppermute | solution.py:75
  48.3 14.0 %collective-permute-start.9 = (bf16[416,512]{1,0:T(8,128)(2,1)}, bf16[416,512]{1,0:T(8,128)(2,1)}, u32[]{:S(2)}, u32[]{:S(2)}) collective-permute-start(bf16[416,512]{1,0:T(8,128)(2,1)} %slice.151), channel_id=1, source_target_pairs={{0,1},{1,0},{2,3},{3,2},{4,5},{5,4},{6,7},{7,6},{8,9},{9,8},{10,11... | collective-permute-start | bytes 1277960 | tf_op jit(solution)/shard_map/ppermute | solution.py:75
  49.0 13.7 %collective-permute-start.11 = (bf16[832,512]{1,0:T(8,128)(2,1)}, bf16[832,512]{1,0:T(8,128)(2,1)}, u32[]{:S(2)}, u32[]{:S(2)}) collective-permute-start(bf16[832,512]{1,0:T(8,128)(2,1)} %collective-permute-done.7.rest_2_.rest_11_), channel_id=1, source_target_pairs={{0,4},{1,5},{2,6},{3,7},{4,0},{5,1},{6,2},{7,3},{8,12},{9,13},{10,... | collective-permute-start | bytes 2555912 | tf_op jit(solution)/shard_map/ppermute | solution.py:75
  60.1 21.6 %collective-permute-start.14 = (bf16[832,512]{1,0:T(8,128)(2,1)}, bf16[832,512]{1,0:T(8,128)(2,1)S(1)}, u32[]{:S(2)}, u32[]{:S(2)}) collective-permute-start(bf16[832,512]{1,0:T(8,128)(2,1)} %pad_maximum_fusion.1), channel_id=1, source_target_pairs={{0,1},{1,0},{2,3},{3,2},{4,5},{5,4},{6,7},{7,6},{8,9},{9,8},{10,11... | collective-permute-start | bytes 2555912 | tf_op jit(solution)/shard_map/ppermute | solution.py:75
  61.4 22.0 %collective-permute-start.15 = (bf16[832,512]{1,0:T(8,128)(2,1)}, bf16[832,512]{1,0:T(8,128)(2,1)S(1)}, u32[]{:S(2)}, u32[]{:S(2)}) collective-permute-start(bf16[832,512]{1,0:T(8,128)(2,1)} %pad_maximum_fusion.1), channel_id=1, source_target_pairs={{0,2},{1,3},{2,0},{3,1},{4,6},{5,7},{6,4},{7,5},{8,10},{9,11},{10,... | collective-permute-start | bytes 2555912 | tf_op jit(solution)/shard_map/ppermute | solution.py:75
  81.8 27.7 %collective-permute-start.20 = (bf16[832,512]{1,0:T(8,128)(2,1)S(1)}, bf16[832,512]{1,0:T(8,128)(2,1)S(1)}, u32[]{:S(2)}, u32[]{:S(2)}) collective-permute-start(bf16[832,512]{1,0:T(8,128)(2,1)S(1)} %collective-permute-done.14.rest_1_.rest_10_), channel_id=1, source_target_pairs={{0,4},{1,5},{2,6},{3,7},{4,0},{5,1},{6,2},{7,3},{8,12},{9,13},{10,... | collective-permute-start | bytes 2555912 | tf_op jit(solution)/shard_map/ppermute | solution.py:75
  81.8 17.7 %collective-permute-start.18 = (bf16[416,512]{1,0:T(8,128)(2,1)S(1)}, bf16[416,512]{1,0:T(8,128)(2,1)S(1)}, u32[]{:S(2)}, u32[]{:S(2)}) collective-permute-start(bf16[416,512]{1,0:T(8,128)(2,1)S(1)} %slice.167), channel_id=1, source_target_pairs={{0,2},{1,3},{2,0},{3,1},{4,6},{5,7},{6,4},{7,5},{8,10},{9,11},{10,... | collective-permute-start | bytes 1277960 | tf_op jit(solution)/shard_map/ppermute | solution.py:75
  83.4 26.6 %collective-permute-start.21 = (bf16[832,512]{1,0:T(8,128)(2,1)S(1)}, bf16[832,512]{1,0:T(8,128)(2,1)S(1)}, u32[]{:S(2)}, u32[]{:S(2)}) collective-permute-start(bf16[832,512]{1,0:T(8,128)(2,1)S(1)} %collective-permute-done.15.rest_2_.rest_11_), channel_id=1, source_target_pairs={{0,4},{1,5},{2,6},{3,7},{4,0},{5,1},{6,2},{7,3},{8,12},{9,13},{10,... | collective-permute-start | bytes 2555912 | tf_op jit(solution)/shard_map/ppermute | solution.py:75
  83.6 16.0 %collective-permute-start.19 = (bf16[416,512]{1,0:T(8,128)(2,1)S(1)}, bf16[416,512]{1,0:T(8,128)(2,1)S(1)}, u32[]{:S(2)}, u32[]{:S(2)}) collective-permute-start(bf16[416,512]{1,0:T(8,128)(2,1)S(1)} %slice.168), channel_id=1, source_target_pairs={{0,1},{1,0},{2,3},{3,2},{4,5},{5,4},{6,7},{7,6},{8,9},{9,8},{10,11... | collective-permute-start | bytes 1277960 | tf_op jit(solution)/shard_map/ppermute | solution.py:75
  84.3 17.1 %collective-permute-start.16 = (bf16[256,512]{1,0:T(8,128)(2,1)S(1)}, bf16[256,512]{1,0:T(8,128)(2,1)S(1)}, u32[]{:S(2)}, u32[]{:S(2)}) collective-permute-start(bf16[256,512]{1,0:T(8,128)(2,1)S(1)} %pad_maximum_fusion.2), channel_id=1, source_target_pairs={{0,1},{1,0},{2,3},{3,2},{4,5},{5,4},{6,7},{7,6},{8,9},{9,8},{10,11... | collective-permute-start | bytes 786440 | tf_op jit(solution)/shard_map/ppermute | solution.py:75
  108.5 30.2 %collective-permute-start.26 = (bf16[256,512]{1,0:T(8,128)(2,1)S(1)}, bf16[256,512]{1,0:T(8,128)(2,1)}, u32[]{:S(2)}, u32[]{:S(2)}) collective-permute-start(bf16[256,512]{1,0:T(8,128)(2,1)S(1)} %collective-permute-done.16.rest_1_), channel_id=1, source_target_pairs={{0,4},{1,5},{2,6},{3,7},{4,0},{5,1},{6,2},{7,3},{8,12},{9,13},{10,... | collective-permute-start | bytes 786440 | tf_op jit(solution)/shard_map/ppermute | solution.py:75
  109.4 29.2 %collective-permute-start.27 = (bf16[256,512]{1,0:T(8,128)(2,1)}, bf16[256,512]{1,0:T(8,128)(2,1)}, u32[]{:S(2)}, u32[]{:S(2)}) collective-permute-start(bf16[256,512]{1,0:T(8,128)(2,1)} %collective-permute-done.17.rest_2_), channel_id=1, source_target_pairs={{0,4},{1,5},{2,6},{3,7},{4,0},{5,1},{6,2},{7,3},{8,12},{9,13},{10,... | collective-permute-start | bytes 786440 | tf_op jit(solution)/shard_map/ppermute | solution.py:75
  110.0 13.7 %collective-permute-start.24 = (bf16[128,512]{1,0:T(8,128)(2,1)S(1)}, bf16[128,512]{1,0:T(8,128)(2,1)}, u32[]{:S(2)}, u32[]{:S(2)}) collective-permute-start(bf16[128,512]{1,0:T(8,128)(2,1)S(1)} %slice.169), channel_id=1, source_target_pairs={{0,2},{1,3},{2,0},{3,1},{4,6},{5,7},{6,4},{7,5},{8,10},{9,11},{10,... | collective-permute-start | bytes 393224 | tf_op jit(solution)/shard_map/ppermute | solution.py:75
  110.5 13.2 %collective-permute-start.25 = (bf16[128,512]{1,0:T(8,128)(2,1)S(1)}, bf16[128,512]{1,0:T(8,128)(2,1)}, u32[]{:S(2)}, u32[]{:S(2)}) collective-permute-start(bf16[128,512]{1,0:T(8,128)(2,1)S(1)} %slice.170), channel_id=1, source_target_pairs={{0,1},{1,0},{2,3},{3,2},{4,5},{5,4},{6,7},{7,6},{8,9},{9,8},{10,11... | collective-permute-start | bytes 393224 | tf_op jit(solution)/shard_map/ppermute | solution.py:75
  123.7 15.0 %collective-permute-start.28 = (bf16[128,512]{1,0:T(8,128)(2,1)}, bf16[128,512]{1,0:T(8,128)(2,1)S(1)}, u32[]{:S(2)}, u32[]{:S(2)}) collective-permute-start(bf16[128,512]{1,0:T(8,128)(2,1)} %collective-permute-done.24.rest_3_), channel_id=1, source_target_pairs={{0,4},{1,5},{2,6},{3,7},{4,0},{5,1},{6,2},{7,3},{8,12},{9,13},{10,... | collective-permute-start | bytes 393224 | tf_op jit(solution)/shard_map/ppermute | solution.py:75
  123.8 14.9 %collective-permute-start.29 = (bf16[128,512]{1,0:T(8,128)(2,1)}, bf16[128,512]{1,0:T(8,128)(2,1)S(1)}, u32[]{:S(2)}, u32[]{:S(2)}) collective-permute-start(bf16[128,512]{1,0:T(8,128)(2,1)} %collective-permute-done.25.rest_4_), channel_id=1, source_target_pairs={{0,4},{1,5},{2,6},{3,7},{4,0},{5,1},{6,2},{7,3},{8,12},{9,13},{10,... | collective-permute-start | bytes 393224 | tf_op jit(solution)/shard_map/ppermute | solution.py:75
  205.6 21.9 %collective-permute-start.32 = (bf16[3,144,512]{2,1,0:T(8,128)(2,1)}, bf16[3,144,512]{2,1,0:T(8,128)(2,1)}, u32[]{:S(2)}, u32[]{:S(2)}) collective-permute-start(bf16[3,144,512]{2,1,0:T(8,128)(2,1)} %get-tuple-element.207), channel_id=1, source_target_pairs={{0,1},{1,0},{2,3},{3,2},{4,5},{5,4},{6,7},{7,6},{8,9},{9,8},{10,11... | collective-permute-start | bytes 1327112 | tf_op jit(solution)/shard_map/ppermute | solution.py:75
  205.7 23.0 %collective-permute-start.33 = (bf16[3,144,512]{2,1,0:T(8,128)(2,1)}, bf16[3,144,512]{2,1,0:T(8,128)(2,1)}, u32[]{:S(2)}, u32[]{:S(2)}) collective-permute-start(bf16[3,144,512]{2,1,0:T(8,128)(2,1)} %get-tuple-element.208), channel_id=1, source_target_pairs={{0,2},{1,3},{2,0},{3,1},{4,6},{5,7},{6,4},{7,5},{8,10},{9,11},{10,... | collective-permute-start | bytes 1327112 | tf_op jit(solution)/shard_map/ppermute | solution.py:75
  229.9 17.6 %collective-permute-start.34 = (bf16[3,144,512]{2,1,0:T(8,128)(2,1)S(1)}, bf16[3,144,512]{2,1,0:T(8,128)(2,1)S(1)}, u32[]{:S(2)}, u32[]{:S(2)}) collective-permute-start(bf16[3,144,512]{2,1,0:T(8,128)(2,1)S(1)} %add.160), channel_id=1, source_target_pairs={{0,2},{1,3},{2,0},{3,1},{4,6},{5,7},{6,4},{7,5},{8,10},{9,11},{10,... | collective-permute-start | bytes 1327112 | tf_op jit(solution)/shard_map/ppermute | solution.py:75
  230.7 17.7 %collective-permute-start.35 = (bf16[3,144,512]{2,1,0:T(8,128)(2,1)S(1)}, bf16[3,144,512]{2,1,0:T(8,128)(2,1)S(1)}, u32[]{:S(2)}, u32[]{:S(2)}) collective-permute-start(bf16[3,144,512]{2,1,0:T(8,128)(2,1)S(1)} %add.161), channel_id=1, source_target_pairs={{0,1},{1,0},{2,3},{3,2},{4,5},{5,4},{6,7},{7,6},{8,9},{9,8},{10,11... | collective-permute-start | bytes 1327112 | tf_op jit(solution)/shard_map/ppermute | solution.py:75
  243.4 22.7 %collective-permute-start.36 = (bf16[2,2,2,288,512]{4,3,2,1,0:T(8,128)(2,1)}, bf16[2,2,2,288,512]{4,3,2,1,0:T(8,128)(2,1)S(1)}, u32[]{:S(2)}, u32[]{:S(2)}) collective-permute-start(bf16[2,2,2,288,512]{4,3,2,1,0:T(8,128)(2,1)} %dynamic-slice_bitcast_fusion.1), channel_id=1, source_target_pairs={{0,4},{1,5},{2,6},{3,7},{4,0},{5,1},{6,2},{7,3},{8,12},{9,13},{10,... | collective-permute-start | bytes 7077896 | tf_op jit(solution)/shard_map/ppermute | solution.py:75
  247.0 19.2 %collective-permute-start.37 = (bf16[2,2,2,128,512]{4,3,2,1,0:T(8,128)(2,1)}, bf16[2,2,2,128,512]{4,3,2,1,0:T(8,128)(2,1)S(1)}, u32[]{:S(2)}, u32[]{:S(2)}) collective-permute-start(bf16[2,2,2,128,512]{4,3,2,1,0:T(8,128)(2,1)} %dynamic-slice_bitcast_fusion.5), channel_id=1, source_target_pairs={{0,4},{1,5},{2,6},{3,7},{4,0},{5,1},{6,2},{7,3},{8,12},{9,13},{10,... | collective-permute-start | bytes 3145736 | tf_op jit(solution)/shard_map/ppermute | solution.py:75
  270.9 26.6 %collective-permute-start.39 = (bf16[2,544,512]{2,1,0:T(8,128)(2,1)S(1)}, bf16[2,544,512]{2,1,0:T(8,128)(2,1)S(1)}, u32[]{:S(2)}, u32[]{:S(2)}) collective-permute-start(bf16[2,544,512]{2,1,0:T(8,128)(2,1)S(1)} %get-tuple-element.232), channel_id=1, source_target_pairs={{0,1},{1,0},{2,3},{3,2},{4,5},{5,4},{6,7},{7,6},{8,9},{9,8},{10,11... | collective-permute-start | bytes 3342344 | tf_op jit(solution)/shard_map/ppermute | solution.py:75
  270.9 26.7 %collective-permute-start.40 = (bf16[2,544,512]{2,1,0:T(8,128)(2,1)}, bf16[2,544,512]{2,1,0:T(8,128)(2,1)S(1)}, u32[]{:S(2)}, u32[]{:S(2)}) collective-permute-start(bf16[2,544,512]{2,1,0:T(8,128)(2,1)} %get-tuple-element.233), channel_id=1, source_target_pairs={{0,2},{1,3},{2,0},{3,1},{4,6},{5,7},{6,4},{7,5},{8,10},{9,11},{10,... | collective-permute-start | bytes 3342344 | tf_op jit(solution)/shard_map/ppermute | solution.py:75
  298.5 15.8 %collective-permute-start.41 = (bf16[544,512]{1,0:T(8,128)(2,1)S(1)}, bf16[544,512]{1,0:T(8,128)(2,1)S(1)}, u32[]{:S(2)}, u32[]{:S(2)}) collective-permute-start(bf16[544,512]{1,0:T(8,128)(2,1)S(1)} %get-tuple-element.245), channel_id=1, source_target_pairs={{0,2},{1,3},{2,0},{3,1},{4,6},{5,7},{6,4},{7,5},{8,10},{9,11},{10,... | collective-permute-start | bytes 1671176 | tf_op jit(solution)/shard_map/ppermute | solution.py:75
  299.6 14.6 %collective-permute-start.42 = (bf16[544,512]{1,0:T(8,128)(2,1)S(1)}, bf16[544,512]{1,0:T(8,128)(2,1)S(1)}, u32[]{:S(2)}, u32[]{:S(2)}) collective-permute-start(bf16[544,512]{1,0:T(8,128)(2,1)S(1)} %get-tuple-element.246), channel_id=1, source_target_pairs={{0,1},{1,0},{2,3},{3,2},{4,5},{5,4},{6,7},{7,6},{8,9},{9,8},{10,11... | collective-permute-start | bytes 1671176 | tf_op jit(solution)/shard_map/ppermute | solution.py:75
  313.2 28.5 %collective-permute-start.44 = (bf16[2,2,2,288,512]{4,3,2,1,0:T(8,128)(2,1)}, bf16[2,2,2,288,512]{4,3,2,1,0:T(8,128)(2,1)}, u32[]{:S(2)}, u32[]{:S(2)}) collective-permute-start(bf16[2,2,2,288,512]{4,3,2,1,0:T(8,128)(2,1)} %dynamic-slice_bitcast_fusion), channel_id=1, source_target_pairs={{0,4},{1,5},{2,6},{3,7},{4,0},{5,1},{6,2},{7,3},{8,12},{9,13},{10,... | collective-permute-start | bytes 7077896 | tf_op jit(solution)/shard_map/ppermute | solution.py:75
  315.1 15.1 %collective-permute-start.43 = (bf16[544,512]{1,0:T(8,128)(2,1)S(1)}, bf16[544,512]{1,0:T(8,128)(2,1)S(1)}, u32[]{:S(2)}, u32[]{:S(2)}) collective-permute-start(bf16[544,512]{1,0:T(8,128)(2,1)S(1)} %get-tuple-element.253), channel_id=1, source_target_pairs={{0,8},{1,9},{2,10},{3,11},{4,12},{5,13},{6,14},{7,15},{8,0},{9,1},... | collective-permute-start | bytes 1671176 | tf_op jit(solution)/shard_map/ppermute | solution.py:75
  315.9 25.7 %collective-permute-start.45 = (bf16[2,2,2,128,512]{4,3,2,1,0:T(8,128)(2,1)}, bf16[2,2,2,128,512]{4,3,2,1,0:T(8,128)(2,1)}, u32[]{:S(2)}, u32[]{:S(2)}) collective-permute-start(bf16[2,2,2,128,512]{4,3,2,1,0:T(8,128)(2,1)} %dynamic-slice_bitcast_fusion.3), channel_id=1, source_target_pairs={{0,4},{1,5},{2,6},{3,7},{4,0},{5,1},{6,2},{7,3},{8,12},{9,13},{10,... | collective-permute-start | bytes 3145736 | tf_op jit(solution)/shard_map/ppermute | solution.py:75
  352.6 31.2 %collective-permute-start.51 = (bf16[2,544,512]{2,1,0:T(8,128)(2,1)}, bf16[2,544,512]{2,1,0:T(8,128)(2,1)S(1)}, u32[]{:S(2)}, u32[]{:S(2)}) collective-permute-start(bf16[2,544,512]{2,1,0:T(8,128)(2,1)} %get-tuple-element.272), channel_id=1, source_target_pairs={{0,1},{1,0},{2,3},{3,2},{4,5},{5,4},{6,7},{7,6},{8,9},{9,8},{10,11... | collective-permute-start | bytes 3342344 | tf_op jit(solution)/shard_map/ppermute | solution.py:75
  353.7 30.1 %collective-permute-start.52 = (bf16[2,544,512]{2,1,0:T(8,128)(2,1)}, bf16[2,544,512]{2,1,0:T(8,128)(2,1)}, u32[]{:S(2)}, u32[]{:S(2)}) collective-permute-start(bf16[2,544,512]{2,1,0:T(8,128)(2,1)} %get-tuple-element.273), channel_id=1, source_target_pairs={{0,2},{1,3},{2,0},{3,1},{4,6},{5,7},{6,4},{7,5},{8,10},{9,11},{10,... | collective-permute-start | bytes 3342344 | tf_op jit(solution)/shard_map/ppermute | solution.py:75
  354.7 27.7 %collective-permute-start.49 = (bf16[544,512]{1,0:T(8,128)(2,1)}, bf16[544,512]{1,0:T(8,128)(2,1)}, u32[]{:S(2)}, u32[]{:S(2)}) collective-permute-start(bf16[544,512]{1,0:T(8,128)(2,1)} %add.165), channel_id=1, source_target_pairs={{0,16},{1,17},{2,18},{3,19},{4,20},{5,21},{6,22},{7,23},{8,24},{9,... | collective-permute-start | bytes 1671176 | tf_op jit(solution)/shard_map/ppermute | solution.py:75
  363.8 20.0 %collective-permute-start.47 = (f32[16,1024]{1,0:T(8,128)S(1)}, f32[16,1024]{1,0:T(8,128)S(1)}, u32[]{:S(2)}, u32[]{:S(2)}) collective-permute-start(f32[16,1024]{1,0:T(8,128)S(1)} %pad_maximum_fusion.3), channel_id=1, source_target_pairs={{0,4},{1,5},{2,6},{3,7},{4,0},{5,1},{6,2},{7,3},{8,12},{9,13},{10,... | collective-permute-start | bytes 196616 | tf_op jit(solution)/shard_map/ppermute | solution.py:75
  383.7 14.4 %collective-permute-start.50 = (bf16[544,512]{1,0:T(8,128)(2,1)S(1)}, bf16[544,512]{1,0:T(8,128)(2,1)S(1)}, u32[]{:S(2)}, u32[]{:S(2)}) collective-permute-start(bf16[544,512]{1,0:T(8,128)(2,1)S(1)} %add.169.rest_0_.rest_4_.rest_8_), channel_id=1, source_target_pairs={{0,8},{1,9},{2,10},{3,11},{4,12},{5,13},{6,14},{7,15},{8,0},{9,1},... | collective-permute-start | bytes 1671176 | tf_op jit(solution)/shard_map/ppermute | solution.py:75
  385.4 14.4 %collective-permute-start.54 = (bf16[544,512]{1,0:T(8,128)(2,1)S(1)}, bf16[544,512]{1,0:T(8,128)(2,1)S(1)}, u32[]{:S(2)}, u32[]{:S(2)}) collective-permute-start(bf16[544,512]{1,0:T(8,128)(2,1)S(1)} %get-tuple-element.283), channel_id=1, source_target_pairs={{0,2},{1,3},{2,0},{3,1},{4,6},{5,7},{6,4},{7,5},{8,10},{9,11},{10,... | collective-permute-start | bytes 1671176 | tf_op jit(solution)/shard_map/ppermute | solution.py:75
  386.4 14.3 %collective-permute-start.55 = (bf16[544,512]{1,0:T(8,128)(2,1)S(1)}, bf16[544,512]{1,0:T(8,128)(2,1)S(1)}, u32[]{:S(2)}, u32[]{:S(2)}) collective-permute-start(bf16[544,512]{1,0:T(8,128)(2,1)S(1)} %get-tuple-element.284), channel_id=1, source_target_pairs={{0,1},{1,0},{2,3},{3,2},{4,5},{5,4},{6,7},{7,6},{8,9},{9,8},{10,11... | collective-permute-start | bytes 1671176 | tf_op jit(solution)/shard_map/ppermute | solution.py:75
  387.5 17.1 %collective-permute-start.53 = (bf16[544,512]{1,0:T(8,128)(2,1)S(1)}, bf16[544,512]{1,0:T(8,128)(2,1)S(1)}, u32[]{:S(2)}, u32[]{:S(2)}) collective-permute-start(bf16[544,512]{1,0:T(8,128)(2,1)S(1)} %add.169.rest_0_.rest_4_.rest_8_), channel_id=1, source_target_pairs={{0,4},{1,5},{2,6},{3,7},{4,0},{5,1},{6,2},{7,3},{8,12},{9,13},{10,... | collective-permute-start | bytes 1671176 | tf_op jit(solution)/shard_map/ppermute | solution.py:75
  402.5 15.0 %collective-permute-start.59 = (bf16[544,512]{1,0:T(8,128)(2,1)}, bf16[544,512]{1,0:T(8,128)(2,1)}, u32[]{:S(2)}, u32[]{:S(2)}) collective-permute-start(bf16[544,512]{1,0:T(8,128)(2,1)} %get-tuple-element.290), channel_id=1, source_target_pairs={{0,8},{1,9},{2,10},{3,11},{4,12},{5,13},{6,14},{7,15},{8,0},{9,1},... | collective-permute-start | bytes 1671176 | tf_op jit(solution)/shard_map/ppermute | solution.py:75
  404.2 13.3 %collective-permute-start.48 = (f32[16,1024]{1,0:T(8,128)S(1)}, f32[16,1024]{1,0:T(8,128)S(1)}, u32[]{:S(2)}, u32[]{:S(2)}) collective-permute-start(f32[16,1024]{1,0:T(8,128)S(1)} %add.168), channel_id=1, source_target_pairs={{0,8},{1,9},{2,10},{3,11},{4,12},{5,13},{6,14},{7,15},{8,0},{9,1},... | collective-permute-start | bytes 196616 | tf_op jit(solution)/shard_map/ppermute | solution.py:75
  418.8 28.3 %collective-permute-start.63 = (bf16[544,512]{1,0:T(8,128)(2,1)S(1)}, bf16[544,512]{1,0:T(8,128)(2,1)S(1)}, u32[]{:S(2)}, u32[]{:S(2)}) collective-permute-start(bf16[544,512]{1,0:T(8,128)(2,1)S(1)} %add.171), channel_id=1, source_target_pairs={{0,16},{1,17},{2,18},{3,19},{4,20},{5,21},{6,22},{7,23},{8,24},{9,... | collective-permute-start | bytes 1671176 | tf_op jit(solution)/shard_map/ppermute | solution.py:75
  422.8 24.2 %collective-permute-start.57 = (f32[16,1024]{1,0:T(8,128)S(1)}, f32[16,1024]{1,0:T(8,128)S(1)}, u32[]{:S(2)}, u32[]{:S(2)}) collective-permute-start(f32[16,1024]{1,0:T(8,128)S(1)} %add.170), channel_id=1, source_target_pairs={{0,16},{1,17},{2,18},{3,19},{4,20},{5,21},{6,22},{7,23},{8,24},{9,... | collective-permute-start | bytes 196616 | tf_op jit(solution)/shard_map/ppermute | solution.py:75
  447.2 14.1 %collective-permute-start.66 = (bf16[544,512]{1,0:T(8,128)(2,1)S(1)}, bf16[544,512]{1,0:T(8,128)(2,1)S(1)}, u32[]{:S(2)}, u32[]{:S(2)}) collective-permute-start(bf16[544,512]{1,0:T(8,128)(2,1)S(1)} %add.175.rest_0_.rest_4_.rest_8_), channel_id=1, source_target_pairs={{0,8},{1,9},{2,10},{3,11},{4,12},{5,13},{6,14},{7,15},{8,0},{9,1},... | collective-permute-start | bytes 1671176 | tf_op jit(solution)/shard_map/ppermute | solution.py:75
  449.9 19.6 %collective-permute-start.71 = (bf16[544,512]{1,0:T(8,128)(2,1)S(1)}, bf16[544,512]{1,0:T(8,128)(2,1)S(1)}, u32[]{:S(2)}, u32[]{:S(2)}) collective-permute-start(bf16[544,512]{1,0:T(8,128)(2,1)S(1)} %add.175.rest_0_.rest_4_.rest_8_), channel_id=1, source_target_pairs={{0,4},{1,5},{2,6},{3,7},{4,0},{5,1},{6,2},{7,3},{8,12},{9,13},{10,... | collective-permute-start | bytes 1671176 | tf_op jit(solution)/shard_map/ppermute | solution.py:75
  478.8 12.9 %collective-permute-start.75 = (bf16[3,144,512]{2,1,0:T(8,128)(2,1)}, bf16[3,144,512]{2,1,0:T(8,128)(2,1)S(1)}, u32[]{:S(2)}, u32[]{:S(2)}) collective-permute-start(bf16[3,144,512]{2,1,0:T(8,128)(2,1)} %get-tuple-element.314), channel_id=1, source_target_pairs={{0,2},{1,3},{2,0},{3,1},{4,6},{5,7},{6,4},{7,5},{8,10},{9,11},{10,... | collective-permute-start | bytes 1327112 | tf_op jit(solution)/shard_map/ppermute | solution.py:75
  (121 other events, 1112.6 us)
